TPU v7x, 256 devices: a whole 4x4x8 slice. The times are simulated.
256 devices in a mesh: dp: 32 (over z, x), mp: 8 (over y, core).
Axes of the slice: x: 4, y: 4, z: 8, core: 2. Of those that a mesh axis runs over, the one named last changes fastest.
Arguments:
- tokens: bfloat16 [32768, 8192], P(('dp', 'mp')), may hold values from -6 to 6
- key_value_weight: bfloat16 [8192, 2048], P(None, 'mp'), may hold values from -0.0625 to 0.0625
- adapter_down_weight: bfloat16 [64, 8192, 128], P(None, ('dp', 'mp')), may hold values from -0.0625 to 0.0625
- adapter_up_weight: bfloat16 [64, 64, 2048], P(None, 'dp', 'mp'), may hold values from -1 to 1
- adapter_per_request: int32 [128], replicated, may hold values from 0 to 63
- request_per_segment: int32 [256], replicated, may hold values from 0 to 127, never falling along the last dimension, each value on 1 to 4 neighbouring positions
Outputs:
- kv_out: bfloat16 [32768, 2048], P('dp', 'mp')
Inputs may be any that keep to these rules, and one draw needn't show every extreme that they name: request_per_segment never falls along the segments; every request has 1 to 4 segments, one has exactly 4.
All inputs are finite; a program needn't handle non-finite values.
Results may differ from a plain program's by a relative error of at most 0.0043.
Values may be sent and summed in bfloat16 or wider, within the bound.
No kernel may reach another device: no remote copies, remote signals or barrier semaphores. Data moves between devices by JAX's collectives and lax.ppermute only.
A program may use at most 128 MiB of HBM per device.

v0:
```python
import jax
import jax.numpy as jnp
from jax import lax
from jax.sharding import PartitionSpec as P


def on_device(
    tokens,
    key_value_weight,
    adapter_down_weight,
    adapter_up_weight,
    adapter_per_request,
    request_per_segment,
):
    n_dp = lax.axis_size("dp")
    n_mp = lax.axis_size("mp")
    group = lax.axis_index("dp")
    column = lax.axis_index("mp")
    seg_total = request_per_segment.shape[0]
    seg_group = seg_total // n_dp
    seg_adapter = jnp.take(adapter_per_request, request_per_segment, axis=0)
    local_portion = lax.dynamic_slice_in_dim(seg_adapter, group * seg_group, seg_group)
    gathered = lax.all_gather(tokens, "mp", axis=0, tiled=True)
    rows = gathered.shape[0]
    seg_len = rows // seg_group
    width_tile = adapter_down_weight.shape[1]
    double_rank = adapter_down_weight.shape[2]
    rank = double_rank // 2
    column_tile = adapter_up_weight.shape[2]
    base = jnp.dot(gathered, key_value_weight, preferred_element_type=jnp.float32)
    strided = lax.dynamic_index_in_dim(
        gathered.reshape(rows, n_dp, n_mp, width_tile), column, 2, keepdims=False
    ).reshape(seg_group, seg_len, n_dp * width_tile)
    selected_factor = jnp.take(
        lax.all_gather(adapter_down_weight, "dp", axis=1, tiled=True), local_portion, axis=0
    )
    partial_low = jnp.einsum(
        "sti,sir->str", strided, selected_factor, preferred_element_type=jnp.float32
    )
    selected_factor = jnp.take(
        lax.all_gather(adapter_up_weight, "dp", axis=1, tiled=True), local_portion, axis=0
    )
    rank_output = lax.psum(partial_low, "mp").astype(jnp.bfloat16)
    key_width = n_mp * column_tile // 2
    half = column * column_tile // key_width
    low_half = lax.dynamic_slice_in_dim(rank_output, half * rank, rank, 2)
    delta = jnp.einsum(
        "str,src->stc", low_half, selected_factor, preferred_element_type=jnp.float32
    )
    return (base + delta.reshape(rows, column_tile)).astype(jnp.bfloat16)


def solution(mesh):
    placed = (
        P(("dp", "mp"), None),
        P(None, "mp"),
        P(None, ("dp", "mp"), None),
        P(None, "dp", "mp"),
        P(),
        P(),
    )
    return jax.shard_map(
        on_device, mesh=mesh, in_specs=placed, out_specs=P("dp", "mp"), check_vma=False
    )
```

profile of v0, /device:TPU:1, one launch (start us, length us, event | category | flops | bytes accessed | tf_op | source)
XLA Modules:
  0.0 393.8 jit_solution(15381608548851995539)
XLA Ops:
  6.5 0.0 copy-start
  6.5 0.0 all-gather.8.cloned.1.call-start
  6.5 1.5 copy.16
  8.0 0.0 all-gather.8.cloned.1.call-update
  8.1 0.0 all-gather.4.cloned.1.call-start
  8.1 4.1 %copy.13 = bf16[128,8192]{0,1:T(8,128)(2,1)} copy(bf16[128,8192]{1,0:T(8,128)(2,1)} %param.6) | data formatting | bytes 4194304 | tf_op args[0]
  12.2 0.0 copy-start.1
  12.2 0.0 all-gather.4.cloned.1.call-update
  12.2 0.0 all-gather.6.cloned.1.call-start
  12.3 0.7 all-gather.6.cloned.1.call-update
  13.0 0.0 copy-done.1
  13.0 0.0 copy-done
  13.0 1.9 gather_fusion
  14.9 0.1 compare_and_fusion
  15.0 72.7 %all-gather.8.cloned.1.call-done = bf16[64,64,256]{2,0,1:T(8,128)(2,1)} async-done(((bf16[64,2,256]{2,0,1:T(8,128)(2,1)}), bf16[64,64,256]{2,0,1:T(8,128)(2,1)}) %all-gather.8.cloned.1.call-update) | async-done | bytes 2097168 | tf_op jit(solution)/shard_map/all_gather | solution.py:41
  87.8 2.8 copy.17
  90.5 0.6 gather_fusion.2
  91.1 92.9 %all-gather.4.cloned.1.call-done = bf16[1024,8192]{0,1:T(8,128)(2,1)} async-done(((bf16[128,8192]{0,1:T(8,128)(2,1)}), bf16[1024,8192]{0,1:T(8,128)(2,1)}) %all-gather.4.cloned.1.call-update) | async-done | bytes 16777232 | tf_op jit(solution)/shard_map/all_gather | solution.py:23
  184.0 1.8 constant_dynamic-slice_fusion
  185.8 0.6 copy.19
  186.4 148.9 %all-gather.6.cloned.1.call-done = bf16[64,1024,128]{2,1,0:T(8,128)(2,1)} async-done(((bf16[64,32,128]{2,1,0:T(8,128)(2,1)}), bf16[64,1024,128]{2,1,0:T(8,128)(2,1)}) %all-gather.6.cloned.1.call-update) | async-done | bytes 16777232 | tf_op jit(solution)/shard_map/all_gather | solution.py:35
  335.3 7.9 %gather_fusion.1 = bf16[8,1024,128]{2,1,0:T(8,128)(2,1)} fusion(bf16[64,1024,128]{2,1,0:T(8,128)(2,1)} %all-gather.6.cloned.1.call-done, s32[1024]{0:T(1024)S(1)} %pad_clamp_fusion), kind=kCustom, calls=%fused_computation.1 | custom fusion | bytes 4194336 | tf_op jit(solution)/shard_map/jit(_take)/gather | solution.py:34
  343.2 2.7 fusion
  345.9 28.6 %all-reduce.1 = bf16[8,128,128]{1,2,0:T(8,128)(2,1)S(1)} all-reduce(f32[8,128,128]{1,2,0:T(8,128)S(1)} %fusion), channel_id=1, replica_groups=mesh['dp'=32,'mp'=8] {'mp'}, use_global_device_ids=true, to_apply=%region_0.1 | all-reduce | flops 131072 | bytes 786432 | tf_op jit(solution)/shard_map/psum | solution.py:43
  374.6 0.4 fusion.6
  374.9 12.3 %fusion.4 = bf16[1024,256]{1,0:T(8,128)(2,1)} fusion(f32[1024,256]{1,0:T(8,128)S(1)} %bitcast.12, bf16[1024,8192]{0,1:T(8,128)(2,1)} %all-gather.4.cloned.1.call-done, bf16[8192,256]{1,0:T(8,128)(2,1)} %param.7), kind=kOutput, calls=%fused_computation.8 | convolution fusion | flops 4295491584 | bytes 22544384 | tf_op jit(solution)/shard_map/dot_general | solution.py:30
  (4 shorter events, 0.0 us)
Async XLA Ops:
  6.5 6.5 %copy-start = (s32[128]{0:T(128)S(1)}, s32[128]{0:T(128)}, u32[]{:S(2)}) copy-start(s32[128]{0:T(128)} %param.10) | copy-start | bytes 1540
  6.5 81.2 %all-gather.8.cloned.1.call-start = ((), (), s32[]{:S(2)}) async-start(), calls=%async_computation.2 | async-start | bytes 2162688 | tf_op jit(solution)/shard_map/all_gather | solution.py:41
  8.1 176.0 %all-gather.4.cloned.1.call-start = ((), (), s32[]{:S(2)}) async-start(), calls=%async_computation | async-start | bytes 18874368 | tf_op jit(solution)/shard_map/all_gather | solution.py:23
  12.2 0.8 copy-start.1
  12.2 323.0 %all-gather.6.cloned.1.call-start = ((), (), s32[]{:S(2)}) async-start(), calls=%async_computation.1 | async-start | bytes 17301504 | tf_op jit(solution)/shard_map/all_gather | solution.py:35
Sparse Core Ops, SparseCore 0:
  9.9 77.7 all-gather.7
  89.6 94.3 all-gather.3
  186.5 148.7 all-gather.5
where the time goes:
time: 396 us; the launch traced here: 394 us
  waiting for transfers between devices  315 us (80%)
  blocking collectives  28.6 us (7%)
  local copies, waits for them, and re-layouts  21.1 us (5%)
  matrix products  15.4 us (4%)
  between operations  13.2 us (3%)
    all_gather x1, waiting for transfers between devices, on_device(): lax.all_gather(adapter_down_weight, 'dp', axis=1, tiled=True)  149 us
    all_gather x1, waiting for transfers between devices, on_device(): gathered = lax.all_gather(tokens, 'mp', axis=0, tiled=True)  92.9 us
    all_gather x1, waiting for transfers between devices, on_device(): lax.all_gather(adapter_up_weight, 'dp', axis=1, tiled=True)  72.7 us
    psum x1, blocking collectives, on_device(): rank_output = lax.psum(partial_low, 'mp').astype(jnp.bfloat16)  28.6 us
    dot_general x1, matrix products, on_device(): jnp.dot(gathered, key_value_weight, preferred_element_type=jnp.float32)  12.3 us
    gather x1, local copies, waits for them, and re-layouts, on_device(): jnp.take(lax.all_gather(adapter_down_weight, 'dp', axis=1, tiled=True), l...  7.93 us
  transfers between devices with their start and end apart: 3, of which 3 were waited for; matrix products, arithmetic and copies ran while one was open for 3% of the time, Pallas kernels for 0%

commit v1 on v0

v1 whole, which is shorter than its diff:
```python
import functools

import jax
import jax.numpy as jnp
from jax import lax
from jax.experimental import pallas as pl
from jax.experimental.pallas import tpu as pltpu
from jax.sharding import Mesh
from jax.sharding import PartitionSpec as P

NZ, NX, NY, NC = 8, 4, 4, 2
NDP = NZ * NX
SEG = 128
K = 8192
RANK = 64
COLS = 256
KQ = K // NY
BF16, F32 = jnp.bfloat16, jnp.float32
VMEM_LIMIT = 48 * 1024 * 1024


def params(**kw):
    return pltpu.CompilerParams(vmem_limit_bytes=VMEM_LIMIT, **kw)


def cost(flops, nbytes):
    return pl.CostEstimate(flops=flops, bytes_accessed=nbytes, transcendentals=0)


def shift(x, axis, by):
    n = {"y": NY, "c": NC}[axis]
    return lax.ppermute(x, axis, [(i, (i + by) % n) for i in range(n)])


def pack_kernel(apr, rps, down_ref, up_ref, out_ref):
    row = lax.broadcasted_iota(jnp.int32, (8, 128), 0)

    def to_device(n, carry):
        first = (n // NC) * (NY * NC) + n % NC
        ids = [apr[rps[first + s * NC]] for s in range(NY)]
        for s in range(NY):
            out_ref[n, 32 * s : 32 * s + 32, :] = down_ref[ids[s]]
        ups = [
            jnp.where(row < 4, up_ref[ids[s]], up_ref[ids[s + 1]]) for s in (0, 2)
        ]
        out_ref[n, 128:144, :] = jnp.concatenate(ups, axis=0).astype(BF16)
        return carry

    lax.fori_loop(0, NDP * NC, to_device, 0, unroll=4)


def pack(apr, rps, down, up_twice):
    return pl.pallas_call(
        pack_kernel,
        grid_spec=pltpu.PrefetchScalarGridSpec(
            num_scalar_prefetch=2,
            grid=(1,),
            in_specs=[
                pl.BlockSpec((64, 32, 128), lambda i, *_: (0, 0, 0)),
                pl.BlockSpec((64, 8, 128), lambda i, *_: (0, 0, 0)),
            ],
            out_specs=pl.BlockSpec((64, 144, 128), lambda i, *_: (0, 0, 0)),
        ),
        out_shape=jax.ShapeDtypeStruct((64, 144, 128), BF16),
        compiler_params=params(),
        cost_estimate=cost(0, 3 << 20),
    )(apr, rps, down, up_twice)


def quarter_of(x_ref, q, pair):
    at = pair * 512 + (q // 2) * 128
    a = x_ref[:, pl.ds(pl.multiple_of(at, 128), 128)]
    b = x_ref[:, pl.ds(pl.multiple_of(at + 256, 128), 128)]
    low = jnp.concatenate([a[:, :64], b[:, :64]], axis=1)
    high = jnp.concatenate([a[:, 64:], b[:, 64:]], axis=1)
    return jnp.where(q % 2 == 0, low, high)


def split_kernel(first, x_ref, *outs):
    for pair in range(16):
        lanes = slice(128 * pair, 128 * pair + 128)
        for i in range(NY):
            q = (first[0] + i) % NY
            part = quarter_of(x_ref, q, pair)
            if i == 0:
                outs[0][:, lanes] = part
            elif i < 3:
                outs[1][i - 1, :, lanes] = part
            else:
                outs[2][:, lanes] = part


def split_quarters(x, first):
    rows = x.shape[0]
    return pl.pallas_call(
        split_kernel,
        grid_spec=pltpu.PrefetchScalarGridSpec(
            num_scalar_prefetch=1,
            grid=(1,),
            in_specs=[pl.BlockSpec((rows, K), lambda i, *_: (0, 0))],
            out_specs=[
                pl.BlockSpec((rows, KQ), lambda i, *_: (0, 0)),
                pl.BlockSpec((2, rows, KQ), lambda i, *_: (0, 0, 0)),
                pl.BlockSpec((rows, KQ), lambda i, *_: (0, 0)),
            ],
        ),
        out_shape=[
            jax.ShapeDtypeStruct((rows, KQ), BF16),
            jax.ShapeDtypeStruct((2, rows, KQ), BF16),
            jax.ShapeDtypeStruct((rows, KQ), BF16),
        ],
        compiler_params=params(),
        cost_estimate=cost(0, 4 * rows * K),
    )(first, x)


def own_quarter_kernel(y, x0, a_lo, a_hi, b_lo, b_hi, out):
    q = y[0]
    for pair in range(16):
        lanes = slice(128 * pair, 128 * pair + 128)
        out[0, :, lanes] = quarter_of(x0, q, pair)
        out[1, 0:64, lanes] = quarter_of(b_lo, q, pair)
        out[1, 64:128, lanes] = quarter_of(b_hi, q, pair)
        out[2, 0:64, lanes] = quarter_of(a_lo, q, pair)
        out[2, 64:128, lanes] = quarter_of(a_hi, q, pair)


def own_quarter(y, x0, a_lo, a_hi, b_lo, b_hi):
    half = pl.BlockSpec((64, K), lambda i, *_: (0, 0))
    return pl.pallas_call(
        own_quarter_kernel,
        grid_spec=pltpu.PrefetchScalarGridSpec(
            num_scalar_prefetch=1,
            grid=(1,),
            in_specs=[pl.BlockSpec((128, K), lambda i, *_: (0, 0))] + [half] * 4,
            out_specs=pl.BlockSpec((3, 128, KQ), lambda i, *_: (0, 0, 0)),
        ),
        out_shape=jax.ShapeDtypeStruct((3, 128, KQ), BF16),
        compiler_params=params(),
        cost_estimate=cost(0, 8 << 20),
    )(y, x0, a_lo, a_hi, b_lo, b_hi)


def low_kernel(y, x_ref, far_lo, far_hi, down_ref, *rest):
    outs, sums = rest[:NY], rest[NY]
    me = y[0]
    for d in range(NY):
        s = (me + d) % NY
        factor = down_ref[:, pl.ds(pl.multiple_of(32 * s, 32), 32), :].reshape(KQ, 128)
        if d == 2:
            x = jnp.concatenate([far_lo[...], far_hi[...]], axis=0)
        else:
            x = x_ref[{0: 0, 1: 1, 3: 2}[d]]
        sums[s] = jnp.dot(x, factor, preferred_element_type=F32)
    lane = lax.broadcasted_iota(jnp.int32, (128, 128), 1)
    for e in range(NY):
        value = (me + e) % NY >= NY // 2
        for pair in range(2):
            a, b = sums[2 * pair], sums[2 * pair + 1]
            keys = jnp.where(lane < 64, a, pltpu.roll(b, 64, 1))
            values = jnp.where(lane < 64, pltpu.roll(a, 64, 1), b)
            outs[e][128 * pair : 128 * pair + 128, :] = jnp.where(value, values, keys)


def low_parts(y, x, far_lo, far_hi, recv):
    quarter = pl.BlockSpec((64, KQ), lambda i, *_: (0, 0))
    return pl.pallas_call(
        low_kernel,
        grid_spec=pltpu.PrefetchScalarGridSpec(
            num_scalar_prefetch=1,
            grid=(1,),
            in_specs=[
                pl.BlockSpec((3, 128, KQ), lambda i, *_: (0, 0, 0)),
                quarter,
                quarter,
                pl.BlockSpec((64, 128, 128), lambda i, *_: (0, 0, 0)),
            ],
            out_specs=[pl.BlockSpec((256, 128), lambda i, *_: (0, 0))] * NY,
            scratch_shapes=[pltpu.VMEM((NY, 128, 128), F32)],
        ),
        out_shape=[jax.ShapeDtypeStruct((256, 128), F32)] * NY,
        compiler_params=params(),
        cost_estimate=cost(2 * 512 * KQ * 128, 5 << 20),
    )(y, x, far_lo, far_hi, recv)


def up_kernel(recv_ref, out_ref):
    r = lax.broadcasted_iota(jnp.int32, (512, 512), 0)
    k = lax.broadcasted_iota(jnp.int32, (512, 512), 1)
    pair, half, seg, rank = r // 256, (r // 128) % 2, (r // 64) % 2, r % 64
    source = (rank // 2) * 16 + (pair * 2 + seg) * 4 + (rank % 2) * 2 + half
    order = (k == source).astype(F32).astype(BF16)
    every = recv_ref[...].reshape(NDP, NC, 16, 128)
    for c in range(NC):
        rows = every[:, c].reshape(512, 128)
        got = jnp.dot(order, rows, preferred_element_type=F32).astype(BF16)
        for p in range(2):
            for h in range(2):
                at = 256 * p + 128 * h
                out_ref[c, p, :, 128 * h : 128 * h + 128] = got[at : at + 128]


def up_rows(recv):
    return pl.pallas_call(
        up_kernel,
        grid=(1,),
        in_specs=[pl.BlockSpec((64, 16, 128), lambda i: (0, 8, 0))],
        out_specs=pl.BlockSpec((NC, 2, 128, COLS), lambda i: (0, 0, 0, 0)),
        out_shape=jax.ShapeDtypeStruct((NC, 2, 128, COLS), BF16),
        compiler_params=params(),
        cost_estimate=cost(2 * 512 * 512 * 256, 1 << 19),
    )(recv)


def near_kernel(x0, a_lo, a_hi, b_lo, b_hi, w0, w1, out):
    @pl.when(pl.program_id(0) == 0)
    def _():
        out[...] = jnp.zeros_like(out)

    x = jnp.concatenate([x0[...], b_lo[...], b_hi[...], a_lo[...], a_hi[...]], axis=0)
    out[:, :COLS] += jnp.dot(x, w0[...], preferred_element_type=F32)
    out[:, COLS:] += jnp.dot(x, w1[...], preferred_element_type=F32)


def near_base(x0, a_lo, a_hi, b_lo, b_hi, w0, w1):
    step = 1024
    half = pl.BlockSpec((64, step), lambda i: (0, i))
    weight = pl.BlockSpec((step, COLS), lambda i: (i, 0))
    return pl.pallas_call(
        near_kernel,
        grid=(K // step,),
        in_specs=[pl.BlockSpec((128, step), lambda i: (0, i))] + [half] * 4 + [weight] * 2,
        out_specs=pl.BlockSpec((384, 512), lambda i: (0, 0)),
        out_shape=jax.ShapeDtypeStruct((384, 512), F32),
        compiler_params=params(),
        cost_estimate=cost(2 * 384 * K * 512, 15 << 20),
    )(x0, a_lo, a_hi, b_lo, b_hi, w0, w1)


def quarter_weight(offset):
    return pl.BlockSpec(
        (8, None, 64, COLS), lambda i, y: (i % 4, (y[0] + offset(i // 4)) % NY, 0, 0)
    )


def far_kernel(y, lo0, hi0, lo1, hi1, w0, w1, out):
    i = pl.program_id(0)

    @pl.when(i == 0)
    def _():
        out[...] = jnp.zeros_like(out)

    lo = jnp.where(i < 4, lo0[...], lo1[...])
    hi = jnp.where(i < 4, hi0[...], hi1[...])
    x = jnp.concatenate([lo, hi], axis=0)
    out[:, :COLS] += jnp.dot(x, w0[...].reshape(512, COLS), preferred_element_type=F32)
    out[:, COLS:] += jnp.dot(x, w1[...].reshape(512, COLS), preferred_element_type=F32)


def far_base(y, lo0, hi0, lo1, hi1, w0, w1):
    first = pl.BlockSpec((64, 512), lambda i, y: (0, jnp.minimum(i, 3)))
    then = pl.BlockSpec(
        (None, 64, 512),
        lambda i, y: (jnp.maximum(i - 4, 0) // 4, 0, jnp.maximum(i - 4, 0) % 4),
    )
    weight = quarter_weight(lambda j: j)
    return pl.pallas_call(
        far_kernel,
        grid_spec=pltpu.PrefetchScalarGridSpec(
            num_scalar_prefetch=1,
            grid=(12,),
            in_specs=[first, first, then, then, weight, weight],
            out_specs=pl.BlockSpec((128, 512), lambda i, y: (0, 0)),
        ),
        out_shape=jax.ShapeDtypeStruct((128, 512), F32),
        compiler_params=params(),
        cost_estimate=cost(2 * 128 * 3 * KQ * 512, 8 << 20),
    )(y, lo0, hi0, lo1, hi1, w0, w1)


def last_kernel(yc, lo, hi, w0, w1, near, far, p0, p1, p2, p3, up, out, out_partner, total):
    i = pl.program_id(0)
    me, core = yc[0], yc[1]

    @pl.when(i == 0)
    def _():
        total[...] = far[...]

    x = jnp.concatenate([lo[...], hi[...]], axis=0)
    total[:, :COLS] += jnp.dot(x, w0[...].reshape(512, COLS), preferred_element_type=F32)
    total[:, COLS:] += jnp.dot(x, w1[...].reshape(512, COLS), preferred_element_type=F32)

    @pl.when(i == 3)
    def _():
        low = (p0[...] + p1[...] + p2[...] + p3[...]).astype(BF16).astype(F32)
        left = lax.broadcasted_iota(jnp.int32, (128, 128), 1) < 64
        for d in range(NY):
            s = (me + d) % NY
            pair = s // 2
            both = jnp.where(pair == 0, low[:128], low[128:])
            mine = jnp.where(left == (s % 2 == 0), both, 0.0).astype(BF16)
            if d == 2:
                base = total[...]
            else:
                at = {0: 0, 1: 128, 3: 256}[d]
                base = near[at : at + 128, :]
            own = jnp.dot(mine, up[core, pair], preferred_element_type=F32)
            other = jnp.dot(mine, up[1 - core, pair], preferred_element_type=F32)
            out[s, core] = (base[:, :COLS] + own).astype(BF16)
            out_partner[s] = (base[:, COLS:] + other).astype(BF16)


def last(yc, lo, hi, w0, w1, near, far, parts, up):
    quarter = pl.BlockSpec((64, 512), lambda i, y: (0, i))
    weight = quarter_weight(lambda j: 3)

    def whole(*shape):
        return pl.BlockSpec(shape, lambda i, y: (0,) * len(shape))

    return pl.pallas_call(
        last_kernel,
        grid_spec=pltpu.PrefetchScalarGridSpec(
            num_scalar_prefetch=1,
            grid=(4,),
            in_specs=[quarter, quarter, weight, weight, whole(384, 512), whole(128, 512)]
            + [whole(256, 128)] * 4
            + [whole(NC, 2, 128, COLS)],
            out_specs=[whole(NY, NC, 128, COLS), whole(NY, 128, COLS)],
            scratch_shapes=[pltpu.VMEM((128, 512), F32)],
        ),
        out_shape=[
            jax.ShapeDtypeStruct((NY, NC, 128, COLS), BF16),
            jax.ShapeDtypeStruct((NY, 128, COLS), BF16),
        ],
        compiler_params=params(),
        cost_estimate=cost(2 * 128 * KQ * 512, 6 << 20),
    )(yc, lo, hi, w0, w1, near, far, *parts, up)


def on_device(tokens, weight, down, up, apr, rps):
    y, c = lax.axis_index("y"), lax.axis_index("c")
    yv = y.reshape(1).astype(jnp.int32)
    yc = jnp.stack([y, c]).astype(jnp.int32)

    lo, hi = tokens[:64], tokens[64:]
    a_lo, b_hi = shift(lo, "y", 1), shift(hi, "y", -1)
    a_hi, b_lo = shift(hi, "y", 1), shift(lo, "y", -1)

    rows = up.reshape(64, 4, 128).astype(F32)
    send = pack(apr, rps, down, jnp.concatenate([rows, rows], axis=1))
    recv = lax.all_to_all(send, ("z", "x", "c"), 0, 0)
    partner_weight = shift(weight, "c", 1)

    lo0, lo12, lo3 = [shift(v, "y", 1) for v in split_quarters(a_lo, (yv + 1) % NY)]
    hi0, hi12, hi3 = [shift(v, "y", -1) for v in split_quarters(b_hi, (yv + 3) % NY)]

    mine = own_quarter(yv, tokens, a_lo, a_hi, b_lo, b_hi)
    near = near_base(tokens, a_lo, a_hi, b_lo, b_hi, weight, partner_weight)
    w0 = weight.reshape(32, NY, 64, COLS)
    w1 = partner_weight.reshape(32, NY, 64, COLS)

    parts = low_parts(yv, mine, lo0, hi0, recv)
    parts = [parts[0]] + [shift(parts[e], "y", e) for e in (1, 2, 3)]
    up_sorted = up_rows(recv)
    far = far_base(yv, lo0, hi0, lo12, hi12, w0, w1)
    out, out_partner = last(yc, lo3, hi3, w0, w1, near, far, parts, up_sorted)
    theirs = shift(out_partner, "c", 1)
    zero = jnp.zeros((), jnp.int32)
    out = lax.dynamic_update_slice(
        out, theirs[:, None], (zero, (1 - c).astype(jnp.int32), zero, zero)
    )
    return out.reshape(NY * NC * 128, COLS)


def solution(mesh):
    axes = Mesh(mesh.devices.reshape(NZ, NX, NY, NC), ("z", "x", "y", "c"))
    every = ("z", "x", "y", "c")
    placed = (
        P(every, None),
        P(None, ("y", "c")),
        P(None, every, None),
        P(None, ("z", "x"), ("y", "c")),
        P(),
        P(),
    )
    return jax.shard_map(
        on_device,
        mesh=axes,
        in_specs=placed,
        out_specs=P(("z", "x"), ("y", "c")),
        check_vma=False,
    )
```

time: 396 us -> 126 us (0.32)
  waiting for transfers between devices: 315 us -> 46.7 us
  Pallas kernels: 0 us -> 34.5 us
  starting transfers between devices: 0.09 us -> 33 us
  blocking collectives: 28.6 us -> 0 us
  matrix products: 15.4 us -> 0 us
  between operations: 13.2 us -> 0.19 us
  local copies, waits for them, and re-layouts: 21.1 us -> 11.1 us
    all_gather x3 -> x0, waiting for transfers between devices: 315 us -> none  [the longest x1 149 us: on_device(): lax.all_gather(adapter_down_weight, 'dp', axis=1, tiled=True)]
    ppermute x0 -> x15, waiting for transfers between devices: none -> 46.7 us  [shift(): return lax.ppermute(x, axis, [(i, (i + by) % n) for i in range(n)])]
    pallas_call x0 -> x9, Pallas kernels: none -> 34.5 us  [the longest x1 9.25 us: near_base(): pl.pallas_call(near_kernel, grid=(K // step,), in_specs=[pl.BlockSpec((12...]
    psum x1 -> x0, blocking collectives: 28.6 us -> none  [on_device(): rank_output = lax.psum(partial_low, 'mp').astype(jnp.bfloat16)]
    ppermute x0 -> x15, starting transfers between devices: none -> 20 us  [shift(): return lax.ppermute(x, axis, [(i, (i + by) % n) for i in range(n)])]
    dot_general x3 -> x0, matrix products: 15.4 us -> none  [the longest x1 12.3 us: on_device(): jnp.dot(gathered, key_value_weight, preferred_element_type=jnp.float32)]
    all_to_all x0 -> x1, starting transfers between devices: none -> 13 us  [on_device(): recv = lax.all_to_all(send, ('z', 'x', 'c'), 0, 0)]
    gather x3 -> x0, local copies, waits for them, and re-layouts: 10.4 us -> none  [the longest x1 7.93 us: on_device(): jnp.take(lax.all_gather(adapter_down_weight, 'dp', axis=1, tiled=True), l...]
  transfers between devices with their start and end apart: 3 -> 16, of which waited for: 3 -> 4; matrix products, arithmetic and copies ran while one was open for 3% -> 3% of each run, Pallas kernels for 0% -> 23%
where the time goes in v1:
time: 126 us
  waiting for transfers between devices  46.7 us (37%)
  Pallas kernels  34.5 us (27%)
  starting transfers between devices  33 us (26%)
  local copies, waits for them, and re-layouts  11.1 us (9%)
    ppermute x15, waiting for transfers between devices, shift(): return lax.ppermute(x, axis, [(i, (i + by) % n) for i in range(n)])  46.7 us
    ppermute x15, starting transfers between devices, shift(): return lax.ppermute(x, axis, [(i, (i + by) % n) for i in range(n)])  20 us
    all_to_all x1, starting transfers between devices, on_device(): recv = lax.all_to_all(send, ('z', 'x', 'c'), 0, 0)  13 us
    pallas_call x1, Pallas kernels, near_base(): pl.pallas_call(near_kernel, grid=(K // step,), in_specs=[pl.BlockSpec((12...  9.25 us
    pallas_call x1, Pallas kernels, far_base(): pl.pallas_call(far_kernel, grid_spec=pltpu.PrefetchScalarGridSpec(num_sca...  8.59 us
    unnamed x14, local copies, waits for them, and re-layouts  6.4 us
    pallas_call x1, Pallas kernels, last(): pl.pallas_call(last_kernel, grid_spec=pltpu.PrefetchScalarGridSpec(num_sc...  4.74 us
    pallas_call x2, Pallas kernels, split_quarters(): pl.pallas_call(split_kernel, grid_spec=pltpu.PrefetchScalarGridSpec(num_s...  4.49 us
  transfers between devices with their start and end apart: 16, of which 4 were waited for; matrix products, arithmetic and copies ran while one was open for 3% of the time, Pallas kernels for 23%

profile of v1, /device:TPU:1, one launch (start us, length us, event | category | flops | bytes accessed | tf_op | source)
XLA Modules:
  0.0 125.7 jit_solution(2772934463524483025)
XLA Ops:
  0.0 0.9 convert_element_type.4
  0.9 0.1 maximum_convert_fusion.up_ref
  1.0 0.0 copy-start.4
  1.0 1.0 copy-done.4
  2.0 0.7 copy-done.5
  2.7 0.7 copy-done.6
  3.3 1.5 %shard_map.69 = bf16[64,144,128]{2,1,0:T(8,128)(2,1)S(1)} custom-call(s32[128]{0:T(128)S(1)} %copy-done.6, s32[256]{0:T(256)S(1)} %copy-done.5, bf16[64,32,128]{2,1,0:T(8,128)(2,1)S(1)} %copy-done.4, f32[64,8,128]{2,1,0:T(8,128)S(1)} %maximum_convert_fusion.up_ref), custom_call_target="tpu_custom_call" | custom-call | bytes 3145728 | tf_op jit(solution)/shard_map/pallas_call | solution.py:53
  4.8 1.5 %copy-done.1 = bf16[64,144,128]{2,1,0:T(8,128)(2,1)} copy-done((bf16[64,144,128]{2,1,0:T(8,128)(2,1)}, bf16[64,144,128]{2,1,0:T(8,128)(2,1)S(1)}, u32[]{:S(2)}) %copy-start.1) | copy-done | bytes 2359320
  6.3 13.0 %all-to-all-start = ((bf16[64,144,128]{2,1,0:T(8,128)(2,1)}), bf16[64,144,128]{2,1,0:T(8,128)(2,1)S(1)}, u32[]{:S(2)}, u32[]{:S(2)}) async-start(bf16[64,144,128]{2,1,0:T(8,128)(2,1)} %copy-done.1), calls=%async_computation | async-start | bytes 4718592 | tf_op jit(solution)/shard_map/all_to_all | solution.py:351
  19.3 0.5 collective-permute-start.4
  19.8 3.1 %fusion = (bf16[64,8192]{1,0:T(8,128)(2,1)}, bf16[64,8192]{1,0:T(8,128)(2,1)}) fusion(bf16[128,8192]{1,0:T(8,128)(2,1)} %x0.3), kind=kLoop, calls=%fused_computation.3 | loop fusion | bytes 4194304 | tf_op jit(solution)/shard_map/slice | solution.py:345
  22.9 2.7 %collective-permute-start.2 = (bf16[64,8192]{1,0:T(8,128)(2,1)}, bf16[64,8192]{1,0:T(8,128)(2,1)S(1)}, u32[]{:S(2)}, u32[]{:S(2)}) collective-permute-start(bf16[64,8192]{1,0:T(8,128)(2,1)} %get-tuple-element.29), channel_id=1, source_target_pairs={{0,6},{2,0},{4,2},{6,4},{1,7},{3,1},{5,3},{7,5},{8,14},{10,8},{12,... | collective-permute-start | bytes 3145736 | tf_op jit(solution)/shard_map/ppermute | solution.py:32
  25.6 0.0 collective-permute-start
  25.6 0.0 collective-permute-start.5
  25.7 2.7 %collective-permute-start.6 = (bf16[64,8192]{1,0:T(8,128)(2,1)}, bf16[64,8192]{1,0:T(8,128)(2,1)}, u32[]{:S(2)}, u32[]{:S(2)}) collective-permute-start(bf16[64,8192]{1,0:T(8,128)(2,1)} %get-tuple-element.30), channel_id=1, source_target_pairs={{0,6},{2,0},{4,2},{6,4},{1,7},{3,1},{5,3},{7,5},{8,14},{10,8},{12,... | collective-permute-start | bytes 3145736 | tf_op jit(solution)/shard_map/ppermute | solution.py:32
  28.4 20.1 %collective-permute-done.2.x_ref.b_hi = bf16[64,8192]{1,0:T(8,128)(2,1)S(1)} collective-permute-done((bf16[64,8192]{1,0:T(8,128)(2,1)}, bf16[64,8192]{1,0:T(8,128)(2,1)S(1)}, u32[]{:S(2)}, u32[]{:S(2)}) %collective-permute-start.2) | collective-permute-done | bytes 1048608 | tf_op jit(solution)/shard_map/ppermute | solution.py:32
  48.5 1.7 %shard_map.65 = (bf16[64,2048]{1,0:T(8,128)(2,1)}, bf16[2,64,2048]{2,1,0:T(8,128)(2,1)}, bf16[64,2048]{1,0:T(8,128)(2,1)}) custom-call(s32[1]{0:T(128)S(6)} %select_n.15.first, bf16[64,8192]{1,0:T(8,128)(2,1)S(1)} %collective-permute-done.2.x_ref.b_hi), custom_call_target="tpu_custom_call" | custom-call | bytes 2097152 | tf_op jit(solution)/shard_map/pallas_call | solution.py:95
  50.2 3.3 %collective-permute-start.10 = (bf16[2,64,2048]{2,1,0:T(8,128)(2,1)}, bf16[2,64,2048]{2,1,0:T(8,128)(2,1)}, u32[]{:S(2)}, u32[]{:S(2)}) collective-permute-start(bf16[2,64,2048]{2,1,0:T(8,128)(2,1)} %get-tuple-element.22), channel_id=1, source_target_pairs={{0,6},{2,0},{4,2},{6,4},{1,7},{3,1},{5,3},{7,5},{8,14},{10,8},{12,... | collective-permute-start | bytes 1572872 | tf_op jit(solution)/shard_map/ppermute | solution.py:32
  53.5 0.0 collective-permute-done.x_ref.a_lo
  53.5 2.8 %shard_map.64 = (bf16[64,2048]{1,0:T(8,128)(2,1)}, bf16[2,64,2048]{2,1,0:T(8,128)(2,1)}, bf16[64,2048]{1,0:T(8,128)(2,1)}) custom-call(s32[1]{0:T(128)S(6)} %select_n.14.first, bf16[64,8192]{1,0:T(8,128)(2,1)} %collective-permute-done.x_ref.a_lo), custom_call_target="tpu_custom_call" | custom-call | bytes 2097152 | tf_op jit(solution)/shard_map/pallas_call | solution.py:95
  56.3 0.0 collective-permute-start.9
  56.3 17.8 %collective-permute-done.5.a_hi = bf16[64,8192]{1,0:T(8,128)(2,1)} collective-permute-done((bf16[64,8192]{1,0:T(8,128)(2,1)}, bf16[64,8192]{1,0:T(8,128)(2,1)}, u32[]{:S(2)}, u32[]{:S(2)}) %collective-permute-start.5) | collective-permute-done | bytes 1048608 | tf_op jit(solution)/shard_map/ppermute | solution.py:32
  74.1 0.0 collective-permute-start.8
  74.1 0.0 collective-permute-done.6.b_lo
  74.1 1.5 %collective-permute-start.7 = (bf16[64,2048]{1,0:T(8,128)(2,1)}, bf16[64,2048]{1,0:T(8,128)(2,1)}, u32[]{:S(2)}, u32[]{:S(2)}) collective-permute-start(bf16[64,2048]{1,0:T(8,128)(2,1)} %get-tuple-element.19), channel_id=1, source_target_pairs={{0,2},{2,4},{4,6},{6,0},{1,3},{3,5},{5,7},{7,1},{8,10},{10,12},{12... | collective-permute-start | bytes 786440 | tf_op jit(solution)/shard_map/ppermute | solution.py:32
  75.5 0.1 pad_add_fusion.yc
  75.6 3.4 %shard_map.68.x_ref = bf16[3,128,2048]{2,1,0:T(8,128)(2,1)S(1)} custom-call(s32[1]{0:T(128)} %bitcast.y, bf16[128,8192]{1,0:T(8,128)(2,1)} %x0.3, bf16[64,8192]{1,0:T(8,128)(2,1)} %collective-permute-done.x_ref.a_lo, bf16[64,8192]{1,0:T(8,128)(2,1)} %collective-permute-done.5.a_hi, bf16[64,8192]{1,0:T(8,128)(2,1)} %collective-permute-done.6.b_lo, ...), custom_call_target="tpu_custom_call" | custom-call | bytes 8388608 | tf_op jit(solution)/shard_map/pallas_call | solution.py:130
  79.1 1.2 copy-done.2
  80.2 7.6 %collective-permute-done.8.hi0.far_hi = bf16[64,2048]{1,0:T(8,128)(2,1)} collective-permute-done((bf16[64,2048]{1,0:T(8,128)(2,1)}, bf16[64,2048]{1,0:T(8,128)(2,1)}, u32[]{:S(2)}, u32[]{:S(2)}) %collective-permute-start.8) | collective-permute-done | bytes 262176 | tf_op jit(solution)/shard_map/ppermute | solution.py:32
  87.8 3.4 %collective-permute-start.3 = (bf16[64,2048]{1,0:T(8,128)(2,1)}, bf16[64,2048]{1,0:T(8,128)(2,1)}, u32[]{:S(2)}, u32[]{:S(2)}) collective-permute-start(bf16[64,2048]{1,0:T(8,128)(2,1)} %get-tuple-element.18), channel_id=1, source_target_pairs={{0,6},{2,0},{4,2},{6,4},{1,7},{3,1},{5,3},{7,5},{8,14},{10,8},{12,... | collective-permute-start | bytes 786440 | tf_op jit(solution)/shard_map/ppermute | solution.py:32
  91.2 0.0 collective-permute-start.1
  91.3 1.4 %copy-done.3 = bf16[3,128,2048]{2,1,0:T(8,128)(2,1)S(1)} copy-done((bf16[3,128,2048]{2,1,0:T(8,128)(2,1)S(1)}, bf16[3,128,2048]{2,1,0:T(8,128)(2,1)}, u32[]{:S(2)}) %copy-start.3) | copy-done | bytes 1572888
  92.7 2.1 %shard_map.70 = (f32[256,128]{1,0:T(8,128)S(1)}, f32[256,128]{1,0:T(8,128)S(1)}, f32[256,128]{1,0:T(8,128)S(1)}, f32[256,128]{1,0:T(8,128)S(1)}) custom-call(s32[1]{0:T(128)} %bitcast.y, bf16[3,128,2048]{2,1,0:T(8,128)(2,1)S(1)} %copy-done.3, bf16[64,2048]{1,0:T(8,128)(2,1)} %collective-permute-done.7.lo0.far_lo, ...), custom_call_target="tpu_custom_call" | custom-call | flops 268435456 | bytes 5242880 | tf_op jit(solution)/shard_map/pallas_call | solution.py:167
  94.7 0.1 collective-permute-start.11
  94.8 3.8 %collective-permute-start.12 = (f32[256,128]{1,0:T(8,128)S(1)}, f32[256,128]{1,0:T(8,128)S(1)}, u32[]{:S(2)}, u32[]{:S(2)}) collective-permute-start(f32[256,128]{1,0:T(8,128)S(1)} %get-tuple-element.25), channel_id=1, source_target_pairs={{0,4},{2,6},{4,0},{6,2},{1,5},{3,7},{5,1},{7,3},{8,12},{10,14},{12... | collective-permute-start | bytes 393224 | tf_op jit(solution)/shard_map/ppermute | solution.py:32
  98.7 0.0 collective-permute-done.4.w1
  98.7 0.0 collective-permute-start.13
  98.7 9.2 %shard_map.66.near = f32[384,512]{1,0:T(8,128)S(1)} custom-call(bf16[128,8192]{1,0:T(8,128)(2,1)} %x0.3, bf16[64,8192]{1,0:T(8,128)(2,1)} %collective-permute-done.x_ref.a_lo, bf16[64,8192]{1,0:T(8,128)(2,1)} %collective-permute-done.5.a_hi, bf16[64,8192]{1,0:T(8,128)(2,1)} %collective-permute-done.6.b_lo, ...), custom_call_target="tpu_custom_call" | custom-call | flops 3221225472 | bytes 15728640 | tf_op jit(solution)/shard_map/pallas_call | solution.py:229
  108.0 8.6 %shard_map.67.far = f32[128,512]{1,0:T(8,128)S(1)} custom-call(s32[1]{0:T(128)} %bitcast.y, bf16[64,2048]{1,0:T(8,128)(2,1)} %collective-permute-done.7.lo0.far_lo, bf16[64,2048]{1,0:T(8,128)(2,1)} %collective-permute-done.8.hi0.far_hi, bf16[2,64,2048]{2,1,0:T(8,128)(2,1)} %collective-permute-done.9.lo1, bf16[2,64,2048]{2,1,0:T(8,128)(2,1)} %collective-permute-done.10.hi1, ...), custom_call_target="tpu_custom_call" | custom-call | flops 805306368 | bytes 8388608 | tf_op jit(solution)/shard_map/pallas_call | solution.py:267
  116.6 0.5 shard_map.71.up
  117.0 0.0 collective-permute-done.3.hi
  117.0 0.0 collective-permute-done.1.lo
  117.1 0.0 collective-permute-done.12.p2
  117.1 0.0 collective-permute-done.13.p3
  117.1 4.7 %shard_map.72 = (bf16[4,2,128,256]{3,2,1,0:T(8,128)(2,1)}, bf16[4,128,256]{2,1,0:T(8,128)(2,1)S(1)}) custom-call(s32[2]{0:T(128)S(1)} %pad_add_fusion.yc, bf16[64,2048]{1,0:T(8,128)(2,1)} %collective-permute-done.1.lo, bf16[64,2048]{1,0:T(8,128)(2,1)} %collective-permute-done.3.hi, bf16[32,4,64,256]{3,2,1,0:T(8,128)(2,1)} %bitcast.9, ...), custom_call_target="tpu_custom_call" | custom-call | flops 268435456 | bytes 6291456 | tf_op jit(solution)/shard_map/pallas_call | solution.py:320
  121.8 2.0 %collective-permute-start.14 = (bf16[4,128,256]{2,1,0:T(8,128)(2,1)S(1)}, bf16[4,128,256]{2,1,0:T(8,128)(2,1)S(1)}, u32[]{:S(2)}, u32[]{:S(2)}) collective-permute-start(bf16[4,128,256]{2,1,0:T(8,128)(2,1)S(1)} %get-tuple-element.28), channel_id=1, source_target_pairs={{0,1},{1,0},{2,3},{3,2},{4,5},{5,4},{6,7},{7,6},{8,9},{9,8},{10,11... | collective-permute-start | bytes 786440 | tf_op jit(solution)/shard_map/ppermute | solution.py:32
  123.8 1.2 collective-permute-done.14
  124.9 0.7 bitcast_dynamic-update-slice_fusion
  (12 shorter events, 0.0 us)
Async XLA Ops:
  1.0 1.0 copy-start.4
  2.0 0.7 copy-start.5
  2.7 0.7 copy-start.6
  4.8 1.5 %copy-start.1 = (bf16[64,144,128]{2,1,0:T(8,128)(2,1)}, bf16[64,144,128]{2,1,0:T(8,128)(2,1)S(1)}, u32[]{:S(2)}) copy-start(bf16[64,144,128]{2,1,0:T(8,128)(2,1)S(1)} %shard_map.69) | copy-start | bytes 7077892
  6.3 84.9 %all-to-all-start = ((bf16[64,144,128]{2,1,0:T(8,128)(2,1)}), bf16[64,144,128]{2,1,0:T(8,128)(2,1)S(1)}, u32[]{:S(2)}, u32[]{:S(2)}) async-start(bf16[64,144,128]{2,1,0:T(8,128)(2,1)} %copy-done.1), calls=%async_computation | async-start | bytes 4718592 | tf_op jit(solution)/shard_map/all_to_all | solution.py:351
  19.3 79.4 %collective-permute-start.4 = (bf16[8192,256]{1,0:T(8,128)(2,1)}, bf16[8192,256]{1,0:T(8,128)(2,1)}, u32[]{:S(2)}, u32[]{:S(2)}) collective-permute-start(bf16[8192,256]{1,0:T(8,128)(2,1)} %w0.1), channel_id=1, source_target_pairs={{0,1},{1,0},{2,3},{3,2},{4,5},{5,4},{6,7},{7,6},{8,9},{9,8},{10,11... | collective-permute-start | bytes 12582920 | tf_op jit(solution)/shard_map/ppermute | solution.py:32
  22.9 25.6 %collective-permute-start.2 = (bf16[64,8192]{1,0:T(8,128)(2,1)}, bf16[64,8192]{1,0:T(8,128)(2,1)S(1)}, u32[]{:S(2)}, u32[]{:S(2)}) collective-permute-start(bf16[64,8192]{1,0:T(8,128)(2,1)} %get-tuple-element.29), channel_id=1, source_target_pairs={{0,6},{2,0},{4,2},{6,4},{1,7},{3,1},{5,3},{7,5},{8,14},{10,8},{12,... | collective-permute-start | bytes 3145736 | tf_op jit(solution)/shard_map/ppermute | solution.py:32
  25.6 27.8 %collective-permute-start = (bf16[64,8192]{1,0:T(8,128)(2,1)}, bf16[64,8192]{1,0:T(8,128)(2,1)}, u32[]{:S(2)}, u32[]{:S(2)}) collective-permute-start(bf16[64,8192]{1,0:T(8,128)(2,1)} %get-tuple-element.30), channel_id=1, source_target_pairs={{0,2},{2,4},{4,6},{6,0},{1,3},{3,5},{5,7},{7,1},{8,10},{10,12},{12... | collective-permute-start | bytes 3145736 | tf_op jit(solution)/shard_map/ppermute | solution.py:32
  25.6 48.4 %collective-permute-start.5 = (bf16[64,8192]{1,0:T(8,128)(2,1)}, bf16[64,8192]{1,0:T(8,128)(2,1)}, u32[]{:S(2)}, u32[]{:S(2)}) collective-permute-start(bf16[64,8192]{1,0:T(8,128)(2,1)} %get-tuple-element.29), channel_id=1, source_target_pairs={{0,2},{2,4},{4,6},{6,0},{1,3},{3,5},{5,7},{7,1},{8,10},{10,12},{12... | collective-permute-start | bytes 3145736 | tf_op jit(solution)/shard_map/ppermute | solution.py:32
  25.7 48.4 %collective-permute-start.6 = (bf16[64,8192]{1,0:T(8,128)(2,1)}, bf16[64,8192]{1,0:T(8,128)(2,1)}, u32[]{:S(2)}, u32[]{:S(2)}) collective-permute-start(bf16[64,8192]{1,0:T(8,128)(2,1)} %get-tuple-element.30), channel_id=1, source_target_pairs={{0,6},{2,0},{4,2},{6,4},{1,7},{3,1},{5,3},{7,5},{8,14},{10,8},{12,... | collective-permute-start | bytes 3145736 | tf_op jit(solution)/shard_map/ppermute | solution.py:32
  50.2 44.6 %collective-permute-start.10 = (bf16[2,64,2048]{2,1,0:T(8,128)(2,1)}, bf16[2,64,2048]{2,1,0:T(8,128)(2,1)}, u32[]{:S(2)}, u32[]{:S(2)}) collective-permute-start(bf16[2,64,2048]{2,1,0:T(8,128)(2,1)} %get-tuple-element.22), channel_id=1, source_target_pairs={{0,6},{2,0},{4,2},{6,4},{1,7},{3,1},{5,3},{7,5},{8,14},{10,8},{12,... | collective-permute-start | bytes 1572872 | tf_op jit(solution)/shard_map/ppermute | solution.py:32
  56.3 38.5 %collective-permute-start.9 = (bf16[2,64,2048]{2,1,0:T(8,128)(2,1)}, bf16[2,64,2048]{2,1,0:T(8,128)(2,1)}, u32[]{:S(2)}, u32[]{:S(2)}) collective-permute-start(bf16[2,64,2048]{2,1,0:T(8,128)(2,1)} %get-tuple-element.21), channel_id=1, source_target_pairs={{0,2},{2,4},{4,6},{6,0},{1,3},{3,5},{5,7},{7,1},{8,10},{10,12},{12... | collective-permute-start | bytes 1572872 | tf_op jit(solution)/shard_map/ppermute | solution.py:32
  74.1 13.8 %collective-permute-start.8 = (bf16[64,2048]{1,0:T(8,128)(2,1)}, bf16[64,2048]{1,0:T(8,128)(2,1)}, u32[]{:S(2)}, u32[]{:S(2)}) collective-permute-start(bf16[64,2048]{1,0:T(8,128)(2,1)} %get-tuple-element.20), channel_id=1, source_target_pairs={{0,6},{2,0},{4,2},{6,4},{1,7},{3,1},{5,3},{7,5},{8,14},{10,8},{12,... | collective-permute-start | bytes 786440 | tf_op jit(solution)/shard_map/ppermute | solution.py:32
  74.1 17.2 %collective-permute-start.7 = (bf16[64,2048]{1,0:T(8,128)(2,1)}, bf16[64,2048]{1,0:T(8,128)(2,1)}, u32[]{:S(2)}, u32[]{:S(2)}) collective-permute-start(bf16[64,2048]{1,0:T(8,128)(2,1)} %get-tuple-element.19), channel_id=1, source_target_pairs={{0,2},{2,4},{4,6},{6,0},{1,3},{3,5},{5,7},{7,1},{8,10},{10,12},{12... | collective-permute-start | bytes 786440 | tf_op jit(solution)/shard_map/ppermute | solution.py:32
  79.1 1.2 copy-start.2
  87.8 29.2 %collective-permute-start.3 = (bf16[64,2048]{1,0:T(8,128)(2,1)}, bf16[64,2048]{1,0:T(8,128)(2,1)}, u32[]{:S(2)}, u32[]{:S(2)}) collective-permute-start(bf16[64,2048]{1,0:T(8,128)(2,1)} %get-tuple-element.18), channel_id=1, source_target_pairs={{0,6},{2,0},{4,2},{6,4},{1,7},{3,1},{5,3},{7,5},{8,14},{10,8},{12,... | collective-permute-start | bytes 786440 | tf_op jit(solution)/shard_map/ppermute | solution.py:32
  91.2 25.8 %collective-permute-start.1 = (bf16[64,2048]{1,0:T(8,128)(2,1)}, bf16[64,2048]{1,0:T(8,128)(2,1)}, u32[]{:S(2)}, u32[]{:S(2)}) collective-permute-start(bf16[64,2048]{1,0:T(8,128)(2,1)} %get-tuple-element.17), channel_id=1, source_target_pairs={{0,2},{2,4},{4,6},{6,0},{1,3},{3,5},{5,7},{7,1},{8,10},{10,12},{12... | collective-permute-start | bytes 786440 | tf_op jit(solution)/shard_map/ppermute | solution.py:32
  91.2 1.4 %copy-start.3 = (bf16[3,128,2048]{2,1,0:T(8,128)(2,1)S(1)}, bf16[3,128,2048]{2,1,0:T(8,128)(2,1)}, u32[]{:S(2)}) copy-start(bf16[3,128,2048]{2,1,0:T(8,128)(2,1)} %copy-done.2) | copy-start | bytes 4718596
  94.7 22.3 %collective-permute-start.11 = (f32[256,128]{1,0:T(8,128)S(1)}, f32[256,128]{1,0:T(8,128)S(1)}, u32[]{:S(2)}, u32[]{:S(2)}) collective-permute-start(f32[256,128]{1,0:T(8,128)S(1)} %get-tuple-element.24), channel_id=1, source_target_pairs={{0,2},{2,4},{4,6},{6,0},{1,3},{3,5},{5,7},{7,1},{8,10},{10,12},{12... | collective-permute-start | bytes 393224 | tf_op jit(solution)/shard_map/ppermute | solution.py:32
  94.8 22.2 %collective-permute-start.12 = (f32[256,128]{1,0:T(8,128)S(1)}, f32[256,128]{1,0:T(8,128)S(1)}, u32[]{:S(2)}, u32[]{:S(2)}) collective-permute-start(f32[256,128]{1,0:T(8,128)S(1)} %get-tuple-element.25), channel_id=1, source_target_pairs={{0,4},{2,6},{4,0},{6,2},{1,5},{3,7},{5,1},{7,3},{8,12},{10,14},{12... | collective-permute-start | bytes 393224 | tf_op jit(solution)/shard_map/ppermute | solution.py:32
  98.7 18.4 %collective-permute-start.13 = (f32[256,128]{1,0:T(8,128)S(1)}, f32[256,128]{1,0:T(8,128)S(1)}, u32[]{:S(2)}, u32[]{:S(2)}) collective-permute-start(f32[256,128]{1,0:T(8,128)S(1)} %get-tuple-element.26), channel_id=1, source_target_pairs={{0,6},{2,0},{4,2},{6,4},{1,7},{3,1},{5,3},{7,5},{8,14},{10,8},{12,... | collective-permute-start | bytes 393224 | tf_op jit(solution)/shard_map/ppermute | solution.py:32
  98.7 9.3 %copy-start = (bf16[8192,256]{1,0:T(8,128)(2,1)S(1)}, bf16[8192,256]{1,0:T(8,128)(2,1)}, u32[]{:S(2)}) copy-start(bf16[8192,256]{1,0:T(8,128)(2,1)} %w0.1) | copy-start | bytes 12582916
  121.8 3.1 %collective-permute-start.14 = (bf16[4,128,256]{2,1,0:T(8,128)(2,1)S(1)}, bf16[4,128,256]{2,1,0:T(8,128)(2,1)S(1)}, u32[]{:S(2)}, u32[]{:S(2)}) collective-permute-start(bf16[4,128,256]{2,1,0:T(8,128)(2,1)S(1)} %get-tuple-element.28), channel_id=1, source_target_pairs={{0,1},{1,0},{2,3},{3,2},{4,5},{5,4},{6,7},{7,6},{8,9},{9,8},{10,11... | collective-permute-start | bytes 786440 | tf_op jit(solution)/shard_map/ppermute | solution.py:32

commit v2 on v1

v2 whole, which is shorter than its diff:
```python
import functools

import jax
import jax.numpy as jnp
from jax import lax
from jax.experimental import pallas as pl
from jax.experimental.pallas import tpu as pltpu
from jax.sharding import Mesh
from jax.sharding import PartitionSpec as P

NZ, NX, NY, NC = 8, 4, 4, 2
NDP = NZ * NX
SEG = 128
K = 8192
RANK = 64
COLS = 256
KQ = K // NY
BF16, F32 = jnp.bfloat16, jnp.float32
VMEM_LIMIT = 20 * 1024 * 1024
PACK = 32
STEP = 2048
AHEAD = 10**11


def params(**kw):
    return pltpu.CompilerParams(vmem_limit_bytes=VMEM_LIMIT, **kw)


def cost(flops, nbytes):
    return pl.CostEstimate(flops=flops, bytes_accessed=nbytes, transcendentals=0)


def in_hbm(x):
    return pltpu.with_memory_space_constraint(x, pltpu.HBM)


def shift(x, axis, by):
    n = {"y": NY, "c": NC}[axis]
    return lax.ppermute(x, axis, [(i, (i + by) % n) for i in range(n)])


def around(x, to_same_core=True):
    pairs = []
    for y in range(NY):
        for c in range(NC):
            to = (y + 1 - 2 * c) % NY
            pairs.append((y * NC + c, to * NC + (c if to_same_core else 1 - c)))
    return lax.ppermute(x, ("y", "c"), pairs)


def pack_kernel(apr, rps, down_ref, up_ref, out_ref, table):
    step = pl.program_id(0)

    @pl.when(step == 0)
    def _():
        def fill(a, carry):
            v = up_ref[a].astype(F32)
            table[a] = jnp.concatenate([v[:, :128], v[:, 128:]] * 2, axis=0)
            return carry

        lax.fori_loop(0, 64, fill, 0, unroll=8)

    row = lax.broadcasted_iota(jnp.int32, (8, 128), 0)

    def to_device(n, carry):
        first = (step * PACK + n) // NC * (NY * NC) + n % NC
        ids = [apr[rps[first + s * NC]] for s in range(NY)]
        for s in range(NY):
            out_ref[n, 32 * s : 32 * s + 32, :] = down_ref[ids[s]]
        ups = [jnp.where(row < 4, table[ids[s]], table[ids[s + 1]]) for s in (0, 2)]
        out_ref[n, 128:144, :] = jnp.concatenate(ups, axis=0).astype(BF16)
        return carry

    lax.fori_loop(0, PACK, to_device, 0, unroll=8)


def pack(apr, rps, down, up):
    return pl.pallas_call(
        pack_kernel,
        grid_spec=pltpu.PrefetchScalarGridSpec(
            num_scalar_prefetch=2,
            grid=(NDP * NC // PACK,),
            in_specs=[
                pl.BlockSpec((64, 32, 128), lambda i, *_: (0, 0, 0)),
                pl.BlockSpec((64, 2, COLS), lambda i, *_: (0, 0, 0)),
            ],
            out_specs=pl.BlockSpec((PACK, 144, 128), lambda i, *_: (i, 0, 0)),
            scratch_shapes=[pltpu.VMEM((64, 8, 128), F32)],
        ),
        out_shape=jax.ShapeDtypeStruct((NDP * NC, 144, 128), BF16),
        compiler_params=pltpu.CompilerParams(vmem_limit_bytes=60 * 1024 * 1024),
        cost_estimate=cost(0, 3 << 20),
    )(apr, rps, down, up)


def quarter_of(x_ref, q, pair):
    at = pair * 512 + (q // 2) * 128
    a = x_ref[:, pl.ds(pl.multiple_of(at, 128), 128)]
    b = x_ref[:, pl.ds(pl.multiple_of(at + 256, 128), 128)]
    low = jnp.concatenate([a[:, :64], b[:, :64]], axis=1)
    high = jnp.concatenate([a[:, 64:], b[:, 64:]], axis=1)
    return jnp.where(q % 2 == 0, low, high)


def split_kernel(first, x_ref, *outs):
    for pair in range(16):
        lanes = slice(128 * pair, 128 * pair + 128)
        for i in range(NY):
            outs[i][:, lanes] = quarter_of(x_ref, (first[0] + i) % NY, pair)


def split_quarters(first, x):
    return pl.pallas_call(
        split_kernel,
        grid_spec=pltpu.PrefetchScalarGridSpec(
            num_scalar_prefetch=1,
            grid=(1,),
            in_specs=[pl.BlockSpec((SEG, K), lambda i, *_: (0, 0))],
            out_specs=[pl.BlockSpec((SEG, KQ), lambda i, *_: (0, 0))] * NY,
        ),
        out_shape=[jax.ShapeDtypeStruct((SEG, KQ), BF16)] * NY,
        compiler_params=params(),
        cost_estimate=cost(AHEAD, 4 * SEG * K),
    )(first, x)


def low_kernel(yc, own, near, other, far, down_ref, after, *rest):
    outs, sums = rest[:NY], rest[NY]
    me, core = yc[0], yc[1]
    for x, d in zip((own, near, other, far), (0, 3 - 2 * core, 1 + 2 * core, 2)):
        s = (me + d) % NY
        factor = down_ref[:, pl.ds(pl.multiple_of(32 * s, 32), 32), :].reshape(KQ, 128)
        sums[s] = jnp.dot(x[...], factor, preferred_element_type=F32)
    lane = lax.broadcasted_iota(jnp.int32, (128, 128), 1)
    for e in range(NY):
        value = (me + e) % NY >= NY // 2
        for pair in range(2):
            a, b = sums[2 * pair], sums[2 * pair + 1]
            keys = jnp.where(lane < 64, a, pltpu.roll(b, 64, 1))
            values = jnp.where(lane < 64, pltpu.roll(a, 64, 1), b)
            outs[e][128 * pair : 128 * pair + 128, :] = jnp.where(value, values, keys)


def low_parts(yc, quarters, recv, after):
    return pl.pallas_call(
        low_kernel,
        grid_spec=pltpu.PrefetchScalarGridSpec(
            num_scalar_prefetch=1,
            grid=(1,),
            in_specs=[pl.BlockSpec((SEG, KQ), lambda i, *_: (0, 0))] * 4
            + [
                pl.BlockSpec((64, 128, 128), lambda i, *_: (0, 0, 0)),
                pl.BlockSpec(memory_space=pl.ANY),
            ],
            out_specs=[pl.BlockSpec((256, 128), lambda i, *_: (0, 0))] * NY,
            scratch_shapes=[pltpu.VMEM((NY, 128, 128), F32)],
        ),
        out_shape=[jax.ShapeDtypeStruct((256, 128), F32)] * NY,
        compiler_params=params(),
        cost_estimate=cost(2 * 512 * KQ * 128, 5 << 20),
    )(yc, *[in_hbm(q) for q in quarters], recv, after)


def up_kernel(recv_ref, out_ref):
    r = lax.broadcasted_iota(jnp.int32, (512, 512), 0)
    k = lax.broadcasted_iota(jnp.int32, (512, 512), 1)
    pair, half, seg, rank = r // 256, (r // 128) % 2, (r // 64) % 2, r % 64
    source = (rank // 2) * 16 + (pair * 2 + seg) * 4 + half * 2 + rank % 2
    order = (k == source).astype(F32).astype(BF16)
    every = recv_ref[...].reshape(NDP, NC, 16, 128)
    for c in range(NC):
        rows = every[:, c].reshape(512, 128)
        got = jnp.dot(order, rows, preferred_element_type=F32).astype(BF16)
        for p in range(2):
            for h in range(2):
                at = 256 * p + 128 * h
                out_ref[c, p, :, 128 * h : 128 * h + 128] = got[at : at + 128]


def up_rows(recv):
    return pl.pallas_call(
        up_kernel,
        grid=(1,),
        in_specs=[pl.BlockSpec((64, 16, 128), lambda i: (0, 8, 0))],
        out_specs=pl.BlockSpec((NC, 2, 128, COLS), lambda i: (0, 0, 0, 0)),
        out_shape=jax.ShapeDtypeStruct((NC, 2, 128, COLS), BF16),
        compiler_params=params(),
        cost_estimate=cost(2 * 512 * 512 * 256, 1 << 19),
    )(recv)


def near_kernel(n, yc, *refs):
    xs, (w0, w1) = refs[:n], refs[n : n + 2]
    out, quarters = refs[-n - 1], refs[-n:]

    @pl.when(pl.program_id(0) == 0)
    def _():
        out[...] = jnp.zeros_like(out)

    for x, quarter in zip(xs, quarters):
        for pair in range(STEP // 512):
            quarter[:, 128 * pair : 128 * pair + 128] = quarter_of(x, yc[0], pair)
    x = jnp.concatenate([x[...] for x in xs], axis=0)
    out[:, :COLS] += jnp.dot(x, w0[...], preferred_element_type=F32)
    out[:, COLS:] += jnp.dot(x, w1[...], preferred_element_type=F32)


def near_base(yc, xs, w0, w1, after=()):
    step, n = STEP, len(xs)
    weight = pl.BlockSpec((step, COLS), lambda i, yc: (i, 0))
    result = pl.pallas_call(
        functools.partial(near_kernel, n),
        grid_spec=pltpu.PrefetchScalarGridSpec(
            num_scalar_prefetch=1,
            grid=(K // step,),
            in_specs=[pl.BlockSpec((SEG, step), lambda i, yc: (0, i))] * n
            + [weight] * 2
            + [pl.BlockSpec(memory_space=pl.ANY)] * len(after),
            out_specs=[pl.BlockSpec((SEG * n, 2 * COLS), lambda i, yc: (0, 0))]
            + [pl.BlockSpec((SEG, step // NY), lambda i, yc: (0, i))] * n,
        ),
        out_shape=[jax.ShapeDtypeStruct((SEG * n, 2 * COLS), F32)]
        + [jax.ShapeDtypeStruct((SEG, KQ), BF16)] * n,
        compiler_params=params(),
        cost_estimate=cost(2 * SEG * n * K * 512, 12 << 20),
    )(yc, *xs, w0, w1, *after)
    return result[0], result[1:]


def quarter_weight(offset):
    return pl.BlockSpec((32, None, 64, COLS), lambda i, yc: (0, (yc[0] + offset(i)) % NY, 0, 0))


def far_kernel(adds, yc, *refs):
    *xs, w0, w1, before, out = refs
    i = pl.program_id(0)

    @pl.when(i == 0)
    def _():
        out[...] = before[...] if adds else jnp.zeros_like(out)

    x = xs[0][...]
    for j in range(1, len(xs)):
        x = jnp.where(i == j, xs[j][...], x)
    out[:, :COLS] += jnp.dot(x, w0[...].reshape(KQ, COLS), preferred_element_type=F32)
    out[:, COLS:] += jnp.dot(x, w1[...].reshape(KQ, COLS), preferred_element_type=F32)


def far_base(yc, xs, start, w0, w1, before, adds):
    weight = quarter_weight(lambda i: start + i)
    n = len(xs)
    return pl.pallas_call(
        functools.partial(far_kernel, adds),
        grid_spec=pltpu.PrefetchScalarGridSpec(
            num_scalar_prefetch=1,
            grid=(n,),
            in_specs=[pl.BlockSpec((SEG, KQ), lambda i, yc: (0, 0))] * n
            + [weight] * 2
            + [whole(SEG, 512) if adds else pl.BlockSpec(memory_space=pl.ANY)],
            out_specs=pl.BlockSpec((SEG, 512), lambda i, yc: (0, 0)),
        ),
        out_shape=jax.ShapeDtypeStruct((SEG, 512), F32),
        compiler_params=params(),
        cost_estimate=cost(2 * SEG * n * KQ * 512, n * (3 << 20)),
    )(yc, *xs, w0, w1, before)


def whole(*shape):
    return pl.BlockSpec(shape, lambda i, yc: (0,) * len(shape))


def sum_kernel(yc, first, second, far, p0, p1, p2, p3, up, out, out_partner):
    me, core = yc[0], yc[1]
    low = (p0[...] + p1[...] + p2[...] + p3[...]).astype(BF16).astype(F32)
    left = lax.broadcasted_iota(jnp.int32, (128, 128), 1) < 64
    bases = (first[:SEG, :], first[SEG:, :], second[...], far[...])
    for d, base in zip((0, 3 - 2 * core, 1 + 2 * core, 2), bases):
        s = (me + d) & 3
        both = jnp.where(s < 2, low[:SEG], low[SEG:])
        mine = jnp.where(left == (s & 1 == 0), both, 0.0).astype(BF16)
        own = jnp.dot(mine, up[core, s // 2], preferred_element_type=F32)
        other = jnp.dot(mine, up[1 - core, s // 2], preferred_element_type=F32)
        out[s] = (base[:, :COLS] + own).astype(BF16)
        out_partner[s] = (base[:, COLS:] + other).astype(BF16)


def sum_up(yc, first, second, far, parts, up):
    return pl.pallas_call(
        sum_kernel,
        grid_spec=pltpu.PrefetchScalarGridSpec(
            num_scalar_prefetch=1,
            grid=(1,),
            in_specs=[whole(2 * SEG, 512), whole(SEG, 512), whole(SEG, 512)]
            + [whole(256, 128)] * NY
            + [whole(NC, 2, 128, COLS)],
            out_specs=[
                pl.BlockSpec((NY, None, SEG, COLS), lambda i, yc: (0, yc[1], 0, 0)),
                whole(NY, SEG, COLS),
            ],
        ),
        out_shape=[
            jax.ShapeDtypeStruct((NY, NC, SEG, COLS), BF16),
            jax.ShapeDtypeStruct((NY, SEG, COLS), BF16),
        ],
        compiler_params=params(),
        cost_estimate=cost(2 * 512 * 128 * 512, 3 << 20),
    )(yc, first, second, far, *parts, up)


def on_device(tokens, weight, down, up, apr, rps):
    y, c = lax.axis_index("y"), lax.axis_index("c")
    yc = jnp.stack([y, c]).astype(jnp.int32)

    near = around(tokens)
    partner_tokens = shift(tokens, "c", 1)
    other = around(partner_tokens, False)
    ahead = ((y + 1 - 2 * c + NY) & 3).reshape(1).astype(jnp.int32)
    q0, q1, q2, q3 = [around(v) for v in split_quarters(ahead, near)]

    send = pack(apr, rps, down, up)
    recv = lax.all_to_all(send, ("z", "x", "c"), 0, 0)
    partner_weight = shift(weight, "c", 1)

    w0 = weight.reshape(32, NY, 64, COLS)
    w1 = partner_weight.reshape(32, NY, 64, COLS)
    first, quarters = near_base(yc, [tokens, near], weight, partner_weight)
    second, more = near_base(yc, [other], weight, partner_weight, (first,))
    far = far_base(yc, [q0, q1, q2], 0, w0, w1, second, False)

    parts = low_parts(yc, [*quarters, *more, q0], recv, far)
    far = far_base(yc, [q3], 3, w0, w1, far, True)
    parts = [parts[0]] + [shift(parts[e], "y", e) for e in (1, 2, 3)]
    up_sorted = up_rows(recv)
    out, out_partner = sum_up(yc, first, second, far, parts, up_sorted)
    theirs = shift(out_partner, "c", 1)
    zero = jnp.zeros((), jnp.int32)
    out = lax.dynamic_update_slice(
        out, theirs[:, None], (zero, (1 - c).astype(jnp.int32), zero, zero)
    )
    return out.reshape(NY * NC * SEG, COLS)


def solution(mesh):
    axes = Mesh(mesh.devices.reshape(NZ, NX, NY, NC), ("z", "x", "y", "c"))
    every = ("z", "x", "y", "c")
    placed = (
        P(every, None),
        P(None, ("y", "c")),
        P(None, every, None),
        P(None, ("z", "x"), ("y", "c")),
        P(),
        P(),
    )
    return jax.shard_map(
        on_device,
        mesh=axes,
        in_specs=placed,
        out_specs=P(("z", "x"), ("y", "c")),
        check_vma=False,
    )
```

time: 126 us -> 93.4 us (0.74)
  waiting for transfers between devices: 46.7 us -> 33 us
  local copies, waits for them, and re-layouts: 11.1 us -> 2.32 us
  starting transfers between devices: 33 us -> 27.3 us
  Pallas kernels: 34.5 us -> 30.2 us
    ppermute x15 -> x6, waiting for transfers between devices: 46.7 us -> 2.45 us  [shift(): return lax.ppermute(x, axis, [(i, (i + by) % n) for i in range(n)])]
    ppermute x0 -> x6, waiting for transfers between devices: none -> 28.1 us  [around(): return lax.ppermute(x, ('y', 'c'), pairs)]
    ppermute x15 -> x6, starting transfers between devices: 20 us -> 9.86 us  [shift(): return lax.ppermute(x, axis, [(i, (i + by) % n) for i in range(n)])]
    pallas_call x4 -> x5, Pallas kernels: 26 us -> 18.5 us  [the longest x2 10.5 us: near_base(): pl.pallas_call(functools.partial(near_kernel, n), grid_spec=pltpu.Prefetc...]
    ppermute x0 -> x6, starting transfers between devices: none -> 5.43 us  [around(): return lax.ppermute(x, ('y', 'c'), pairs)]
    unnamed x14, local copies, waits for them, and re-layouts: 6.4 us -> 1.61 us
    slice x1 -> x0, local copies, waits for them, and re-layouts: 3.08 us -> none  [on_device(): lo, hi = (tokens[:64], tokens[64:])]
    pallas_call x1, Pallas kernels: 1.49 us -> 3.98 us  [pack(): pl.pallas_call(pack_kernel, grid_spec=pltpu.PrefetchScalarGridSpec(num_sc...]
  transfers between devices with their start and end apart: 16 -> 13, of which waited for: 4 -> 8; matrix products, arithmetic and copies ran while one was open for 3% -> 0% of each run, Pallas kernels for 23% -> 31%
where the time goes in v2:
time: 93.4 us; the launch traced here: 93 us
  waiting for transfers between devices  33 us (35%)
  Pallas kernels  30.2 us (32%)
  starting transfers between devices  27.3 us (29%)
  local copies, waits for them, and re-layouts  2.32 us (2%)
    ppermute x6, waiting for transfers between devices, around(): return lax.ppermute(x, ('y', 'c'), pairs)  28.1 us
    all_to_all x1, starting transfers between devices, on_device(): recv = lax.all_to_all(send, ('z', 'x', 'c'), 0, 0)  12 us
    pallas_call x2, Pallas kernels, near_base(): pl.pallas_call(functools.partial(near_kernel, n), grid_spec=pltpu.Prefetc...  10.5 us
    ppermute x6, starting transfers between devices, shift(): return lax.ppermute(x, axis, [(i, (i + by) % n) for i in range(n)])  9.86 us
    pallas_call x2, Pallas kernels, far_base(): pl.pallas_call(functools.partial(far_kernel, adds), grid_spec=pltpu.Prefe...  6.53 us
    ppermute x6, starting transfers between devices, around(): return lax.ppermute(x, ('y', 'c'), pairs)  5.43 us
    pallas_call x1, Pallas kernels, pack(): pl.pallas_call(pack_kernel, grid_spec=pltpu.PrefetchScalarGridSpec(num_sc...  3.98 us
    pallas_call x1, Pallas kernels, split_quarters(): pl.pallas_call(split_kernel, grid_spec=pltpu.PrefetchScalarGridSpec(num_s...  3.8 us
  transfers between devices with their start and end apart: 13, of which 8 were waited for; matrix products, arithmetic and copies ran while one was open for 0% of the time, Pallas kernels for 31%

profile of v2, /device:TPU:1, one launch (start us, length us, event | category | flops | bytes accessed | tf_op | source)
XLA Modules:
  0.0 93.0 jit_solution(4074102552755445370)
XLA Ops:
  0.0 3.2 %collective-permute-start.2 = (bf16[128,8192]{1,0:T(8,128)(2,1)}, bf16[128,8192]{1,0:T(8,128)(2,1)}, u32[]{:S(2)}, u32[]{:S(2)}) collective-permute-start(bf16[128,8192]{1,0:T(8,128)(2,1)} %refs_0_.1), channel_id=1, source_target_pairs={{0,1},{1,0},{2,3},{3,2},{4,5},{5,4},{6,7},{7,6},{8,9},{9,8},{10,11... | collective-permute-start | bytes 6291464 | tf_op jit(solution)/shard_map/ppermute | solution.py:39
  3.2 1.0 %collective-permute-start = (bf16[128,8192]{1,0:T(8,128)(2,1)}, bf16[128,8192]{1,0:T(8,128)(2,1)}, u32[]{:S(2)}, u32[]{:S(2)}) collective-permute-start(bf16[128,8192]{1,0:T(8,128)(2,1)} %refs_0_.1), channel_id=1, source_target_pairs={{0,2},{1,7},{2,4},{3,1},{4,6},{5,3},{6,0},{7,5},{8,10},{9,15},{10,... | collective-permute-start | bytes 6291464 | tf_op jit(solution)/shard_map/ppermute | solution.py:48
  4.2 0.0 collective-permute-start.1
  4.2 4.0 %shard_map.69 = bf16[64,144,128]{2,1,0:T(8,128)(2,1)} custom-call(s32[128]{0:T(128)} %apr.1, s32[256]{0:T(256)} %rps.1, bf16[64,32,128]{2,1,0:T(8,128)(2,1)} %down_ref.1, bf16[64,2,256]{2,1,0:T(2,128)(2,1)} %up_ref.1), custom_call_target="tpu_custom_call" | custom-call | bytes 3145728 | tf_op jit(solution)/shard_map/pallas_call | solution.py:78
  8.2 12.0 %all-to-all-start = ((bf16[64,144,128]{2,1,0:T(8,128)(2,1)}), bf16[64,144,128]{2,1,0:T(8,128)(2,1)S(1)}, u32[]{:S(2)}, u32[]{:S(2)}) async-start(bf16[64,144,128]{2,1,0:T(8,128)(2,1)} %shard_map.69), calls=%async_computation | async-start | bytes 4718592 | tf_op jit(solution)/shard_map/all_to_all | solution.py:321
  20.2 0.0 collective-permute-done.2
  20.2 0.9 collective-permute-start.3
  21.1 7.6 %collective-permute-done.refs_1_.x_ref = bf16[128,8192]{1,0:T(8,128)(2,1)} collective-permute-done((bf16[128,8192]{1,0:T(8,128)(2,1)}, bf16[128,8192]{1,0:T(8,128)(2,1)}, u32[]{:S(2)}, u32[]{:S(2)}) %collective-permute-start) | collective-permute-done | bytes 2097184 | tf_op jit(solution)/shard_map/ppermute | solution.py:48
  28.7 3.8 %shard_map.66 = (bf16[128,2048]{1,0:T(8,128)(2,1)S(1)}, bf16[128,2048]{1,0:T(8,128)(2,1)S(1)}, bf16[128,2048]{1,0:T(8,128)(2,1)S(1)}, bf16[128,2048]{1,0:T(8,128)(2,1)}) custom-call(s32[1]{0:T(128)} %bitcast.2.first, bf16[128,8192]{1,0:T(8,128)(2,1)} %collective-permute-done.refs_1_.x_ref), custom_call_target="tpu_custom_call" | custom-call | flops 99999997952 | bytes 4194304 | tf_op jit(solution)/shard_map/pallas_call | solution.py:113
  32.5 2.1 %collective-permute-start.5 = (bf16[128,2048]{1,0:T(8,128)(2,1)S(1)}, bf16[128,2048]{1,0:T(8,128)(2,1)S(1)}, u32[]{:S(2)}, u32[]{:S(2)}) collective-permute-start(bf16[128,2048]{1,0:T(8,128)(2,1)S(1)} %get-tuple-element.23), channel_id=1, source_target_pairs={{0,2},{1,7},{2,4},{3,1},{4,6},{5,3},{6,0},{7,5},{8,10},{9,15},{10,... | collective-permute-start | bytes 1572872 | tf_op jit(solution)/shard_map/ppermute | solution.py:48
  34.6 0.0 collective-permute-start.6
  34.7 0.0 collective-permute-start.7
  34.7 0.0 collective-permute-done.1.refs_3_.refs_2_
  34.7 1.4 %collective-permute-start.4 = (bf16[128,2048]{1,0:T(8,128)(2,1)}, bf16[128,2048]{1,0:T(8,128)(2,1)}, u32[]{:S(2)}, u32[]{:S(2)}) collective-permute-start(bf16[128,2048]{1,0:T(8,128)(2,1)} %get-tuple-element.22), channel_id=1, source_target_pairs={{0,2},{1,7},{2,4},{3,1},{4,6},{5,3},{6,0},{7,5},{8,10},{9,15},{10,... | collective-permute-start | bytes 1572872 | tf_op jit(solution)/shard_map/ppermute | solution.py:48
  36.1 0.1 pad_add_fusion.yc
  36.2 0.0 copy-done
  36.2 0.0 copy-done.2
  36.2 5.9 %shard_map.64 = (f32[256,512]{1,0:T(8,128)S(1)}, bf16[128,2048]{1,0:T(8,128)(2,1)S(1)}, bf16[128,2048]{1,0:T(8,128)(2,1)S(1)}) custom-call(s32[2]{0:T(128)S(1)} %pad_add_fusion.yc, bf16[128,8192]{1,0:T(8,128)(2,1)S(1)} %copy-done.2, bf16[128,8192]{1,0:T(8,128)(2,1)} %collective-permute-done.refs_1_.x_ref, bf16[8192,256]{1,0:T(8,128)(2,1)S(1)} %copy-done, ...), custom_call_target="tpu_custom_call" | custom-call | flops 2147483648 | bytes 12582912 | tf_op jit(solution)/shard_map/pallas_call | solution.py:211
  42.0 0.0 copy-start.4
  42.0 0.0 copy-start.5
  42.1 10.7 %collective-permute-done.3.refs_0_ = bf16[128,8192]{1,0:T(8,128)(2,1)S(1)} collective-permute-done((bf16[128,8192]{1,0:T(8,128)(2,1)}, bf16[128,8192]{1,0:T(8,128)(2,1)S(1)}, u32[]{:S(2)}, u32[]{:S(2)}) %collective-permute-start.3) | collective-permute-done | bytes 2097184 | tf_op jit(solution)/shard_map/ppermute | solution.py:48
  52.8 4.6 %shard_map.65 = (f32[128,512]{1,0:T(8,128)S(1)}, bf16[128,2048]{1,0:T(8,128)(2,1)S(1)}) custom-call(s32[2]{0:T(128)S(1)} %pad_add_fusion.yc, bf16[128,8192]{1,0:T(8,128)(2,1)S(1)} %collective-permute-done.3.refs_0_, bf16[8192,256]{1,0:T(8,128)(2,1)S(1)} %copy-done, bf16[8192,256]{1,0:T(8,128)(2,1)} %collective-permute-done.1.refs_3_.refs_2_, ...), custom_call_target="tpu_custom_call" | custom-call | flops 1073741824 | bytes 12582912 | tf_op jit(solution)/shard_map/pallas_call | solution.py:211
  57.4 0.0 copy-done.4
  57.4 0.0 copy-done.5
  57.4 0.0 copy-start.6
  57.4 0.8 copy-done.6
  58.2 0.0 collective-permute-done.5.refs_0_.far
  58.2 4.1 %collective-permute-done.6.refs_1_ = bf16[128,2048]{1,0:T(8,128)(2,1)S(1)} collective-permute-done((bf16[128,2048]{1,0:T(8,128)(2,1)S(1)}, bf16[128,2048]{1,0:T(8,128)(2,1)S(1)}, u32[]{:S(2)}, u32[]{:S(2)}) %collective-permute-start.6) | collective-permute-done | bytes 524320 | tf_op jit(solution)/shard_map/ppermute | solution.py:48
  62.3 5.6 %collective-permute-done.7.refs_2_ = bf16[128,2048]{1,0:T(8,128)(2,1)S(1)} collective-permute-done((bf16[128,2048]{1,0:T(8,128)(2,1)S(1)}, bf16[128,2048]{1,0:T(8,128)(2,1)S(1)}, u32[]{:S(2)}, u32[]{:S(2)}) %collective-permute-start.7) | collective-permute-done | bytes 524320 | tf_op jit(solution)/shard_map/ppermute | solution.py:48
  68.0 4.1 %shard_map.67.refs_3_.after = f32[128,512]{1,0:T(8,128)S(1)} custom-call(s32[2]{0:T(128)S(1)} %pad_add_fusion.yc, bf16[128,2048]{1,0:T(8,128)(2,1)S(1)} %collective-permute-done.5.refs_0_.far, bf16[128,2048]{1,0:T(8,128)(2,1)S(1)} %collective-permute-done.6.refs_1_, bf16[128,2048]{1,0:T(8,128)(2,1)S(1)} %collective-permute-done.7.refs_2_, ...), custom_call_target="tpu_custom_call" | custom-call | flops 805306368 | bytes 9437184 | tf_op jit(solution)/shard_map/pallas_call | solution.py:252
  72.1 0.0 copy-start.3
  72.1 0.8 copy-done.3
  72.9 2.5 %all-to-all-done.down_ref.recv_ref = bf16[64,144,128]{2,1,0:T(8,128)(2,1)S(1)} async-done(((bf16[64,144,128]{2,1,0:T(8,128)(2,1)}), bf16[64,144,128]{2,1,0:T(8,128)(2,1)S(1)}, u32[]{:S(2)}, u32[]{:S(2)}) %all-to-all-start) | async-done | bytes 2359328 | tf_op jit(solution)/shard_map/all_to_all | solution.py:321
  75.4 3.4 %shard_map.70 = (f32[256,128]{1,0:T(8,128)S(1)}, f32[256,128]{1,0:T(8,128)S(1)}, f32[256,128]{1,0:T(8,128)S(1)}, f32[256,128]{1,0:T(8,128)S(1)}) custom-call(s32[2]{0:T(128)S(1)} %pad_add_fusion.yc, bf16[128,2048]{1,0:T(8,128)(2,1)} %copy-done.4, bf16[128,2048]{1,0:T(8,128)(2,1)} %copy-done.5, bf16[128,2048]{1,0:T(8,128)(2,1)} %copy-done.6, ...), custom_call_target="tpu_custom_call" | custom-call | flops 268435456 | bytes 5242880 | tf_op jit(solution)/shard_map/pallas_call | solution.py:145
  78.8 0.1 collective-permute-start.8
  78.9 1.6 %collective-permute-start.9 = (f32[256,128]{1,0:T(8,128)S(1)}, f32[256,128]{1,0:T(8,128)S(1)}, u32[]{:S(2)}, u32[]{:S(2)}) collective-permute-start(f32[256,128]{1,0:T(8,128)S(1)} %get-tuple-element.31), channel_id=1, source_target_pairs={{0,4},{2,6},{4,0},{6,2},{1,5},{3,7},{5,1},{7,3},{8,12},{10,14},{12... | collective-permute-start | bytes 393224 | tf_op jit(solution)/shard_map/ppermute | solution.py:39
  80.5 1.5 %collective-permute-start.10 = (f32[256,128]{1,0:T(8,128)S(1)}, f32[256,128]{1,0:T(8,128)S(1)}, u32[]{:S(2)}, u32[]{:S(2)}) collective-permute-start(f32[256,128]{1,0:T(8,128)S(1)} %get-tuple-element.32), channel_id=1, source_target_pairs={{0,6},{2,0},{4,2},{6,4},{1,7},{3,1},{5,3},{7,5},{8,14},{10,8},{12,... | collective-permute-start | bytes 393224 | tf_op jit(solution)/shard_map/ppermute | solution.py:39
  82.0 0.0 collective-permute-done.4.refs_0_
  82.0 0.0 copy-done.1
  82.0 2.4 %shard_map.68.far = f32[128,512]{1,0:T(8,128)S(1)} custom-call(s32[2]{0:T(128)S(1)} %pad_add_fusion.yc, bf16[128,2048]{1,0:T(8,128)(2,1)} %collective-permute-done.4.refs_0_, bf16[32,4,64,256]{3,2,1,0:T(8,128)(2,1)S(1)} %bitcast.11, bf16[32,4,64,256]{3,2,1,0:T(8,128)(2,1)} %bitcast.4.refs_4_.refs_2_, f32[128,512]{1,0:T(8,128)S(1)} %shard_map.67.refs_3_.after), custom_call_target="tpu_custom_call" | custom-call | flops 268435456 | bytes 3145728 | tf_op jit(solution)/shard_map/pallas_call | solution.py:252
  84.4 0.5 shard_map.71.up
  84.9 0.7 collective-permute-done.8.p1
  85.6 0.0 collective-permute-done.9.p2
  85.6 0.6 collective-permute-done.10.p3
  86.1 1.5 %shard_map.72 = (bf16[4,2,128,256]{3,2,1,0:T(8,128)(2,1)}, bf16[4,128,256]{2,1,0:T(8,128)(2,1)S(1)}) custom-call(s32[2]{0:T(128)S(1)} %pad_add_fusion.yc, f32[256,512]{1,0:T(8,128)S(1)} %get-tuple-element.20.refs_3_.first, f32[128,512]{1,0:T(8,128)S(1)} %get-tuple-element.21.refs_5_.second, f32[128,512]{1,0:T(8,128)S(1)} %shard_map.68.far, ...), custom_call_target="tpu_custom_call" | custom-call | flops 67108864 | bytes 3145728 | tf_op jit(solution)/shard_map/pallas_call | solution.py:288
  87.7 3.4 %collective-permute-start.11 = (bf16[4,128,256]{2,1,0:T(8,128)(2,1)S(1)}, bf16[4,128,256]{2,1,0:T(8,128)(2,1)S(1)}, u32[]{:S(2)}, u32[]{:S(2)}) collective-permute-start(bf16[4,128,256]{2,1,0:T(8,128)(2,1)S(1)} %get-tuple-element.34), channel_id=1, source_target_pairs={{0,1},{1,0},{2,3},{3,2},{4,5},{5,4},{6,7},{7,6},{8,9},{9,8},{10,11... | collective-permute-start | bytes 786440 | tf_op jit(solution)/shard_map/ppermute | solution.py:39
  91.1 1.2 %collective-permute-done.11 = bf16[4,128,256]{2,1,0:T(8,128)(2,1)S(1)} collective-permute-done((bf16[4,128,256]{2,1,0:T(8,128)(2,1)S(1)}, bf16[4,128,256]{2,1,0:T(8,128)(2,1)S(1)}, u32[]{:S(2)}, u32[]{:S(2)}) %collective-permute-start.11) | collective-permute-done | bytes 262176 | tf_op jit(solution)/shard_map/ppermute | solution.py:39
  92.3 0.7 bitcast_dynamic-update-slice_fusion
  (3 shorter events, 0.0 us)
Async XLA Ops:
  0.0 20.2 %collective-permute-start.2 = (bf16[128,8192]{1,0:T(8,128)(2,1)}, bf16[128,8192]{1,0:T(8,128)(2,1)}, u32[]{:S(2)}, u32[]{:S(2)}) collective-permute-start(bf16[128,8192]{1,0:T(8,128)(2,1)} %refs_0_.1), channel_id=1, source_target_pairs={{0,1},{1,0},{2,3},{3,2},{4,5},{5,4},{6,7},{7,6},{8,9},{9,8},{10,11... | collective-permute-start | bytes 6291464 | tf_op jit(solution)/shard_map/ppermute | solution.py:39
  3.2 25.5 %collective-permute-start = (bf16[128,8192]{1,0:T(8,128)(2,1)}, bf16[128,8192]{1,0:T(8,128)(2,1)}, u32[]{:S(2)}, u32[]{:S(2)}) collective-permute-start(bf16[128,8192]{1,0:T(8,128)(2,1)} %refs_0_.1), channel_id=1, source_target_pairs={{0,2},{1,7},{2,4},{3,1},{4,6},{5,3},{6,0},{7,5},{8,10},{9,15},{10,... | collective-permute-start | bytes 6291464 | tf_op jit(solution)/shard_map/ppermute | solution.py:48
  4.2 30.5 %collective-permute-start.1 = (bf16[8192,256]{1,0:T(8,128)(2,1)}, bf16[8192,256]{1,0:T(8,128)(2,1)}, u32[]{:S(2)}, u32[]{:S(2)}) collective-permute-start(bf16[8192,256]{1,0:T(8,128)(2,1)} %refs_1_.1), channel_id=1, source_target_pairs={{0,1},{1,0},{2,3},{3,2},{4,5},{5,4},{6,7},{7,6},{8,9},{9,8},{10,11... | collective-permute-start | bytes 12582920 | tf_op jit(solution)/shard_map/ppermute | solution.py:39
  8.2 67.2 %all-to-all-start = ((bf16[64,144,128]{2,1,0:T(8,128)(2,1)}), bf16[64,144,128]{2,1,0:T(8,128)(2,1)S(1)}, u32[]{:S(2)}, u32[]{:S(2)}) async-start(bf16[64,144,128]{2,1,0:T(8,128)(2,1)} %shard_map.69), calls=%async_computation | async-start | bytes 4718592 | tf_op jit(solution)/shard_map/all_to_all | solution.py:321
  20.2 32.5 %collective-permute-start.3 = (bf16[128,8192]{1,0:T(8,128)(2,1)}, bf16[128,8192]{1,0:T(8,128)(2,1)S(1)}, u32[]{:S(2)}, u32[]{:S(2)}) collective-permute-start(bf16[128,8192]{1,0:T(8,128)(2,1)} %collective-permute-done.2), channel_id=1, source_target_pairs={{0,3},{1,6},{2,5},{3,0},{4,7},{5,2},{6,1},{7,4},{8,11},{9,14},{10,... | collective-permute-start | bytes 6291464 | tf_op jit(solution)/shard_map/ppermute | solution.py:48
  28.7 7.4 %copy-start = (bf16[8192,256]{1,0:T(8,128)(2,1)S(1)}, bf16[8192,256]{1,0:T(8,128)(2,1)}, u32[]{:S(2)}) copy-start(bf16[8192,256]{1,0:T(8,128)(2,1)} %refs_1_.1) | copy-start | bytes 12582916
  28.7 7.4 %copy-start.2 = (bf16[128,8192]{1,0:T(8,128)(2,1)S(1)}, bf16[128,8192]{1,0:T(8,128)(2,1)}, u32[]{:S(2)}) copy-start(bf16[128,8192]{1,0:T(8,128)(2,1)} %refs_0_.1) | copy-start | bytes 6291460
  32.5 25.7 %collective-permute-start.5 = (bf16[128,2048]{1,0:T(8,128)(2,1)S(1)}, bf16[128,2048]{1,0:T(8,128)(2,1)S(1)}, u32[]{:S(2)}, u32[]{:S(2)}) collective-permute-start(bf16[128,2048]{1,0:T(8,128)(2,1)S(1)} %get-tuple-element.23), channel_id=1, source_target_pairs={{0,2},{1,7},{2,4},{3,1},{4,6},{5,3},{6,0},{7,5},{8,10},{9,15},{10,... | collective-permute-start | bytes 1572872 | tf_op jit(solution)/shard_map/ppermute | solution.py:48
  34.6 27.7 %collective-permute-start.6 = (bf16[128,2048]{1,0:T(8,128)(2,1)S(1)}, bf16[128,2048]{1,0:T(8,128)(2,1)S(1)}, u32[]{:S(2)}, u32[]{:S(2)}) collective-permute-start(bf16[128,2048]{1,0:T(8,128)(2,1)S(1)} %get-tuple-element.24), channel_id=1, source_target_pairs={{0,2},{1,7},{2,4},{3,1},{4,6},{5,3},{6,0},{7,5},{8,10},{9,15},{10,... | collective-permute-start | bytes 1572872 | tf_op jit(solution)/shard_map/ppermute | solution.py:48
  34.7 33.3 %collective-permute-start.7 = (bf16[128,2048]{1,0:T(8,128)(2,1)S(1)}, bf16[128,2048]{1,0:T(8,128)(2,1)S(1)}, u32[]{:S(2)}, u32[]{:S(2)}) collective-permute-start(bf16[128,2048]{1,0:T(8,128)(2,1)S(1)} %get-tuple-element.25), channel_id=1, source_target_pairs={{0,2},{1,7},{2,4},{3,1},{4,6},{5,3},{6,0},{7,5},{8,10},{9,15},{10,... | collective-permute-start | bytes 1572872 | tf_op jit(solution)/shard_map/ppermute | solution.py:48
  34.7 47.3 %collective-permute-start.4 = (bf16[128,2048]{1,0:T(8,128)(2,1)}, bf16[128,2048]{1,0:T(8,128)(2,1)}, u32[]{:S(2)}, u32[]{:S(2)}) collective-permute-start(bf16[128,2048]{1,0:T(8,128)(2,1)} %get-tuple-element.22), channel_id=1, source_target_pairs={{0,2},{1,7},{2,4},{3,1},{4,6},{5,3},{6,0},{7,5},{8,10},{9,15},{10,... | collective-permute-start | bytes 1572872 | tf_op jit(solution)/shard_map/ppermute | solution.py:48
  42.0 15.4 %copy-start.4 = (bf16[128,2048]{1,0:T(8,128)(2,1)}, bf16[128,2048]{1,0:T(8,128)(2,1)S(1)}, u32[]{:S(2)}) copy-start(bf16[128,2048]{1,0:T(8,128)(2,1)S(1)} %get-tuple-element.26.own) | copy-start | bytes 1572868
  42.0 15.4 %copy-start.5 = (bf16[128,2048]{1,0:T(8,128)(2,1)}, bf16[128,2048]{1,0:T(8,128)(2,1)S(1)}, u32[]{:S(2)}) copy-start(bf16[128,2048]{1,0:T(8,128)(2,1)S(1)} %get-tuple-element.27.near) | copy-start | bytes 1572868
  57.4 0.8 copy-start.6
  72.1 0.8 copy-start.3
  75.4 6.6 %copy-start.1 = (bf16[8192,256]{1,0:T(8,128)(2,1)S(1)}, bf16[8192,256]{1,0:T(8,128)(2,1)}, u32[]{:S(2)}) copy-start(bf16[8192,256]{1,0:T(8,128)(2,1)} %refs_1_.1) | copy-start | bytes 12582916
  78.8 6.8 %collective-permute-start.8 = (f32[256,128]{1,0:T(8,128)S(1)}, f32[256,128]{1,0:T(8,128)S(1)}, u32[]{:S(2)}, u32[]{:S(2)}) collective-permute-start(f32[256,128]{1,0:T(8,128)S(1)} %get-tuple-element.30), channel_id=1, source_target_pairs={{0,2},{2,4},{4,6},{6,0},{1,3},{3,5},{5,7},{7,1},{8,10},{10,12},{12... | collective-permute-start | bytes 393224 | tf_op jit(solution)/shard_map/ppermute | solution.py:39
  78.9 6.7 %collective-permute-start.9 = (f32[256,128]{1,0:T(8,128)S(1)}, f32[256,128]{1,0:T(8,128)S(1)}, u32[]{:S(2)}, u32[]{:S(2)}) collective-permute-start(f32[256,128]{1,0:T(8,128)S(1)} %get-tuple-element.31), channel_id=1, source_target_pairs={{0,4},{2,6},{4,0},{6,2},{1,5},{3,7},{5,1},{7,3},{8,12},{10,14},{12... | collective-permute-start | bytes 393224 | tf_op jit(solution)/shard_map/ppermute | solution.py:39
  80.5 5.7 %collective-permute-start.10 = (f32[256,128]{1,0:T(8,128)S(1)}, f32[256,128]{1,0:T(8,128)S(1)}, u32[]{:S(2)}, u32[]{:S(2)}) collective-permute-start(f32[256,128]{1,0:T(8,128)S(1)} %get-tuple-element.32), channel_id=1, source_target_pairs={{0,6},{2,0},{4,2},{6,4},{1,7},{3,1},{5,3},{7,5},{8,14},{10,8},{12,... | collective-permute-start | bytes 393224 | tf_op jit(solution)/shard_map/ppermute | solution.py:39
  87.7 4.6 %collective-permute-start.11 = (bf16[4,128,256]{2,1,0:T(8,128)(2,1)S(1)}, bf16[4,128,256]{2,1,0:T(8,128)(2,1)S(1)}, u32[]{:S(2)}, u32[]{:S(2)}) collective-permute-start(bf16[4,128,256]{2,1,0:T(8,128)(2,1)S(1)} %get-tuple-element.34), channel_id=1, source_target_pairs={{0,1},{1,0},{2,3},{3,2},{4,5},{5,4},{6,7},{7,6},{8,9},{9,8},{10,11... | collective-permute-start | bytes 786440 | tf_op jit(solution)/shard_map/ppermute | solution.py:39

commit v3 on v2

--- a/solution.py
+++ b/solution.py
@@ -17,7 +17,7 @@
 KQ = K // NY
 BF16, F32 = jnp.bfloat16, jnp.float32
 VMEM_LIMIT = 20 * 1024 * 1024
-PACK = 32
+PACK = 8
 STEP = 2048
 AHEAD = 10**11
 
@@ -48,30 +48,36 @@
     return lax.ppermute(x, ("y", "c"), pairs)
 
 
-def pack_kernel(apr, rps, down_ref, up_ref, out_ref, table):
-    step = pl.program_id(0)
-
-    @pl.when(step == 0)
-    def _():
-        def fill(a, carry):
-            v = up_ref[a].astype(F32)
-            table[a] = jnp.concatenate([v[:, :128], v[:, 128:]] * 2, axis=0)
+def pack_kernel(apr, rps, down_ref, up_ref, out_ref, table, held, sems):
+    def fill(a, carry):
+        v = up_ref[a].astype(F32)
+        table[a] = jnp.concatenate([v[:, :128], v[:, 128:]] * 2, axis=0)
+        return carry
+
+    lax.fori_loop(0, 64, fill, 0, unroll=8)
+    row = lax.broadcasted_iota(jnp.int32, (8, 128), 0)
+
+    def copy(g):
+        part = pl.ds(PACK * g, PACK)
+        return pltpu.make_async_copy(held.at[part], out_ref.at[part], sems.at[g])
+
+    for g in range(NDP * NC // PACK):
+
+        def to_device(n, carry):
+            first = n // NC * (NY * NC) + n % NC
+            ids = [apr[rps[first + s * NC]] for s in range(NY)]
+            for s in range(NY):
+                held[n, 32 * s : 32 * s + 32, :] = down_ref[ids[s]]
+            ups = [
+                jnp.where(row < 4, table[ids[s]], table[ids[s + 1]]) for s in (0, 2)
+            ]
+            held[n, 128:144, :] = jnp.concatenate(ups, axis=0).astype(BF16)
             return carry
 
-        lax.fori_loop(0, 64, fill, 0, unroll=8)
-
-    row = lax.broadcasted_iota(jnp.int32, (8, 128), 0)
-
-    def to_device(n, carry):
-        first = (step * PACK + n) // NC * (NY * NC) + n % NC
-        ids = [apr[rps[first + s * NC]] for s in range(NY)]
-        for s in range(NY):
-            out_ref[n, 32 * s : 32 * s + 32, :] = down_ref[ids[s]]
-        ups = [jnp.where(row < 4, table[ids[s]], table[ids[s + 1]]) for s in (0, 2)]
-        out_ref[n, 128:144, :] = jnp.concatenate(ups, axis=0).astype(BF16)
-        return carry
-
-    lax.fori_loop(0, PACK, to_device, 0, unroll=8)
+        lax.fori_loop(PACK * g, PACK * g + PACK, to_device, 0, unroll=8)
+        copy(g).start()
+    for g in range(NDP * NC // PACK):
+        copy(g).wait()
 
 
 def pack(apr, rps, down, up):
@@ -79,13 +85,17 @@
         pack_kernel,
         grid_spec=pltpu.PrefetchScalarGridSpec(
             num_scalar_prefetch=2,
-            grid=(NDP * NC // PACK,),
+            grid=(1,),
             in_specs=[
                 pl.BlockSpec((64, 32, 128), lambda i, *_: (0, 0, 0)),
                 pl.BlockSpec((64, 2, COLS), lambda i, *_: (0, 0, 0)),
             ],
-            out_specs=pl.BlockSpec((PACK, 144, 128), lambda i, *_: (i, 0, 0)),
-            scratch_shapes=[pltpu.VMEM((64, 8, 128), F32)],
+            out_specs=pl.BlockSpec(memory_space=pl.ANY),
+            scratch_shapes=[
+                pltpu.VMEM((64, 8, 128), F32),
+                pltpu.VMEM((NDP * NC, 144, 128), BF16),
+                pltpu.SemaphoreType.DMA((NDP * NC // PACK,)),
+            ],
         ),
         out_shape=jax.ShapeDtypeStruct((NDP * NC, 144, 128), BF16),
         compiler_params=pltpu.CompilerParams(vmem_limit_bytes=60 * 1024 * 1024),
@@ -124,16 +134,16 @@
     )(first, x)
 
 
-def low_kernel(yc, own, near, other, far, down_ref, after, *rest):
+def low_kernel(yc, x_ref, down_ref, after, *rest):
     outs, sums = rest[:NY], rest[NY]
     me, core = yc[0], yc[1]
-    for x, d in zip((own, near, other, far), (0, 3 - 2 * core, 1 + 2 * core, 2)):
-        s = (me + d) % NY
+    for i, d in enumerate((0, 3 - 2 * core, 1 + 2 * core, 2)):
+        s = (me + d) & 3
         factor = down_ref[:, pl.ds(pl.multiple_of(32 * s, 32), 32), :].reshape(KQ, 128)
-        sums[s] = jnp.dot(x[...], factor, preferred_element_type=F32)
+        sums[s] = jnp.dot(x_ref[i], factor, preferred_element_type=F32)
     lane = lax.broadcasted_iota(jnp.int32, (128, 128), 1)
     for e in range(NY):
-        value = (me + e) % NY >= NY // 2
+        value = ((me + e) & 3) >= 2
         for pair in range(2):
             a, b = sums[2 * pair], sums[2 * pair + 1]
             keys = jnp.where(lane < 64, a, pltpu.roll(b, 64, 1))
@@ -141,14 +151,14 @@
             outs[e][128 * pair : 128 * pair + 128, :] = jnp.where(value, values, keys)
 
 
-def low_parts(yc, quarters, recv, after):
+def low_parts(yc, x, recv, after):
     return pl.pallas_call(
         low_kernel,
         grid_spec=pltpu.PrefetchScalarGridSpec(
             num_scalar_prefetch=1,
             grid=(1,),
-            in_specs=[pl.BlockSpec((SEG, KQ), lambda i, *_: (0, 0))] * 4
-            + [
+            in_specs=[
+                pl.BlockSpec((4, SEG, KQ), lambda i, *_: (0, 0, 0)),
                 pl.BlockSpec((64, 128, 128), lambda i, *_: (0, 0, 0)),
                 pl.BlockSpec(memory_space=pl.ANY),
             ],
@@ -158,7 +168,7 @@
         out_shape=[jax.ShapeDtypeStruct((256, 128), F32)] * NY,
         compiler_params=params(),
         cost_estimate=cost(2 * 512 * KQ * 128, 5 << 20),
-    )(yc, *[in_hbm(q) for q in quarters], recv, after)
+    )(yc, x, recv, after)
 
 
 def up_kernel(recv_ref, out_ref):
@@ -231,38 +241,63 @@
     return pl.BlockSpec((32, None, 64, COLS), lambda i, yc: (0, (yc[0] + offset(i)) % NY, 0, 0))
 
 
-def far_kernel(adds, yc, *refs):
-    *xs, w0, w1, before, out = refs
+def far_kernel(yc, q0, q1, w0, w1, own, near, other, out, stack):
     i = pl.program_id(0)
 
     @pl.when(i == 0)
     def _():
-        out[...] = before[...] if adds else jnp.zeros_like(out)
-
-    x = xs[0][...]
-    for j in range(1, len(xs)):
-        x = jnp.where(i == j, xs[j][...], x)
+        out[...] = jnp.zeros_like(out)
+        for j, x in enumerate((own, near, other, q0)):
+            stack[j] = x[...]
+
+    x = jnp.where(i == 0, q0[...], q1[...])
     out[:, :COLS] += jnp.dot(x, w0[...].reshape(KQ, COLS), preferred_element_type=F32)
     out[:, COLS:] += jnp.dot(x, w1[...].reshape(KQ, COLS), preferred_element_type=F32)
 
 
-def far_base(yc, xs, start, w0, w1, before, adds):
-    weight = quarter_weight(lambda i: start + i)
-    n = len(xs)
-    return pl.pallas_call(
-        functools.partial(far_kernel, adds),
-        grid_spec=pltpu.PrefetchScalarGridSpec(
-            num_scalar_prefetch=1,
-            grid=(n,),
-            in_specs=[pl.BlockSpec((SEG, KQ), lambda i, yc: (0, 0))] * n
-            + [weight] * 2
-            + [whole(SEG, 512) if adds else pl.BlockSpec(memory_space=pl.ANY)],
-            out_specs=pl.BlockSpec((SEG, 512), lambda i, yc: (0, 0)),
+def far_base(yc, q0, q1, w0, w1, quarters):
+    weight = quarter_weight(lambda i: i)
+    return pl.pallas_call(
+        far_kernel,
+        grid_spec=pltpu.PrefetchScalarGridSpec(
+            num_scalar_prefetch=1,
+            grid=(2,),
+            in_specs=[whole(SEG, KQ)] * 2 + [weight] * 2 + [whole(SEG, KQ)] * 3,
+            out_specs=[whole(SEG, 512), whole(4, SEG, KQ)],
+        ),
+        out_shape=[
+            jax.ShapeDtypeStruct((SEG, 512), F32),
+            jax.ShapeDtypeStruct((4, SEG, KQ), BF16),
+        ],
+        compiler_params=params(),
+        cost_estimate=cost(2 * SEG * 2 * KQ * 512, 10 << 20),
+    )(yc, q0, q1, w0, w1, *quarters)
+
+
+def more_kernel(yc, x, w0, w1, before, out):
+    x = x[...]
+    out[:, :COLS] = before[:, :COLS] + jnp.dot(
+        x, w0[...].reshape(KQ, COLS), preferred_element_type=F32
+    )
+    out[:, COLS:] = before[:, COLS:] + jnp.dot(
+        x, w1[...].reshape(KQ, COLS), preferred_element_type=F32
+    )
+
+
+def more_base(yc, x, quarter, w0, w1, before):
+    weight = quarter_weight(lambda i: quarter)
+    return pl.pallas_call(
+        more_kernel,
+        grid_spec=pltpu.PrefetchScalarGridSpec(
+            num_scalar_prefetch=1,
+            grid=(1,),
+            in_specs=[whole(SEG, KQ), weight, weight, whole(SEG, 512)],
+            out_specs=whole(SEG, 512),
         ),
         out_shape=jax.ShapeDtypeStruct((SEG, 512), F32),
         compiler_params=params(),
-        cost_estimate=cost(2 * SEG * n * KQ * 512, n * (3 << 20)),
-    )(yc, *xs, w0, w1, before)
+        cost_estimate=cost(2 * SEG * KQ * 512, 3 << 20),
+    )(yc, x, w0, w1, before)
 
 
 def whole(*shape):
@@ -325,11 +360,12 @@
     w1 = partner_weight.reshape(32, NY, 64, COLS)
     first, quarters = near_base(yc, [tokens, near], weight, partner_weight)
     second, more = near_base(yc, [other], weight, partner_weight, (first,))
-    far = far_base(yc, [q0, q1, q2], 0, w0, w1, second, False)
-
-    parts = low_parts(yc, [*quarters, *more, q0], recv, far)
-    far = far_base(yc, [q3], 3, w0, w1, far, True)
-    parts = [parts[0]] + [shift(parts[e], "y", e) for e in (1, 2, 3)]
+    far, stack = far_base(yc, q0, q1, w0, w1, [*quarters, *more])
+    far = more_base(yc, q2, 2, w0, w1, far)
+
+    parts = low_parts(yc, stack, recv, far)
+    far = more_base(yc, q3, 3, w0, w1, far)
+    parts = [parts[0]] + [shift(parts[e], "y", e) for e in (2, 1, 3)]
     up_sorted = up_rows(recv)
     out, out_partner = sum_up(yc, first, second, far, parts, up_sorted)
     theirs = shift(out_partner, "c", 1)

time: 93.4 us -> 92.6 us (level)
  waiting for transfers between devices: 33 us -> 31.2 us
  local copies, waits for them, and re-layouts: 2.32 us -> 3.72 us
  Pallas kernels: 30.2 us -> 29.2 us
    ppermute x6, waiting for transfers between devices: 28.1 us -> 25.1 us  [around(): return lax.ppermute(x, ('y', 'c'), pairs)]
    all_to_all x1, waiting for transfers between devices: 2.47 us -> 4.6 us  [on_device(): recv = lax.all_to_all(send, ('z', 'x', 'c'), 0, 0)]
    pallas_call x1, Pallas kernels: 3.37 us -> 1.8 us  [low_parts(): pl.pallas_call(low_kernel, grid_spec=pltpu.PrefetchScalarGridSpec(num_sca...]
    unnamed x14 -> x10, local copies, waits for them, and re-layouts: 1.61 us -> 3 us
    pallas_call x2 -> x3, Pallas kernels: 6.53 us -> 7.65 us  [the longest x2 4.68 us: more_base(): pl.pallas_call(more_kernel, grid_spec=pltpu.PrefetchScalarGridSpec(num_sc...]
  transfers between devices with their start and end apart: 13 -> 13, of which waited for: 8 -> 7; matrix products, arithmetic and copies ran while one was open for 0% -> 0% of each run, Pallas kernels for 31% -> 30%
where the time goes in v3:
time: 92.6 us; the launch traced here: 92.2 us
  waiting for transfers between devices  31.2 us (34%)
  Pallas kernels  29.2 us (32%)
  starting transfers between devices  27.9 us (30%)
  local copies, waits for them, and re-layouts  3.72 us (4%)
    ppermute x6, waiting for transfers between devices, around(): return lax.ppermute(x, ('y', 'c'), pairs)  25.1 us
    all_to_all x1, starting transfers between devices, on_device(): recv = lax.all_to_all(send, ('z', 'x', 'c'), 0, 0)  12 us
    pallas_call x2, Pallas kernels, near_base(): pl.pallas_call(functools.partial(near_kernel, n), grid_spec=pltpu.Prefetc...  10.5 us
    ppermute x6, starting transfers between devices, shift(): return lax.ppermute(x, axis, [(i, (i + by) % n) for i in range(n)])  10.5 us
    ppermute x6, starting transfers between devices, around(): return lax.ppermute(x, ('y', 'c'), pairs)  5.43 us
    pallas_call x2, Pallas kernels, more_base(): pl.pallas_call(more_kernel, grid_spec=pltpu.PrefetchScalarGridSpec(num_sc...  4.68 us
    all_to_all x1, waiting for transfers between devices, on_device(): recv = lax.all_to_all(send, ('z', 'x', 'c'), 0, 0)  4.6 us
    pallas_call x1, Pallas kernels, split_quarters(): pl.pallas_call(split_kernel, grid_spec=pltpu.PrefetchScalarGridSpec(num_s...  3.8 us
  transfers between devices with their start and end apart: 13, of which 7 were waited for; matrix products, arithmetic and copies ran while one was open for 0% of the time, Pallas kernels for 30%

profile of v3, /device:TPU:1, one launch (start us, length us, event | category | flops | bytes accessed | tf_op | source)
XLA Modules:
  0.0 92.2 jit_solution(6253190440408804617)
XLA Ops:
  0.0 3.2 %collective-permute-start.2 = (bf16[128,8192]{1,0:T(8,128)(2,1)}, bf16[128,8192]{1,0:T(8,128)(2,1)}, u32[]{:S(2)}, u32[]{:S(2)}) collective-permute-start(bf16[128,8192]{1,0:T(8,128)(2,1)} %refs_0_.1), channel_id=1, source_target_pairs={{0,1},{1,0},{2,3},{3,2},{4,5},{5,4},{6,7},{7,6},{8,9},{9,8},{10,11... | collective-permute-start | bytes 6291464 | tf_op jit(solution)/shard_map/ppermute | solution.py:39
  3.2 1.0 %collective-permute-start = (bf16[128,8192]{1,0:T(8,128)(2,1)}, bf16[128,8192]{1,0:T(8,128)(2,1)}, u32[]{:S(2)}, u32[]{:S(2)}) collective-permute-start(bf16[128,8192]{1,0:T(8,128)(2,1)} %refs_0_.1), channel_id=1, source_target_pairs={{0,2},{1,7},{2,4},{3,1},{4,6},{5,3},{6,0},{7,5},{8,10},{9,15},{10,... | collective-permute-start | bytes 6291464 | tf_op jit(solution)/shard_map/ppermute | solution.py:48
  4.2 0.0 collective-permute-start.1
  4.2 3.4 %shard_map.70 = bf16[64,144,128]{2,1,0:T(8,128)(2,1)} custom-call(s32[128]{0:T(128)} %apr.1, s32[256]{0:T(256)} %rps.1, bf16[64,32,128]{2,1,0:T(8,128)(2,1)} %down_ref.1, bf16[64,2,256]{2,1,0:T(2,128)(2,1)} %up_ref.1), custom_call_target="tpu_custom_call" | custom-call | bytes 3145728 | tf_op jit(solution)/shard_map/pallas_call | solution.py:84
  7.7 12.0 %all-to-all-start = ((bf16[64,144,128]{2,1,0:T(8,128)(2,1)}), bf16[64,144,128]{2,1,0:T(8,128)(2,1)S(1)}, u32[]{:S(2)}, u32[]{:S(2)}) async-start(bf16[64,144,128]{2,1,0:T(8,128)(2,1)} %shard_map.70), calls=%async_computation | async-start | bytes 4718592 | tf_op jit(solution)/shard_map/all_to_all | solution.py:356
  19.7 0.0 collective-permute-done.2
  19.7 0.9 collective-permute-start.3
  20.6 8.1 %collective-permute-done.refs_1_.x_ref = bf16[128,8192]{1,0:T(8,128)(2,1)} collective-permute-done((bf16[128,8192]{1,0:T(8,128)(2,1)}, bf16[128,8192]{1,0:T(8,128)(2,1)}, u32[]{:S(2)}, u32[]{:S(2)}) %collective-permute-start) | collective-permute-done | bytes 2097184 | tf_op jit(solution)/shard_map/ppermute | solution.py:48
  28.7 0.0 copy-start
  28.7 0.0 copy-start.2
  28.7 3.8 %shard_map.66 = (bf16[128,2048]{1,0:T(8,128)(2,1)S(1)}, bf16[128,2048]{1,0:T(8,128)(2,1)S(1)}, bf16[128,2048]{1,0:T(8,128)(2,1)S(1)}, bf16[128,2048]{1,0:T(8,128)(2,1)}) custom-call(s32[1]{0:T(128)} %bitcast.2.first, bf16[128,8192]{1,0:T(8,128)(2,1)} %collective-permute-done.refs_1_.x_ref), custom_call_target="tpu_custom_call" | custom-call | flops 99999997952 | bytes 4194304 | tf_op jit(solution)/shard_map/pallas_call | solution.py:123
  32.5 2.1 %collective-permute-start.6 = (bf16[128,2048]{1,0:T(8,128)(2,1)S(1)}, bf16[128,2048]{1,0:T(8,128)(2,1)S(1)}, u32[]{:S(2)}, u32[]{:S(2)}) collective-permute-start(bf16[128,2048]{1,0:T(8,128)(2,1)S(1)} %get-tuple-element.26), channel_id=1, source_target_pairs={{0,2},{1,7},{2,4},{3,1},{4,6},{5,3},{6,0},{7,5},{8,10},{9,15},{10,... | collective-permute-start | bytes 1572872 | tf_op jit(solution)/shard_map/ppermute | solution.py:48
  34.6 0.0 collective-permute-start.7
  34.7 0.0 collective-permute-start.5
  34.7 0.0 collective-permute-done.1.refs_3_.refs_2_
  34.7 1.4 %collective-permute-start.4 = (bf16[128,2048]{1,0:T(8,128)(2,1)}, bf16[128,2048]{1,0:T(8,128)(2,1)}, u32[]{:S(2)}, u32[]{:S(2)}) collective-permute-start(bf16[128,2048]{1,0:T(8,128)(2,1)} %get-tuple-element.24), channel_id=1, source_target_pairs={{0,2},{1,7},{2,4},{3,1},{4,6},{5,3},{6,0},{7,5},{8,10},{9,15},{10,... | collective-permute-start | bytes 1572872 | tf_op jit(solution)/shard_map/ppermute | solution.py:48
  36.1 0.1 pad_add_fusion.yc
  36.2 0.0 copy-done
  36.2 0.0 copy-done.2
  36.2 5.9 %shard_map.64 = (f32[256,512]{1,0:T(8,128)S(1)}, bf16[128,2048]{1,0:T(8,128)(2,1)S(1)}, bf16[128,2048]{1,0:T(8,128)(2,1)S(1)}) custom-call(s32[2]{0:T(128)S(1)} %pad_add_fusion.yc, bf16[128,8192]{1,0:T(8,128)(2,1)S(1)} %copy-done.2, bf16[128,8192]{1,0:T(8,128)(2,1)} %collective-permute-done.refs_1_.x_ref, bf16[8192,256]{1,0:T(8,128)(2,1)S(1)} %copy-done, ...), custom_call_target="tpu_custom_call" | custom-call | flops 2147483648 | bytes 12582912 | tf_op jit(solution)/shard_map/pallas_call | solution.py:221
  42.0 10.7 %collective-permute-done.3.refs_0_ = bf16[128,8192]{1,0:T(8,128)(2,1)S(1)} collective-permute-done((bf16[128,8192]{1,0:T(8,128)(2,1)}, bf16[128,8192]{1,0:T(8,128)(2,1)S(1)}, u32[]{:S(2)}, u32[]{:S(2)}) %collective-permute-start.3) | collective-permute-done | bytes 2097184 | tf_op jit(solution)/shard_map/ppermute | solution.py:48
  52.8 4.6 %shard_map.65 = (f32[128,512]{1,0:T(8,128)S(1)}, bf16[128,2048]{1,0:T(8,128)(2,1)S(1)}) custom-call(s32[2]{0:T(128)S(1)} %pad_add_fusion.yc, bf16[128,8192]{1,0:T(8,128)(2,1)S(1)} %collective-permute-done.3.refs_0_, bf16[8192,256]{1,0:T(8,128)(2,1)S(1)} %copy-done, bf16[8192,256]{1,0:T(8,128)(2,1)} %collective-permute-done.1.refs_3_.refs_2_, ...), custom_call_target="tpu_custom_call" | custom-call | flops 1073741824 | bytes 12582912 | tf_op jit(solution)/shard_map/pallas_call | solution.py:221
  57.4 0.0 collective-permute-done.6.q0
  57.4 4.9 %collective-permute-done.7.q1 = bf16[128,2048]{1,0:T(8,128)(2,1)S(1)} collective-permute-done((bf16[128,2048]{1,0:T(8,128)(2,1)S(1)}, bf16[128,2048]{1,0:T(8,128)(2,1)S(1)}, u32[]{:S(2)}, u32[]{:S(2)}) %collective-permute-start.7) | collective-permute-done | bytes 524320 | tf_op jit(solution)/shard_map/ppermute | solution.py:48
  62.3 3.0 %shard_map.67 = (f32[128,512]{1,0:T(8,128)S(1)}, bf16[4,128,2048]{2,1,0:T(8,128)(2,1)S(1)}) custom-call(s32[2]{0:T(128)S(1)} %pad_add_fusion.yc, bf16[128,2048]{1,0:T(8,128)(2,1)S(1)} %collective-permute-done.6.q0, bf16[128,2048]{1,0:T(8,128)(2,1)S(1)} %collective-permute-done.7.q1, bf16[32,4,64,256]{3,2,1,0:T(8,128)(2,1)S(1)} %bitcast.10, ...), custom_call_target="tpu_custom_call" | custom-call | flops 536870912 | bytes 10485760 | tf_op jit(solution)/shard_map/pallas_call | solution.py:260
  65.3 0.0 copy-start.3
  65.3 1.4 %copy-done.3 = bf16[4,128,2048]{2,1,0:T(8,128)(2,1)} copy-done((bf16[4,128,2048]{2,1,0:T(8,128)(2,1)}, bf16[4,128,2048]{2,1,0:T(8,128)(2,1)S(1)}, u32[]{:S(2)}) %copy-start.3) | copy-done | bytes 2097176
  66.7 1.2 %collective-permute-done.5.x = bf16[128,2048]{1,0:T(8,128)(2,1)S(1)} collective-permute-done((bf16[128,2048]{1,0:T(8,128)(2,1)S(1)}, bf16[128,2048]{1,0:T(8,128)(2,1)S(1)}, u32[]{:S(2)}, u32[]{:S(2)}) %collective-permute-start.5) | collective-permute-done | bytes 524320 | tf_op jit(solution)/shard_map/ppermute | solution.py:48
  68.0 2.3 %shard_map.68.before.after = f32[128,512]{1,0:T(8,128)S(1)} custom-call(s32[2]{0:T(128)S(1)} %pad_add_fusion.yc, bf16[128,2048]{1,0:T(8,128)(2,1)S(1)} %collective-permute-done.5.x, bf16[32,4,64,256]{3,2,1,0:T(8,128)(2,1)S(1)} %bitcast.11, bf16[32,4,64,256]{3,2,1,0:T(8,128)(2,1)} %bitcast.4.w1, f32[128,512]{1,0:T(8,128)S(1)} %get-tuple-element.31.before), custom_call_target="tpu_custom_call" | custom-call | flops 268435456 | bytes 3145728 | tf_op jit(solution)/shard_map/pallas_call | solution.py:289
  70.2 4.6 %all-to-all-done.down_ref.recv_ref = bf16[64,144,128]{2,1,0:T(8,128)(2,1)S(1)} async-done(((bf16[64,144,128]{2,1,0:T(8,128)(2,1)}), bf16[64,144,128]{2,1,0:T(8,128)(2,1)S(1)}, u32[]{:S(2)}, u32[]{:S(2)}) %all-to-all-start) | async-done | bytes 2359328 | tf_op jit(solution)/shard_map/all_to_all | solution.py:356
  74.9 0.0 copy-start.4
  74.9 1.6 %copy-done.4 = bf16[4,128,2048]{2,1,0:T(8,128)(2,1)S(1)} copy-done((bf16[4,128,2048]{2,1,0:T(8,128)(2,1)S(1)}, bf16[4,128,2048]{2,1,0:T(8,128)(2,1)}, u32[]{:S(2)}) %copy-start.4) | copy-done | bytes 2097176
  76.4 0.0 copy-start.1
  76.4 1.8 %shard_map.71 = (f32[256,128]{1,0:T(8,128)S(1)}, f32[256,128]{1,0:T(8,128)S(1)}, f32[256,128]{1,0:T(8,128)S(1)}, f32[256,128]{1,0:T(8,128)S(1)}) custom-call(s32[2]{0:T(128)S(1)} %pad_add_fusion.yc, bf16[4,128,2048]{2,1,0:T(8,128)(2,1)S(1)} %copy-done.4, bf16[64,144,128]{2,1,0:T(8,128)(2,1)S(1)} %all-to-all-done.down_ref.recv_ref, ...), custom_call_target="tpu_custom_call" | custom-call | flops 268435456 | bytes 5242880 | tf_op jit(solution)/shard_map/pallas_call | solution.py:155
  78.3 1.3 %collective-permute-start.8 = (f32[256,128]{1,0:T(8,128)S(1)}, f32[256,128]{1,0:T(8,128)S(1)}, u32[]{:S(2)}, u32[]{:S(2)}) collective-permute-start(f32[256,128]{1,0:T(8,128)S(1)} %get-tuple-element.34), channel_id=1, source_target_pairs={{0,4},{2,6},{4,0},{6,2},{1,5},{3,7},{5,1},{7,3},{8,12},{10,14},{12... | collective-permute-start | bytes 393224 | tf_op jit(solution)/shard_map/ppermute | solution.py:39
  79.6 0.0 collective-permute-start.9
  79.6 2.7 %collective-permute-start.10 = (f32[256,128]{1,0:T(8,128)S(1)}, f32[256,128]{1,0:T(8,128)S(1)}, u32[]{:S(2)}, u32[]{:S(2)}) collective-permute-start(f32[256,128]{1,0:T(8,128)S(1)} %get-tuple-element.36), channel_id=1, source_target_pairs={{0,6},{2,0},{4,2},{6,4},{1,7},{3,1},{5,3},{7,5},{8,14},{10,8},{12,... | collective-permute-start | bytes 393224 | tf_op jit(solution)/shard_map/ppermute | solution.py:39
  82.3 0.0 collective-permute-done.4.x
  82.3 0.0 copy-done.1
  82.3 2.4 %shard_map.69.far = f32[128,512]{1,0:T(8,128)S(1)} custom-call(s32[2]{0:T(128)S(1)} %pad_add_fusion.yc, bf16[128,2048]{1,0:T(8,128)(2,1)} %collective-permute-done.4.x, bf16[32,4,64,256]{3,2,1,0:T(8,128)(2,1)S(1)} %bitcast.12, bf16[32,4,64,256]{3,2,1,0:T(8,128)(2,1)} %bitcast.4.w1, f32[128,512]{1,0:T(8,128)S(1)} %shard_map.68.before.after), custom_call_target="tpu_custom_call" | custom-call | flops 268435456 | bytes 3145728 | tf_op jit(solution)/shard_map/pallas_call | solution.py:289
  84.7 0.5 shard_map.72.up
  85.2 0.0 collective-permute-done.8.p1
  85.2 0.4 collective-permute-done.9.p2
  85.6 0.0 collective-permute-done.10.p3
  85.6 1.5 %shard_map.73 = (bf16[4,2,128,256]{3,2,1,0:T(8,128)(2,1)}, bf16[4,128,256]{2,1,0:T(8,128)(2,1)S(1)}) custom-call(s32[2]{0:T(128)S(1)} %pad_add_fusion.yc, f32[256,512]{1,0:T(8,128)S(1)} %get-tuple-element.22.refs_3_.first, f32[128,512]{1,0:T(8,128)S(1)} %get-tuple-element.23.second, f32[128,512]{1,0:T(8,128)S(1)} %shard_map.69.far, ...), custom_call_target="tpu_custom_call" | custom-call | flops 67108864 | bytes 3145728 | tf_op jit(solution)/shard_map/pallas_call | solution.py:323
  87.1 3.2 %collective-permute-start.11 = (bf16[4,128,256]{2,1,0:T(8,128)(2,1)S(1)}, bf16[4,128,256]{2,1,0:T(8,128)(2,1)S(1)}, u32[]{:S(2)}, u32[]{:S(2)}) collective-permute-start(bf16[4,128,256]{2,1,0:T(8,128)(2,1)S(1)} %get-tuple-element.38), channel_id=1, source_target_pairs={{0,1},{1,0},{2,3},{3,2},{4,5},{5,4},{6,7},{7,6},{8,9},{9,8},{10,11... | collective-permute-start | bytes 786440 | tf_op jit(solution)/shard_map/ppermute | solution.py:39
  90.3 1.2 %collective-permute-done.11 = bf16[4,128,256]{2,1,0:T(8,128)(2,1)S(1)} collective-permute-done((bf16[4,128,256]{2,1,0:T(8,128)(2,1)S(1)}, bf16[4,128,256]{2,1,0:T(8,128)(2,1)S(1)}, u32[]{:S(2)}, u32[]{:S(2)}) %collective-permute-start.11) | collective-permute-done | bytes 262176 | tf_op jit(solution)/shard_map/ppermute | solution.py:39
  91.5 0.7 bitcast_dynamic-update-slice_fusion
Async XLA Ops:
  0.0 19.7 %collective-permute-start.2 = (bf16[128,8192]{1,0:T(8,128)(2,1)}, bf16[128,8192]{1,0:T(8,128)(2,1)}, u32[]{:S(2)}, u32[]{:S(2)}) collective-permute-start(bf16[128,8192]{1,0:T(8,128)(2,1)} %refs_0_.1), channel_id=1, source_target_pairs={{0,1},{1,0},{2,3},{3,2},{4,5},{5,4},{6,7},{7,6},{8,9},{9,8},{10,11... | collective-permute-start | bytes 6291464 | tf_op jit(solution)/shard_map/ppermute | solution.py:39
  3.2 25.5 %collective-permute-start = (bf16[128,8192]{1,0:T(8,128)(2,1)}, bf16[128,8192]{1,0:T(8,128)(2,1)}, u32[]{:S(2)}, u32[]{:S(2)}) collective-permute-start(bf16[128,8192]{1,0:T(8,128)(2,1)} %refs_0_.1), channel_id=1, source_target_pairs={{0,2},{1,7},{2,4},{3,1},{4,6},{5,3},{6,0},{7,5},{8,10},{9,15},{10,... | collective-permute-start | bytes 6291464 | tf_op jit(solution)/shard_map/ppermute | solution.py:48
  4.2 30.5 %collective-permute-start.1 = (bf16[8192,256]{1,0:T(8,128)(2,1)}, bf16[8192,256]{1,0:T(8,128)(2,1)}, u32[]{:S(2)}, u32[]{:S(2)}) collective-permute-start(bf16[8192,256]{1,0:T(8,128)(2,1)} %refs_1_.1), channel_id=1, source_target_pairs={{0,1},{1,0},{2,3},{3,2},{4,5},{5,4},{6,7},{7,6},{8,9},{9,8},{10,11... | collective-permute-start | bytes 12582920 | tf_op jit(solution)/shard_map/ppermute | solution.py:39
  7.7 67.2 %all-to-all-start = ((bf16[64,144,128]{2,1,0:T(8,128)(2,1)}), bf16[64,144,128]{2,1,0:T(8,128)(2,1)S(1)}, u32[]{:S(2)}, u32[]{:S(2)}) async-start(bf16[64,144,128]{2,1,0:T(8,128)(2,1)} %shard_map.70), calls=%async_computation | async-start | bytes 4718592 | tf_op jit(solution)/shard_map/all_to_all | solution.py:356
  19.7 33.1 %collective-permute-start.3 = (bf16[128,8192]{1,0:T(8,128)(2,1)}, bf16[128,8192]{1,0:T(8,128)(2,1)S(1)}, u32[]{:S(2)}, u32[]{:S(2)}) collective-permute-start(bf16[128,8192]{1,0:T(8,128)(2,1)} %collective-permute-done.2), channel_id=1, source_target_pairs={{0,3},{1,6},{2,5},{3,0},{4,7},{5,2},{6,1},{7,4},{8,11},{9,14},{10,... | collective-permute-start | bytes 6291464 | tf_op jit(solution)/shard_map/ppermute | solution.py:48
  28.7 7.4 %copy-start = (bf16[8192,256]{1,0:T(8,128)(2,1)S(1)}, bf16[8192,256]{1,0:T(8,128)(2,1)}, u32[]{:S(2)}) copy-start(bf16[8192,256]{1,0:T(8,128)(2,1)} %refs_1_.1) | copy-start | bytes 12582916
  28.7 7.4 %copy-start.2 = (bf16[128,8192]{1,0:T(8,128)(2,1)S(1)}, bf16[128,8192]{1,0:T(8,128)(2,1)}, u32[]{:S(2)}) copy-start(bf16[128,8192]{1,0:T(8,128)(2,1)} %refs_0_.1) | copy-start | bytes 6291460
  32.5 24.9 %collective-permute-start.6 = (bf16[128,2048]{1,0:T(8,128)(2,1)S(1)}, bf16[128,2048]{1,0:T(8,128)(2,1)S(1)}, u32[]{:S(2)}, u32[]{:S(2)}) collective-permute-start(bf16[128,2048]{1,0:T(8,128)(2,1)S(1)} %get-tuple-element.26), channel_id=1, source_target_pairs={{0,2},{1,7},{2,4},{3,1},{4,6},{5,3},{6,0},{7,5},{8,10},{9,15},{10,... | collective-permute-start | bytes 1572872 | tf_op jit(solution)/shard_map/ppermute | solution.py:48
  34.6 27.7 %collective-permute-start.7 = (bf16[128,2048]{1,0:T(8,128)(2,1)S(1)}, bf16[128,2048]{1,0:T(8,128)(2,1)S(1)}, u32[]{:S(2)}, u32[]{:S(2)}) collective-permute-start(bf16[128,2048]{1,0:T(8,128)(2,1)S(1)} %get-tuple-element.27), channel_id=1, source_target_pairs={{0,2},{1,7},{2,4},{3,1},{4,6},{5,3},{6,0},{7,5},{8,10},{9,15},{10,... | collective-permute-start | bytes 1572872 | tf_op jit(solution)/shard_map/ppermute | solution.py:48
  34.7 33.3 %collective-permute-start.5 = (bf16[128,2048]{1,0:T(8,128)(2,1)S(1)}, bf16[128,2048]{1,0:T(8,128)(2,1)S(1)}, u32[]{:S(2)}, u32[]{:S(2)}) collective-permute-start(bf16[128,2048]{1,0:T(8,128)(2,1)S(1)} %get-tuple-element.25), channel_id=1, source_target_pairs={{0,2},{1,7},{2,4},{3,1},{4,6},{5,3},{6,0},{7,5},{8,10},{9,15},{10,... | collective-permute-start | bytes 1572872 | tf_op jit(solution)/shard_map/ppermute | solution.py:48
  34.7 47.6 %collective-permute-start.4 = (bf16[128,2048]{1,0:T(8,128)(2,1)}, bf16[128,2048]{1,0:T(8,128)(2,1)}, u32[]{:S(2)}, u32[]{:S(2)}) collective-permute-start(bf16[128,2048]{1,0:T(8,128)(2,1)} %get-tuple-element.24), channel_id=1, source_target_pairs={{0,2},{1,7},{2,4},{3,1},{4,6},{5,3},{6,0},{7,5},{8,10},{9,15},{10,... | collective-permute-start | bytes 1572872 | tf_op jit(solution)/shard_map/ppermute | solution.py:48
  65.3 1.4 %copy-start.3 = (bf16[4,128,2048]{2,1,0:T(8,128)(2,1)}, bf16[4,128,2048]{2,1,0:T(8,128)(2,1)S(1)}, u32[]{:S(2)}) copy-start(bf16[4,128,2048]{2,1,0:T(8,128)(2,1)S(1)} %get-tuple-element.32.x_ref) | copy-start | bytes 6291460
  74.9 1.6 %copy-start.4 = (bf16[4,128,2048]{2,1,0:T(8,128)(2,1)S(1)}, bf16[4,128,2048]{2,1,0:T(8,128)(2,1)}, u32[]{:S(2)}) copy-start(bf16[4,128,2048]{2,1,0:T(8,128)(2,1)} %copy-done.3) | copy-start | bytes 6291460
  76.4 5.8 %copy-start.1 = (bf16[8192,256]{1,0:T(8,128)(2,1)S(1)}, bf16[8192,256]{1,0:T(8,128)(2,1)}, u32[]{:S(2)}) copy-start(bf16[8192,256]{1,0:T(8,128)(2,1)} %refs_1_.1) | copy-start | bytes 12582916
  78.3 6.9 %collective-permute-start.8 = (f32[256,128]{1,0:T(8,128)S(1)}, f32[256,128]{1,0:T(8,128)S(1)}, u32[]{:S(2)}, u32[]{:S(2)}) collective-permute-start(f32[256,128]{1,0:T(8,128)S(1)} %get-tuple-element.34), channel_id=1, source_target_pairs={{0,4},{2,6},{4,0},{6,2},{1,5},{3,7},{5,1},{7,3},{8,12},{10,14},{12... | collective-permute-start | bytes 393224 | tf_op jit(solution)/shard_map/ppermute | solution.py:39
  79.6 6.0 %collective-permute-start.9 = (f32[256,128]{1,0:T(8,128)S(1)}, f32[256,128]{1,0:T(8,128)S(1)}, u32[]{:S(2)}, u32[]{:S(2)}) collective-permute-start(f32[256,128]{1,0:T(8,128)S(1)} %get-tuple-element.35), channel_id=1, source_target_pairs={{0,2},{2,4},{4,6},{6,0},{1,3},{3,5},{5,7},{7,1},{8,10},{10,12},{12... | collective-permute-start | bytes 393224 | tf_op jit(solution)/shard_map/ppermute | solution.py:39
  79.6 6.0 %collective-permute-start.10 = (f32[256,128]{1,0:T(8,128)S(1)}, f32[256,128]{1,0:T(8,128)S(1)}, u32[]{:S(2)}, u32[]{:S(2)}) collective-permute-start(f32[256,128]{1,0:T(8,128)S(1)} %get-tuple-element.36), channel_id=1, source_target_pairs={{0,6},{2,0},{4,2},{6,4},{1,7},{3,1},{5,3},{7,5},{8,14},{10,8},{12,... | collective-permute-start | bytes 393224 | tf_op jit(solution)/shard_map/ppermute | solution.py:39
  87.1 4.4 %collective-permute-start.11 = (bf16[4,128,256]{2,1,0:T(8,128)(2,1)S(1)}, bf16[4,128,256]{2,1,0:T(8,128)(2,1)S(1)}, u32[]{:S(2)}, u32[]{:S(2)}) collective-permute-start(bf16[4,128,256]{2,1,0:T(8,128)(2,1)S(1)} %get-tuple-element.38), channel_id=1, source_target_pairs={{0,1},{1,0},{2,3},{3,2},{4,5},{5,4},{6,7},{7,6},{8,9},{9,8},{10,11... | collective-permute-start | bytes 786440 | tf_op jit(solution)/shard_map/ppermute | solution.py:39

commit v4 on v3

--- a/solution.py
+++ b/solution.py
@@ -83,20 +83,18 @@
 def pack(apr, rps, down, up):
     return pl.pallas_call(
         pack_kernel,
-        grid_spec=pltpu.PrefetchScalarGridSpec(
-            num_scalar_prefetch=2,
-            grid=(1,),
-            in_specs=[
-                pl.BlockSpec((64, 32, 128), lambda i, *_: (0, 0, 0)),
-                pl.BlockSpec((64, 2, COLS), lambda i, *_: (0, 0, 0)),
-            ],
-            out_specs=pl.BlockSpec(memory_space=pl.ANY),
-            scratch_shapes=[
-                pltpu.VMEM((64, 8, 128), F32),
-                pltpu.VMEM((NDP * NC, 144, 128), BF16),
-                pltpu.SemaphoreType.DMA((NDP * NC // PACK,)),
-            ],
-        ),
+        in_specs=[
+            pl.BlockSpec(memory_space=pltpu.SMEM),
+            pl.BlockSpec(memory_space=pltpu.SMEM),
+            pl.BlockSpec(memory_space=pltpu.VMEM),
+            pl.BlockSpec(memory_space=pltpu.VMEM),
+        ],
+        out_specs=pl.BlockSpec(memory_space=pl.ANY),
+        scratch_shapes=[
+            pltpu.VMEM((64, 8, 128), F32),
+            pltpu.VMEM((NDP * NC, 144, 128), BF16),
+            pltpu.SemaphoreType.DMA((NDP * NC // PACK,)),
+        ],
         out_shape=jax.ShapeDtypeStruct((NDP * NC, 144, 128), BF16),
         compiler_params=pltpu.CompilerParams(vmem_limit_bytes=60 * 1024 * 1024),
         cost_estimate=cost(0, 3 << 20),
@@ -134,16 +132,16 @@
     )(first, x)
 
 
-def low_kernel(yc, x_ref, down_ref, after, *rest):
+def low_kernel(yc, x_ref, recv_ref, after, *rest):
     outs, sums = rest[:NY], rest[NY]
     me, core = yc[0], yc[1]
     for i, d in enumerate((0, 3 - 2 * core, 1 + 2 * core, 2)):
         s = (me + d) & 3
-        factor = down_ref[:, pl.ds(pl.multiple_of(32 * s, 32), 32), :].reshape(KQ, 128)
+        factor = recv_ref[:, pl.ds(pl.multiple_of(32 * s, 32), 32), :].reshape(KQ, 128)
         sums[s] = jnp.dot(x_ref[i], factor, preferred_element_type=F32)
     lane = lax.broadcasted_iota(jnp.int32, (128, 128), 1)
     for e in range(NY):
-        value = ((me + e) & 3) >= 2
+        value = (me + e) % NY >= NY // 2
         for pair in range(2):
             a, b = sums[2 * pair], sums[2 * pair + 1]
             keys = jnp.where(lane < 64, a, pltpu.roll(b, 64, 1))
@@ -151,20 +149,17 @@
             outs[e][128 * pair : 128 * pair + 128, :] = jnp.where(value, values, keys)
 
 
+SMEM = pl.BlockSpec(memory_space=pltpu.SMEM)
+VMEM = pl.BlockSpec(memory_space=pltpu.VMEM)
+ANY = pl.BlockSpec(memory_space=pl.ANY)
+
+
 def low_parts(yc, x, recv, after):
     return pl.pallas_call(
         low_kernel,
-        grid_spec=pltpu.PrefetchScalarGridSpec(
-            num_scalar_prefetch=1,
-            grid=(1,),
-            in_specs=[
-                pl.BlockSpec((4, SEG, KQ), lambda i, *_: (0, 0, 0)),
-                pl.BlockSpec((64, 128, 128), lambda i, *_: (0, 0, 0)),
-                pl.BlockSpec(memory_space=pl.ANY),
-            ],
-            out_specs=[pl.BlockSpec((256, 128), lambda i, *_: (0, 0))] * NY,
-            scratch_shapes=[pltpu.VMEM((NY, 128, 128), F32)],
-        ),
+        in_specs=[SMEM, VMEM, VMEM, ANY],
+        out_specs=[VMEM] * NY,
+        scratch_shapes=[pltpu.VMEM((NY, 128, 128), F32)],
         out_shape=[jax.ShapeDtypeStruct((256, 128), F32)] * NY,
         compiler_params=params(),
         cost_estimate=cost(2 * 512 * KQ * 128, 5 << 20),
@@ -177,7 +172,7 @@
     pair, half, seg, rank = r // 256, (r // 128) % 2, (r // 64) % 2, r % 64
     source = (rank // 2) * 16 + (pair * 2 + seg) * 4 + half * 2 + rank % 2
     order = (k == source).astype(F32).astype(BF16)
-    every = recv_ref[...].reshape(NDP, NC, 16, 128)
+    every = recv_ref[:, 128:, :].reshape(NDP, NC, 16, 128)
     for c in range(NC):
         rows = every[:, c].reshape(512, 128)
         got = jnp.dot(order, rows, preferred_element_type=F32).astype(BF16)
@@ -190,9 +185,8 @@
 def up_rows(recv):
     return pl.pallas_call(
         up_kernel,
-        grid=(1,),
-        in_specs=[pl.BlockSpec((64, 16, 128), lambda i: (0, 8, 0))],
-        out_specs=pl.BlockSpec((NC, 2, 128, COLS), lambda i: (0, 0, 0, 0)),
+        in_specs=[VMEM],
+        out_specs=VMEM,
         out_shape=jax.ShapeDtypeStruct((NC, 2, 128, COLS), BF16),
         compiler_params=params(),
         cost_estimate=cost(2 * 512 * 512 * 256, 1 << 19),
@@ -304,7 +298,9 @@
     return pl.BlockSpec(shape, lambda i, yc: (0,) * len(shape))
 
 
-def sum_kernel(yc, first, second, far, p0, p1, p2, p3, up, out, out_partner):
+def sum_kernel(
+    yc, first, second, far, p0, p1, p2, p3, up, out, out_partner, held, sem
+):
     me, core = yc[0], yc[1]
     low = (p0[...] + p1[...] + p2[...] + p3[...]).astype(BF16).astype(F32)
     left = lax.broadcasted_iota(jnp.int32, (128, 128), 1) < 64
@@ -315,28 +311,26 @@
         mine = jnp.where(left == (s & 1 == 0), both, 0.0).astype(BF16)
         own = jnp.dot(mine, up[core, s // 2], preferred_element_type=F32)
         other = jnp.dot(mine, up[1 - core, s // 2], preferred_element_type=F32)
-        out[s] = (base[:, :COLS] + own).astype(BF16)
+        held[s] = (base[:, :COLS] + own).astype(BF16)
         out_partner[s] = (base[:, COLS:] + other).astype(BF16)
+    copy = pltpu.make_async_copy(held, out.at[:, core], sem)
+    copy.start()
+    copy.wait()
 
 
 def sum_up(yc, first, second, far, parts, up):
     return pl.pallas_call(
         sum_kernel,
-        grid_spec=pltpu.PrefetchScalarGridSpec(
-            num_scalar_prefetch=1,
-            grid=(1,),
-            in_specs=[whole(2 * SEG, 512), whole(SEG, 512), whole(SEG, 512)]
-            + [whole(256, 128)] * NY
-            + [whole(NC, 2, 128, COLS)],
-            out_specs=[
-                pl.BlockSpec((NY, None, SEG, COLS), lambda i, yc: (0, yc[1], 0, 0)),
-                whole(NY, SEG, COLS),
-            ],
-        ),
+        in_specs=[SMEM] + [VMEM] * 8,
+        out_specs=[ANY, VMEM],
         out_shape=[
             jax.ShapeDtypeStruct((NY, NC, SEG, COLS), BF16),
             jax.ShapeDtypeStruct((NY, SEG, COLS), BF16),
         ],
+        scratch_shapes=[
+            pltpu.VMEM((NY, SEG, COLS), BF16),
+            pltpu.SemaphoreType.DMA(()),
+        ],
         compiler_params=params(),
         cost_estimate=cost(2 * 512 * 128 * 512, 3 << 20),
     )(yc, first, second, far, *parts, up)
@@ -346,14 +340,16 @@
     y, c = lax.axis_index("y"), lax.axis_index("c")
     yc = jnp.stack([y, c]).astype(jnp.int32)
 
+    send = pack(apr, rps, down, up)
+    tokens, send = lax.optimization_barrier((tokens, send))
     near = around(tokens)
     partner_tokens = shift(tokens, "c", 1)
     other = around(partner_tokens, False)
     ahead = ((y + 1 - 2 * c + NY) & 3).reshape(1).astype(jnp.int32)
     q0, q1, q2, q3 = [around(v) for v in split_quarters(ahead, near)]
 
-    send = pack(apr, rps, down, up)
     recv = lax.all_to_all(send, ("z", "x", "c"), 0, 0)
+    weight, _ = lax.optimization_barrier((weight, partner_tokens))
     partner_weight = shift(weight, "c", 1)
 
     w0 = weight.reshape(32, NY, 64, COLS)
@@ -361,11 +357,11 @@
     first, quarters = near_base(yc, [tokens, near], weight, partner_weight)
     second, more = near_base(yc, [other], weight, partner_weight, (first,))
     far, stack = far_base(yc, q0, q1, w0, w1, [*quarters, *more])
+
     far = more_base(yc, q2, 2, w0, w1, far)
-
     parts = low_parts(yc, stack, recv, far)
-    far = more_base(yc, q3, 3, w0, w1, far)
-    parts = [parts[0]] + [shift(parts[e], "y", e) for e in (2, 1, 3)]
+    far = more_base(yc, q3, 3, in_hbm(w0), in_hbm(w1), far)
+    parts = [parts[0]] + [shift(parts[e], "y", e) for e in (1, 2, 3)]
     up_sorted = up_rows(recv)
     out, out_partner = sum_up(yc, first, second, far, parts, up_sorted)
     theirs = shift(out_partner, "c", 1)

time: 92.6 us -> 91.9 us (level)
  Pallas kernels: 29.2 us -> 23.7 us
  waiting for transfers between devices: 31.2 us -> 36.3 us
    ppermute x6, waiting for transfers between devices: 25.1 us -> 32.3 us  [around(): return lax.ppermute(x, ('y', 'c'), pairs)]
    all_to_all x1, waiting for transfers between devices: 4.6 us -> 2.05 us  [on_device(): recv = lax.all_to_all(send, ('z', 'x', 'c'), 0, 0)]
    pallas_call x2, Pallas kernels: 10.5 us -> 7.93 us  [near_base(): pl.pallas_call(functools.partial(near_kernel, n), grid_spec=pltpu.Prefetc...]
    pallas_call x2, Pallas kernels: 4.68 us -> 3.69 us  [more_base(): pl.pallas_call(more_kernel, grid_spec=pltpu.PrefetchScalarGridSpec(num_sc...]
    pallas_call x1, Pallas kernels: 2.96 us -> 1.98 us  [far_base(): pl.pallas_call(far_kernel, grid_spec=pltpu.PrefetchScalarGridSpec(num_sca...]
    unnamed x10 -> x8, local copies, waits for them, and re-layouts: 3 us -> 3 us
  transfers between devices with their start and end apart: 13 -> 13, of which waited for: 7 -> 8; matrix products, arithmetic and copies ran while one was open for 0% -> 0% of each run, Pallas kernels for 30% -> 21%
where the time goes in v4:
time: 91.9 us; the launch traced here: 91.6 us
  waiting for transfers between devices  36.3 us (39%)
  starting transfers between devices  27.6 us (30%)
  Pallas kernels  23.7 us (26%)
  local copies, waits for them, and re-layouts  3.72 us (4%)
    ppermute x6, waiting for transfers between devices, around(): return lax.ppermute(x, ('y', 'c'), pairs)  32.3 us
    all_to_all x1, starting transfers between devices, on_device(): recv = lax.all_to_all(send, ('z', 'x', 'c'), 0, 0)  11.6 us
    ppermute x6, starting transfers between devices, shift(): return lax.ppermute(x, axis, [(i, (i + by) % n) for i in range(n)])  11 us
    pallas_call x2, Pallas kernels, near_base(): pl.pallas_call(functools.partial(near_kernel, n), grid_spec=pltpu.Prefetc...  7.93 us
    ppermute x6, starting transfers between devices, around(): return lax.ppermute(x, ('y', 'c'), pairs)  4.99 us
    pallas_call x1, Pallas kernels, split_quarters(): pl.pallas_call(split_kernel, grid_spec=pltpu.PrefetchScalarGridSpec(num_s...  3.8 us
    pallas_call x2, Pallas kernels, more_base(): pl.pallas_call(more_kernel, grid_spec=pltpu.PrefetchScalarGridSpec(num_sc...  3.69 us
    unnamed x8, local copies, waits for them, and re-layouts  3 us
  transfers between devices with their start and end apart: 13, of which 8 were waited for; matrix products, arithmetic and copies ran while one was open for 0% of the time, Pallas kernels for 21%

profile of v4, /device:TPU:1, one launch (start us, length us, event | category | flops | bytes accessed | tf_op | source)
XLA Modules:
  0.0 91.6 jit_solution(2459295227280775713)
XLA Ops:
  0.0 2.8 %shard_map.64 = bf16[64,144,128]{2,1,0:T(8,128)(2,1)} custom-call(s32[128]{0:T(128)} %apr.1, s32[256]{0:T(256)} %rps.1, bf16[64,32,128]{2,1,0:T(8,128)(2,1)} %down_ref.1, bf16[64,2,256]{2,1,0:T(2,128)(2,1)} %up_ref.1), custom_call_target="tpu_custom_call" | custom-call | bytes 3145728 | tf_op jit(solution)/shard_map/pallas_call | solution.py:84
  2.8 3.3 %collective-permute-start.1 = (bf16[128,8192]{1,0:T(8,128)(2,1)}, bf16[128,8192]{1,0:T(8,128)(2,1)}, u32[]{:S(2)}, u32[]{:S(2)}) collective-permute-start(bf16[128,8192]{1,0:T(8,128)(2,1)} %refs_0_), channel_id=1, source_target_pairs={{0,1},{1,0},{2,3},{3,2},{4,5},{5,4},{6,7},{7,6},{8,9},{9,8},{10,11... | collective-permute-start | bytes 6291464 | tf_op jit(solution)/shard_map/ppermute | solution.py:39
  6.1 1.0 %collective-permute-start = (bf16[128,8192]{1,0:T(8,128)(2,1)}, bf16[128,8192]{1,0:T(8,128)(2,1)}, u32[]{:S(2)}, u32[]{:S(2)}) collective-permute-start(bf16[128,8192]{1,0:T(8,128)(2,1)} %refs_0_), channel_id=1, source_target_pairs={{0,2},{1,7},{2,4},{3,1},{4,6},{5,3},{6,0},{7,5},{8,10},{9,15},{10,... | collective-permute-start | bytes 6291464 | tf_op jit(solution)/shard_map/ppermute | solution.py:48
  7.1 11.6 %all-to-all-start = ((bf16[64,144,128]{2,1,0:T(8,128)(2,1)}), bf16[64,144,128]{2,1,0:T(8,128)(2,1)S(1)}, u32[]{:S(2)}, u32[]{:S(2)}) async-start(bf16[64,144,128]{2,1,0:T(8,128)(2,1)} %shard_map.64), calls=%async_computation | async-start | bytes 4718592 | tf_op jit(solution)/shard_map/all_to_all | solution.py:351
  18.7 0.0 collective-permute-done.1
  18.7 0.5 collective-permute-start.2
  19.3 0.5 collective-permute-start.3
  19.7 11.9 %collective-permute-done.refs_1_.x_ref = bf16[128,8192]{1,0:T(8,128)(2,1)} collective-permute-done((bf16[128,8192]{1,0:T(8,128)(2,1)}, bf16[128,8192]{1,0:T(8,128)(2,1)}, u32[]{:S(2)}, u32[]{:S(2)}) %collective-permute-start) | collective-permute-done | bytes 2097184 | tf_op jit(solution)/shard_map/ppermute | solution.py:48
  31.6 0.0 copy-start
  31.6 3.8 %shard_map.67 = (bf16[128,2048]{1,0:T(8,128)(2,1)S(1)}, bf16[128,2048]{1,0:T(8,128)(2,1)S(1)}, bf16[128,2048]{1,0:T(8,128)(2,1)S(1)}, bf16[128,2048]{1,0:T(8,128)(2,1)}) custom-call(s32[1]{0:T(128)} %bitcast.2.first, bf16[128,8192]{1,0:T(8,128)(2,1)} %collective-permute-done.refs_1_.x_ref), custom_call_target="tpu_custom_call" | custom-call | flops 99999997952 | bytes 4194304 | tf_op jit(solution)/shard_map/pallas_call | solution.py:121
  35.4 2.0 %collective-permute-start.6 = (bf16[128,2048]{1,0:T(8,128)(2,1)S(1)}, bf16[128,2048]{1,0:T(8,128)(2,1)S(1)}, u32[]{:S(2)}, u32[]{:S(2)}) collective-permute-start(bf16[128,2048]{1,0:T(8,128)(2,1)S(1)} %get-tuple-element.31), channel_id=1, source_target_pairs={{0,2},{1,7},{2,4},{3,1},{4,6},{5,3},{6,0},{7,5},{8,10},{9,15},{10,... | collective-permute-start | bytes 1572872 | tf_op jit(solution)/shard_map/ppermute | solution.py:48
  37.4 0.0 collective-permute-start.7
  37.4 0.0 collective-permute-start.5
  37.4 0.0 collective-permute-done.2.refs_3_.refs_2_
  37.4 0.0 copy-start.1
  37.4 1.5 %collective-permute-start.4 = (bf16[128,2048]{1,0:T(8,128)(2,1)}, bf16[128,2048]{1,0:T(8,128)(2,1)}, u32[]{:S(2)}, u32[]{:S(2)}) collective-permute-start(bf16[128,2048]{1,0:T(8,128)(2,1)} %get-tuple-element.29), channel_id=1, source_target_pairs={{0,2},{1,7},{2,4},{3,1},{4,6},{5,3},{6,0},{7,5},{8,10},{9,15},{10,... | collective-permute-start | bytes 1572872 | tf_op jit(solution)/shard_map/ppermute | solution.py:48
  38.9 0.1 pad_add_fusion.yc
  39.0 0.0 copy-done
  39.0 5.3 %shard_map.65 = (f32[256,512]{1,0:T(8,128)S(1)}, bf16[128,2048]{1,0:T(8,128)(2,1)S(1)}, bf16[128,2048]{1,0:T(8,128)(2,1)S(1)}) custom-call(s32[2]{0:T(128)S(1)} %pad_add_fusion.yc, bf16[128,8192]{1,0:T(8,128)(2,1)} %refs_0_, bf16[128,8192]{1,0:T(8,128)(2,1)} %collective-permute-done.refs_1_.x_ref, bf16[8192,256]{1,0:T(8,128)(2,1)S(1)} %copy-done, ...), custom_call_target="tpu_custom_call" | custom-call | flops 2147483648 | bytes 12582912 | tf_op jit(solution)/shard_map/pallas_call | solution.py:215
  44.3 11.4 %collective-permute-done.3.refs_0_ = bf16[128,8192]{1,0:T(8,128)(2,1)S(1)} collective-permute-done((bf16[128,8192]{1,0:T(8,128)(2,1)}, bf16[128,8192]{1,0:T(8,128)(2,1)S(1)}, u32[]{:S(2)}, u32[]{:S(2)}) %collective-permute-start.3) | collective-permute-done | bytes 2097184 | tf_op jit(solution)/shard_map/ppermute | solution.py:48
  55.7 2.6 %shard_map.66 = (f32[128,512]{1,0:T(8,128)S(1)}, bf16[128,2048]{1,0:T(8,128)(2,1)S(1)}) custom-call(s32[2]{0:T(128)S(1)} %pad_add_fusion.yc, bf16[128,8192]{1,0:T(8,128)(2,1)S(1)} %collective-permute-done.3.refs_0_, bf16[8192,256]{1,0:T(8,128)(2,1)S(1)} %copy-done, bf16[8192,256]{1,0:T(8,128)(2,1)S(1)} %collective-permute-done.2.refs_3_.refs_2_, ...), custom_call_target="tpu_custom_call" | custom-call | flops 1073741824 | bytes 12582912 | tf_op jit(solution)/shard_map/pallas_call | solution.py:215
  58.3 1.2 %collective-permute-done.6.q0 = bf16[128,2048]{1,0:T(8,128)(2,1)S(1)} collective-permute-done((bf16[128,2048]{1,0:T(8,128)(2,1)S(1)}, bf16[128,2048]{1,0:T(8,128)(2,1)S(1)}, u32[]{:S(2)}, u32[]{:S(2)}) %collective-permute-start.6) | collective-permute-done | bytes 524320 | tf_op jit(solution)/shard_map/ppermute | solution.py:48
  59.6 5.6 %collective-permute-done.7.q1 = bf16[128,2048]{1,0:T(8,128)(2,1)S(1)} collective-permute-done((bf16[128,2048]{1,0:T(8,128)(2,1)S(1)}, bf16[128,2048]{1,0:T(8,128)(2,1)S(1)}, u32[]{:S(2)}, u32[]{:S(2)}) %collective-permute-start.7) | collective-permute-done | bytes 524320 | tf_op jit(solution)/shard_map/ppermute | solution.py:48
  65.2 2.0 %shard_map.68 = (f32[128,512]{1,0:T(8,128)S(1)}, bf16[4,128,2048]{2,1,0:T(8,128)(2,1)S(1)}) custom-call(s32[2]{0:T(128)S(1)} %pad_add_fusion.yc, bf16[128,2048]{1,0:T(8,128)(2,1)S(1)} %collective-permute-done.6.q0, bf16[128,2048]{1,0:T(8,128)(2,1)S(1)} %collective-permute-done.7.q1, bf16[32,4,64,256]{3,2,1,0:T(8,128)(2,1)S(1)} %bitcast.11, ...), custom_call_target="tpu_custom_call" | custom-call | flops 536870912 | bytes 10485760 | tf_op jit(solution)/shard_map/pallas_call | solution.py:254
  67.2 0.0 copy-start.2
  67.2 1.4 %copy-done.2 = bf16[4,128,2048]{2,1,0:T(8,128)(2,1)} copy-done((bf16[4,128,2048]{2,1,0:T(8,128)(2,1)}, bf16[4,128,2048]{2,1,0:T(8,128)(2,1)S(1)}, u32[]{:S(2)}) %copy-start.2) | copy-done | bytes 2097176
  68.6 2.2 %collective-permute-done.5.x = bf16[128,2048]{1,0:T(8,128)(2,1)S(1)} collective-permute-done((bf16[128,2048]{1,0:T(8,128)(2,1)S(1)}, bf16[128,2048]{1,0:T(8,128)(2,1)S(1)}, u32[]{:S(2)}, u32[]{:S(2)}) %collective-permute-start.5) | collective-permute-done | bytes 524320 | tf_op jit(solution)/shard_map/ppermute | solution.py:48
  70.8 0.0 copy-done.1
  70.8 1.0 %shard_map.69.before.after = f32[128,512]{1,0:T(8,128)S(1)} custom-call(s32[2]{0:T(128)S(1)} %pad_add_fusion.yc, bf16[128,2048]{1,0:T(8,128)(2,1)S(1)} %collective-permute-done.5.x, bf16[32,4,64,256]{3,2,1,0:T(8,128)(2,1)S(1)} %bitcast.12, bf16[32,4,64,256]{3,2,1,0:T(8,128)(2,1)S(1)} %bitcast.14, f32[128,512]{1,0:T(8,128)S(1)} %get-tuple-element.36.before), custom_call_target="tpu_custom_call" | custom-call | flops 268435456 | bytes 3145728 | tf_op jit(solution)/shard_map/pallas_call | solution.py:283
  71.8 2.1 %all-to-all-done.recv_ref = bf16[64,144,128]{2,1,0:T(8,128)(2,1)S(1)} async-done(((bf16[64,144,128]{2,1,0:T(8,128)(2,1)}), bf16[64,144,128]{2,1,0:T(8,128)(2,1)S(1)}, u32[]{:S(2)}, u32[]{:S(2)}) %all-to-all-start) | async-done | bytes 2359328 | tf_op jit(solution)/shard_map/all_to_all | solution.py:351
  73.9 0.0 copy-start.3
  73.9 1.6 %copy-done.3 = bf16[4,128,2048]{2,1,0:T(8,128)(2,1)S(1)} copy-done((bf16[4,128,2048]{2,1,0:T(8,128)(2,1)S(1)}, bf16[4,128,2048]{2,1,0:T(8,128)(2,1)}, u32[]{:S(2)}) %copy-start.3) | copy-done | bytes 2097176
  75.5 1.6 %shard_map.71 = (f32[256,128]{1,0:T(8,128)S(1)}, f32[256,128]{1,0:T(8,128)S(1)}, f32[256,128]{1,0:T(8,128)S(1)}, f32[256,128]{1,0:T(8,128)S(1)}) custom-call(s32[2]{0:T(128)S(1)} %pad_add_fusion.yc, bf16[4,128,2048]{2,1,0:T(8,128)(2,1)S(1)} %copy-done.3, bf16[64,144,128]{2,1,0:T(8,128)(2,1)S(1)} %all-to-all-done.recv_ref, f32[128,512]{1,0:T(8,128)S(1)} %shard_map.69.before.after), custom_call_target="tpu_custom_call" | custom-call | flops 268435456 | bytes 5242880 | tf_op jit(solution)/shard_map/pallas_call | solution.py:158
  77.0 0.7 collective-permute-start.10
  77.7 1.0 %collective-permute-start.8 = (f32[256,128]{1,0:T(8,128)S(1)}, f32[256,128]{1,0:T(8,128)S(1)}, u32[]{:S(2)}, u32[]{:S(2)}) collective-permute-start(f32[256,128]{1,0:T(8,128)S(1)} %get-tuple-element.40), channel_id=1, source_target_pairs={{0,2},{2,4},{4,6},{6,0},{1,3},{3,5},{5,7},{7,1},{8,10},{10,12},{12... | collective-permute-start | bytes 393224 | tf_op jit(solution)/shard_map/ppermute | solution.py:39
  78.7 1.4 %collective-permute-start.9 = (f32[256,128]{1,0:T(8,128)S(1)}, f32[256,128]{1,0:T(8,128)S(1)}, u32[]{:S(2)}, u32[]{:S(2)}) collective-permute-start(f32[256,128]{1,0:T(8,128)S(1)} %get-tuple-element.41), channel_id=1, source_target_pairs={{0,4},{2,6},{4,0},{6,2},{1,5},{3,7},{5,1},{7,3},{8,12},{10,14},{12... | collective-permute-start | bytes 393224 | tf_op jit(solution)/shard_map/ppermute | solution.py:39
  80.2 0.5 shard_map.72.up
  80.7 0.0 collective-permute-done.4.x
  80.7 2.7 %shard_map.70.far = f32[128,512]{1,0:T(8,128)S(1)} custom-call(s32[2]{0:T(128)S(1)} %pad_add_fusion.yc, bf16[128,2048]{1,0:T(8,128)(2,1)} %collective-permute-done.4.x, bf16[32,4,64,256]{3,2,1,0:T(8,128)(2,1)} %bitcast.10, bf16[32,4,64,256]{3,2,1,0:T(8,128)(2,1)} %bitcast.15, f32[128,512]{1,0:T(8,128)S(1)} %shard_map.69.before.after), custom_call_target="tpu_custom_call" | custom-call | flops 268435456 | bytes 3145728 | tf_op jit(solution)/shard_map/pallas_call | solution.py:283
  83.4 0.0 collective-permute-done.10.p3
  83.4 0.8 collective-permute-done.8.p1
  84.2 0.0 collective-permute-done.9.p2
  84.2 1.5 %shard_map.73 = (bf16[4,2,128,256]{3,2,1,0:T(8,128)(2,1)}, bf16[4,128,256]{2,1,0:T(8,128)(2,1)S(1)}) custom-call(s32[2]{0:T(128)S(1)} %pad_add_fusion.yc, f32[256,512]{1,0:T(8,128)S(1)} %get-tuple-element.27.refs_3_.first, f32[128,512]{1,0:T(8,128)S(1)} %get-tuple-element.28.second, f32[128,512]{1,0:T(8,128)S(1)} %shard_map.70.far, ...), custom_call_target="tpu_custom_call" | custom-call | flops 67108864 | bytes 3145728 | tf_op jit(solution)/shard_map/pallas_call | solution.py:322
  85.7 4.0 %collective-permute-start.11 = (bf16[4,128,256]{2,1,0:T(8,128)(2,1)S(1)}, bf16[4,128,256]{2,1,0:T(8,128)(2,1)S(1)}, u32[]{:S(2)}, u32[]{:S(2)}) collective-permute-start(bf16[4,128,256]{2,1,0:T(8,128)(2,1)S(1)} %get-tuple-element.44), channel_id=1, source_target_pairs={{0,1},{1,0},{2,3},{3,2},{4,5},{5,4},{6,7},{7,6},{8,9},{9,8},{10,11... | collective-permute-start | bytes 786440 | tf_op jit(solution)/shard_map/ppermute | solution.py:39
  89.7 1.2 %collective-permute-done.11 = bf16[4,128,256]{2,1,0:T(8,128)(2,1)S(1)} collective-permute-done((bf16[4,128,256]{2,1,0:T(8,128)(2,1)S(1)}, bf16[4,128,256]{2,1,0:T(8,128)(2,1)S(1)}, u32[]{:S(2)}, u32[]{:S(2)}) %collective-permute-start.11) | collective-permute-done | bytes 262176 | tf_op jit(solution)/shard_map/ppermute | solution.py:39
  90.9 0.7 bitcast_dynamic-update-slice_fusion
Async XLA Ops:
  2.8 15.9 %collective-permute-start.1 = (bf16[128,8192]{1,0:T(8,128)(2,1)}, bf16[128,8192]{1,0:T(8,128)(2,1)}, u32[]{:S(2)}, u32[]{:S(2)}) collective-permute-start(bf16[128,8192]{1,0:T(8,128)(2,1)} %refs_0_), channel_id=1, source_target_pairs={{0,1},{1,0},{2,3},{3,2},{4,5},{5,4},{6,7},{7,6},{8,9},{9,8},{10,11... | collective-permute-start | bytes 6291464 | tf_op jit(solution)/shard_map/ppermute | solution.py:39
  6.1 25.5 %collective-permute-start = (bf16[128,8192]{1,0:T(8,128)(2,1)}, bf16[128,8192]{1,0:T(8,128)(2,1)}, u32[]{:S(2)}, u32[]{:S(2)}) collective-permute-start(bf16[128,8192]{1,0:T(8,128)(2,1)} %refs_0_), channel_id=1, source_target_pairs={{0,2},{1,7},{2,4},{3,1},{4,6},{5,3},{6,0},{7,5},{8,10},{9,15},{10,... | collective-permute-start | bytes 6291464 | tf_op jit(solution)/shard_map/ppermute | solution.py:48
  7.1 66.8 %all-to-all-start = ((bf16[64,144,128]{2,1,0:T(8,128)(2,1)}), bf16[64,144,128]{2,1,0:T(8,128)(2,1)S(1)}, u32[]{:S(2)}, u32[]{:S(2)}) async-start(bf16[64,144,128]{2,1,0:T(8,128)(2,1)} %shard_map.64), calls=%async_computation | async-start | bytes 4718592 | tf_op jit(solution)/shard_map/all_to_all | solution.py:351
  18.7 18.7 %collective-permute-start.2 = (bf16[8192,256]{1,0:T(8,128)(2,1)}, bf16[8192,256]{1,0:T(8,128)(2,1)S(1)}, u32[]{:S(2)}, u32[]{:S(2)}) collective-permute-start(bf16[8192,256]{1,0:T(8,128)(2,1)} %refs_1_), channel_id=1, source_target_pairs={{0,1},{1,0},{2,3},{3,2},{4,5},{5,4},{6,7},{7,6},{8,9},{9,8},{10,11... | collective-permute-start | bytes 12582920 | tf_op jit(solution)/shard_map/ppermute | solution.py:39
  19.3 36.5 %collective-permute-start.3 = (bf16[128,8192]{1,0:T(8,128)(2,1)}, bf16[128,8192]{1,0:T(8,128)(2,1)S(1)}, u32[]{:S(2)}, u32[]{:S(2)}) collective-permute-start(bf16[128,8192]{1,0:T(8,128)(2,1)} %collective-permute-done.1), channel_id=1, source_target_pairs={{0,3},{1,6},{2,5},{3,0},{4,7},{5,2},{6,1},{7,4},{8,11},{9,14},{10,... | collective-permute-start | bytes 6291464 | tf_op jit(solution)/shard_map/ppermute | solution.py:48
  31.6 7.4 %copy-start = (bf16[8192,256]{1,0:T(8,128)(2,1)S(1)}, bf16[8192,256]{1,0:T(8,128)(2,1)}, u32[]{:S(2)}) copy-start(bf16[8192,256]{1,0:T(8,128)(2,1)} %refs_1_) | copy-start | bytes 12582916
  35.4 24.2 %collective-permute-start.6 = (bf16[128,2048]{1,0:T(8,128)(2,1)S(1)}, bf16[128,2048]{1,0:T(8,128)(2,1)S(1)}, u32[]{:S(2)}, u32[]{:S(2)}) collective-permute-start(bf16[128,2048]{1,0:T(8,128)(2,1)S(1)} %get-tuple-element.31), channel_id=1, source_target_pairs={{0,2},{1,7},{2,4},{3,1},{4,6},{5,3},{6,0},{7,5},{8,10},{9,15},{10,... | collective-permute-start | bytes 1572872 | tf_op jit(solution)/shard_map/ppermute | solution.py:48
  37.4 27.8 %collective-permute-start.7 = (bf16[128,2048]{1,0:T(8,128)(2,1)S(1)}, bf16[128,2048]{1,0:T(8,128)(2,1)S(1)}, u32[]{:S(2)}, u32[]{:S(2)}) collective-permute-start(bf16[128,2048]{1,0:T(8,128)(2,1)S(1)} %get-tuple-element.32), channel_id=1, source_target_pairs={{0,2},{1,7},{2,4},{3,1},{4,6},{5,3},{6,0},{7,5},{8,10},{9,15},{10,... | collective-permute-start | bytes 1572872 | tf_op jit(solution)/shard_map/ppermute | solution.py:48
  37.4 33.4 %collective-permute-start.5 = (bf16[128,2048]{1,0:T(8,128)(2,1)S(1)}, bf16[128,2048]{1,0:T(8,128)(2,1)S(1)}, u32[]{:S(2)}, u32[]{:S(2)}) collective-permute-start(bf16[128,2048]{1,0:T(8,128)(2,1)S(1)} %get-tuple-element.30), channel_id=1, source_target_pairs={{0,2},{1,7},{2,4},{3,1},{4,6},{5,3},{6,0},{7,5},{8,10},{9,15},{10,... | collective-permute-start | bytes 1572872 | tf_op jit(solution)/shard_map/ppermute | solution.py:48
  37.4 33.4 %copy-start.1 = (bf16[8192,256]{1,0:T(8,128)(2,1)}, bf16[8192,256]{1,0:T(8,128)(2,1)S(1)}, u32[]{:S(2)}) copy-start(bf16[8192,256]{1,0:T(8,128)(2,1)S(1)} %collective-permute-done.2.refs_3_.refs_2_) | copy-start | bytes 12582916
  37.4 43.3 %collective-permute-start.4 = (bf16[128,2048]{1,0:T(8,128)(2,1)}, bf16[128,2048]{1,0:T(8,128)(2,1)}, u32[]{:S(2)}, u32[]{:S(2)}) collective-permute-start(bf16[128,2048]{1,0:T(8,128)(2,1)} %get-tuple-element.29), channel_id=1, source_target_pairs={{0,2},{1,7},{2,4},{3,1},{4,6},{5,3},{6,0},{7,5},{8,10},{9,15},{10,... | collective-permute-start | bytes 1572872 | tf_op jit(solution)/shard_map/ppermute | solution.py:48
  67.2 1.4 %copy-start.2 = (bf16[4,128,2048]{2,1,0:T(8,128)(2,1)}, bf16[4,128,2048]{2,1,0:T(8,128)(2,1)S(1)}, u32[]{:S(2)}) copy-start(bf16[4,128,2048]{2,1,0:T(8,128)(2,1)S(1)} %get-tuple-element.37.x_ref) | copy-start | bytes 6291460
  73.9 1.6 %copy-start.3 = (bf16[4,128,2048]{2,1,0:T(8,128)(2,1)S(1)}, bf16[4,128,2048]{2,1,0:T(8,128)(2,1)}, u32[]{:S(2)}) copy-start(bf16[4,128,2048]{2,1,0:T(8,128)(2,1)} %copy-done.2) | copy-start | bytes 6291460
  77.0 6.4 %collective-permute-start.10 = (f32[256,128]{1,0:T(8,128)S(1)}, f32[256,128]{1,0:T(8,128)S(1)}, u32[]{:S(2)}, u32[]{:S(2)}) collective-permute-start(f32[256,128]{1,0:T(8,128)S(1)} %get-tuple-element.42), channel_id=1, source_target_pairs={{0,6},{2,0},{4,2},{6,4},{1,7},{3,1},{5,3},{7,5},{8,14},{10,8},{12,... | collective-permute-start | bytes 393224 | tf_op jit(solution)/shard_map/ppermute | solution.py:39
  77.7 6.4 %collective-permute-start.8 = (f32[256,128]{1,0:T(8,128)S(1)}, f32[256,128]{1,0:T(8,128)S(1)}, u32[]{:S(2)}, u32[]{:S(2)}) collective-permute-start(f32[256,128]{1,0:T(8,128)S(1)} %get-tuple-element.40), channel_id=1, source_target_pairs={{0,2},{2,4},{4,6},{6,0},{1,3},{3,5},{5,7},{7,1},{8,10},{10,12},{12... | collective-permute-start | bytes 393224 | tf_op jit(solution)/shard_map/ppermute | solution.py:39
  78.7 5.4 %collective-permute-start.9 = (f32[256,128]{1,0:T(8,128)S(1)}, f32[256,128]{1,0:T(8,128)S(1)}, u32[]{:S(2)}, u32[]{:S(2)}) collective-permute-start(f32[256,128]{1,0:T(8,128)S(1)} %get-tuple-element.41), channel_id=1, source_target_pairs={{0,4},{2,6},{4,0},{6,2},{1,5},{3,7},{5,1},{7,3},{8,12},{10,14},{12... | collective-permute-start | bytes 393224 | tf_op jit(solution)/shard_map/ppermute | solution.py:39
  85.7 5.1 %collective-permute-start.11 = (bf16[4,128,256]{2,1,0:T(8,128)(2,1)S(1)}, bf16[4,128,256]{2,1,0:T(8,128)(2,1)S(1)}, u32[]{:S(2)}, u32[]{:S(2)}) collective-permute-start(bf16[4,128,256]{2,1,0:T(8,128)(2,1)S(1)} %get-tuple-element.44), channel_id=1, source_target_pairs={{0,1},{1,0},{2,3},{3,2},{4,5},{5,4},{6,7},{7,6},{8,9},{9,8},{10,11... | collective-permute-start | bytes 786440 | tf_op jit(solution)/shard_map/ppermute | solution.py:39

commit v5 on v4

--- a/solution.py
+++ b/solution.py
@@ -140,13 +140,13 @@
         factor = recv_ref[:, pl.ds(pl.multiple_of(32 * s, 32), 32), :].reshape(KQ, 128)
         sums[s] = jnp.dot(x_ref[i], factor, preferred_element_type=F32)
     lane = lax.broadcasted_iota(jnp.int32, (128, 128), 1)
-    for e in range(NY):
-        value = (me + e) % NY >= NY // 2
-        for pair in range(2):
-            a, b = sums[2 * pair], sums[2 * pair + 1]
-            keys = jnp.where(lane < 64, a, pltpu.roll(b, 64, 1))
-            values = jnp.where(lane < 64, pltpu.roll(a, 64, 1), b)
-            outs[e][128 * pair : 128 * pair + 128, :] = jnp.where(value, values, keys)
+    for pair in range(2):
+        rows = slice(128 * pair, 128 * pair + 128)
+        a, b = sums[2 * pair], sums[2 * pair + 1]
+        keys = jnp.where(lane < 64, a, pltpu.roll(b, 64, 1))
+        values = jnp.where(lane < 64, pltpu.roll(a, 64, 1), b)
+        for e in range(NY):
+            outs[e][rows, :] = jnp.where(((me + e) & 3) >= 2, values, keys)
 
 
 SMEM = pl.BlockSpec(memory_space=pltpu.SMEM)
@@ -304,17 +304,21 @@
     me, core = yc[0], yc[1]
     low = (p0[...] + p1[...] + p2[...] + p3[...]).astype(BF16).astype(F32)
     left = lax.broadcasted_iota(jnp.int32, (128, 128), 1) < 64
-    bases = (first[:SEG, :], first[SEG:, :], second[...], far[...])
-    for d, base in zip((0, 3 - 2 * core, 1 + 2 * core, 2), bases):
-        s = (me + d) & 3
-        both = jnp.where(s < 2, low[:SEG], low[SEG:])
-        mine = jnp.where(left == (s & 1 == 0), both, 0.0).astype(BF16)
-        own = jnp.dot(mine, up[core, s // 2], preferred_element_type=F32)
-        other = jnp.dot(mine, up[1 - core, s // 2], preferred_element_type=F32)
-        held[s] = (base[:, :COLS] + own).astype(BF16)
-        out_partner[s] = (base[:, COLS:] + other).astype(BF16)
     copy = pltpu.make_async_copy(held, out.at[:, core], sem)
-    copy.start()
+    for side, columns, to in (
+        (core, slice(0, COLS), held),
+        (1 - core, slice(COLS, 2 * COLS), out_partner),
+    ):
+        bases = (first[:SEG, columns], first[SEG:, columns])
+        bases += (second[:, columns], far[:, columns])
+        for d, base in zip((0, 3 - 2 * core, 1 + 2 * core, 2), bases):
+            s = (me + d) & 3
+            both = jnp.where(s < 2, low[:SEG], low[SEG:])
+            mine = jnp.where(left == (s & 1 == 0), both, 0.0).astype(BF16)
+            delta = jnp.dot(mine, up[side, s // 2], preferred_element_type=F32)
+            to[s] = (base + delta).astype(BF16)
+        if to is held:
+            copy.start()
     copy.wait()
 
 

time: 91.9 us -> 91.7 us (level)
  no operation moved by 1% of the time
where the time goes in v5:
time: 91.7 us; the launch traced here: 91.3 us
  waiting for transfers between devices  36.3 us (40%)
  starting transfers between devices  27.6 us (30%)
  Pallas kernels  23.5 us (26%)
  local copies, waits for them, and re-layouts  3.72 us (4%)
    ppermute x6, waiting for transfers between devices, around(): return lax.ppermute(x, ('y', 'c'), pairs)  32.3 us
    all_to_all x1, starting transfers between devices, on_device(): recv = lax.all_to_all(send, ('z', 'x', 'c'), 0, 0)  11.6 us
    ppermute x6, starting transfers between devices, shift(): return lax.ppermute(x, axis, [(i, (i + by) % n) for i in range(n)])  11 us
    pallas_call x2, Pallas kernels, near_base(): pl.pallas_call(functools.partial(near_kernel, n), grid_spec=pltpu.Prefetc...  7.93 us
    ppermute x6, starting transfers between devices, around(): return lax.ppermute(x, ('y', 'c'), pairs)  4.99 us
    pallas_call x1, Pallas kernels, split_quarters(): pl.pallas_call(split_kernel, grid_spec=pltpu.PrefetchScalarGridSpec(num_s...  3.8 us
    pallas_call x2, Pallas kernels, more_base(): pl.pallas_call(more_kernel, grid_spec=pltpu.PrefetchScalarGridSpec(num_sc...  3.69 us
    unnamed x8, local copies, waits for them, and re-layouts  3 us
  transfers between devices with their start and end apart: 13, of which 8 were waited for; matrix products, arithmetic and copies ran while one was open for 0% of the time, Pallas kernels for 21%

profile of v5, /device:TPU:1, one launch (start us, length us, event | category | flops | bytes accessed | tf_op | source)
XLA Modules:
  0.0 91.3 jit_solution(1087206078332307254)
XLA Ops:
  0.0 2.8 %shard_map.64 = bf16[64,144,128]{2,1,0:T(8,128)(2,1)} custom-call(s32[128]{0:T(128)} %apr.1, s32[256]{0:T(256)} %rps.1, bf16[64,32,128]{2,1,0:T(8,128)(2,1)} %down_ref.1, bf16[64,2,256]{2,1,0:T(2,128)(2,1)} %up_ref.1), custom_call_target="tpu_custom_call" | custom-call | bytes 3145728 | tf_op jit(solution)/shard_map/pallas_call | solution.py:84
  2.8 3.3 %collective-permute-start.1 = (bf16[128,8192]{1,0:T(8,128)(2,1)}, bf16[128,8192]{1,0:T(8,128)(2,1)}, u32[]{:S(2)}, u32[]{:S(2)}) collective-permute-start(bf16[128,8192]{1,0:T(8,128)(2,1)} %refs_0_), channel_id=1, source_target_pairs={{0,1},{1,0},{2,3},{3,2},{4,5},{5,4},{6,7},{7,6},{8,9},{9,8},{10,11... | collective-permute-start | bytes 6291464 | tf_op jit(solution)/shard_map/ppermute | solution.py:39
  6.1 1.0 %collective-permute-start = (bf16[128,8192]{1,0:T(8,128)(2,1)}, bf16[128,8192]{1,0:T(8,128)(2,1)}, u32[]{:S(2)}, u32[]{:S(2)}) collective-permute-start(bf16[128,8192]{1,0:T(8,128)(2,1)} %refs_0_), channel_id=1, source_target_pairs={{0,2},{1,7},{2,4},{3,1},{4,6},{5,3},{6,0},{7,5},{8,10},{9,15},{10,... | collective-permute-start | bytes 6291464 | tf_op jit(solution)/shard_map/ppermute | solution.py:48
  7.1 11.6 %all-to-all-start = ((bf16[64,144,128]{2,1,0:T(8,128)(2,1)}), bf16[64,144,128]{2,1,0:T(8,128)(2,1)S(1)}, u32[]{:S(2)}, u32[]{:S(2)}) async-start(bf16[64,144,128]{2,1,0:T(8,128)(2,1)} %shard_map.64), calls=%async_computation | async-start | bytes 4718592 | tf_op jit(solution)/shard_map/all_to_all | solution.py:355
  18.7 0.0 collective-permute-done.1
  18.7 0.5 collective-permute-start.2
  19.3 0.5 collective-permute-start.3
  19.7 11.9 %collective-permute-done.refs_1_.x_ref = bf16[128,8192]{1,0:T(8,128)(2,1)} collective-permute-done((bf16[128,8192]{1,0:T(8,128)(2,1)}, bf16[128,8192]{1,0:T(8,128)(2,1)}, u32[]{:S(2)}, u32[]{:S(2)}) %collective-permute-start) | collective-permute-done | bytes 2097184 | tf_op jit(solution)/shard_map/ppermute | solution.py:48
  31.6 0.0 copy-start
  31.6 3.8 %shard_map.67 = (bf16[128,2048]{1,0:T(8,128)(2,1)S(1)}, bf16[128,2048]{1,0:T(8,128)(2,1)S(1)}, bf16[128,2048]{1,0:T(8,128)(2,1)S(1)}, bf16[128,2048]{1,0:T(8,128)(2,1)}) custom-call(s32[1]{0:T(128)} %bitcast.2.first, bf16[128,8192]{1,0:T(8,128)(2,1)} %collective-permute-done.refs_1_.x_ref), custom_call_target="tpu_custom_call" | custom-call | flops 99999997952 | bytes 4194304 | tf_op jit(solution)/shard_map/pallas_call | solution.py:121
  35.4 2.0 %collective-permute-start.6 = (bf16[128,2048]{1,0:T(8,128)(2,1)S(1)}, bf16[128,2048]{1,0:T(8,128)(2,1)S(1)}, u32[]{:S(2)}, u32[]{:S(2)}) collective-permute-start(bf16[128,2048]{1,0:T(8,128)(2,1)S(1)} %get-tuple-element.31), channel_id=1, source_target_pairs={{0,2},{1,7},{2,4},{3,1},{4,6},{5,3},{6,0},{7,5},{8,10},{9,15},{10,... | collective-permute-start | bytes 1572872 | tf_op jit(solution)/shard_map/ppermute | solution.py:48
  37.4 0.0 collective-permute-start.7
  37.4 0.0 collective-permute-start.5
  37.4 0.0 collective-permute-done.2.refs_3_.refs_2_
  37.4 0.0 copy-start.1
  37.4 1.5 %collective-permute-start.4 = (bf16[128,2048]{1,0:T(8,128)(2,1)}, bf16[128,2048]{1,0:T(8,128)(2,1)}, u32[]{:S(2)}, u32[]{:S(2)}) collective-permute-start(bf16[128,2048]{1,0:T(8,128)(2,1)} %get-tuple-element.29), channel_id=1, source_target_pairs={{0,2},{1,7},{2,4},{3,1},{4,6},{5,3},{6,0},{7,5},{8,10},{9,15},{10,... | collective-permute-start | bytes 1572872 | tf_op jit(solution)/shard_map/ppermute | solution.py:48
  38.9 0.1 pad_add_fusion.yc
  39.0 0.0 copy-done
  39.0 5.3 %shard_map.65 = (f32[256,512]{1,0:T(8,128)S(1)}, bf16[128,2048]{1,0:T(8,128)(2,1)S(1)}, bf16[128,2048]{1,0:T(8,128)(2,1)S(1)}) custom-call(s32[2]{0:T(128)S(1)} %pad_add_fusion.yc, bf16[128,8192]{1,0:T(8,128)(2,1)} %refs_0_, bf16[128,8192]{1,0:T(8,128)(2,1)} %collective-permute-done.refs_1_.x_ref, bf16[8192,256]{1,0:T(8,128)(2,1)S(1)} %copy-done, ...), custom_call_target="tpu_custom_call" | custom-call | flops 2147483648 | bytes 12582912 | tf_op jit(solution)/shard_map/pallas_call | solution.py:215
  44.3 11.4 %collective-permute-done.3.refs_0_ = bf16[128,8192]{1,0:T(8,128)(2,1)S(1)} collective-permute-done((bf16[128,8192]{1,0:T(8,128)(2,1)}, bf16[128,8192]{1,0:T(8,128)(2,1)S(1)}, u32[]{:S(2)}, u32[]{:S(2)}) %collective-permute-start.3) | collective-permute-done | bytes 2097184 | tf_op jit(solution)/shard_map/ppermute | solution.py:48
  55.7 2.6 %shard_map.66 = (f32[128,512]{1,0:T(8,128)S(1)}, bf16[128,2048]{1,0:T(8,128)(2,1)S(1)}) custom-call(s32[2]{0:T(128)S(1)} %pad_add_fusion.yc, bf16[128,8192]{1,0:T(8,128)(2,1)S(1)} %collective-permute-done.3.refs_0_, bf16[8192,256]{1,0:T(8,128)(2,1)S(1)} %copy-done, bf16[8192,256]{1,0:T(8,128)(2,1)S(1)} %collective-permute-done.2.refs_3_.refs_2_, ...), custom_call_target="tpu_custom_call" | custom-call | flops 1073741824 | bytes 12582912 | tf_op jit(solution)/shard_map/pallas_call | solution.py:215
  58.3 1.2 %collective-permute-done.6.q0 = bf16[128,2048]{1,0:T(8,128)(2,1)S(1)} collective-permute-done((bf16[128,2048]{1,0:T(8,128)(2,1)S(1)}, bf16[128,2048]{1,0:T(8,128)(2,1)S(1)}, u32[]{:S(2)}, u32[]{:S(2)}) %collective-permute-start.6) | collective-permute-done | bytes 524320 | tf_op jit(solution)/shard_map/ppermute | solution.py:48
  59.6 5.6 %collective-permute-done.7.q1 = bf16[128,2048]{1,0:T(8,128)(2,1)S(1)} collective-permute-done((bf16[128,2048]{1,0:T(8,128)(2,1)S(1)}, bf16[128,2048]{1,0:T(8,128)(2,1)S(1)}, u32[]{:S(2)}, u32[]{:S(2)}) %collective-permute-start.7) | collective-permute-done | bytes 524320 | tf_op jit(solution)/shard_map/ppermute | solution.py:48
  65.2 2.0 %shard_map.68 = (f32[128,512]{1,0:T(8,128)S(1)}, bf16[4,128,2048]{2,1,0:T(8,128)(2,1)S(1)}) custom-call(s32[2]{0:T(128)S(1)} %pad_add_fusion.yc, bf16[128,2048]{1,0:T(8,128)(2,1)S(1)} %collective-permute-done.6.q0, bf16[128,2048]{1,0:T(8,128)(2,1)S(1)} %collective-permute-done.7.q1, bf16[32,4,64,256]{3,2,1,0:T(8,128)(2,1)S(1)} %bitcast.11, ...), custom_call_target="tpu_custom_call" | custom-call | flops 536870912 | bytes 10485760 | tf_op jit(solution)/shard_map/pallas_call | solution.py:254
  67.2 0.0 copy-start.2
  67.2 1.4 %copy-done.2 = bf16[4,128,2048]{2,1,0:T(8,128)(2,1)} copy-done((bf16[4,128,2048]{2,1,0:T(8,128)(2,1)}, bf16[4,128,2048]{2,1,0:T(8,128)(2,1)S(1)}, u32[]{:S(2)}) %copy-start.2) | copy-done | bytes 2097176
  68.6 2.2 %collective-permute-done.5.x = bf16[128,2048]{1,0:T(8,128)(2,1)S(1)} collective-permute-done((bf16[128,2048]{1,0:T(8,128)(2,1)S(1)}, bf16[128,2048]{1,0:T(8,128)(2,1)S(1)}, u32[]{:S(2)}, u32[]{:S(2)}) %collective-permute-start.5) | collective-permute-done | bytes 524320 | tf_op jit(solution)/shard_map/ppermute | solution.py:48
  70.8 0.0 copy-done.1
  70.8 1.0 %shard_map.69.before.after = f32[128,512]{1,0:T(8,128)S(1)} custom-call(s32[2]{0:T(128)S(1)} %pad_add_fusion.yc, bf16[128,2048]{1,0:T(8,128)(2,1)S(1)} %collective-permute-done.5.x, bf16[32,4,64,256]{3,2,1,0:T(8,128)(2,1)S(1)} %bitcast.12, bf16[32,4,64,256]{3,2,1,0:T(8,128)(2,1)S(1)} %bitcast.14, f32[128,512]{1,0:T(8,128)S(1)} %get-tuple-element.36.before), custom_call_target="tpu_custom_call" | custom-call | flops 268435456 | bytes 3145728 | tf_op jit(solution)/shard_map/pallas_call | solution.py:283
  71.8 2.1 %all-to-all-done.recv_ref = bf16[64,144,128]{2,1,0:T(8,128)(2,1)S(1)} async-done(((bf16[64,144,128]{2,1,0:T(8,128)(2,1)}), bf16[64,144,128]{2,1,0:T(8,128)(2,1)S(1)}, u32[]{:S(2)}, u32[]{:S(2)}) %all-to-all-start) | async-done | bytes 2359328 | tf_op jit(solution)/shard_map/all_to_all | solution.py:355
  73.9 0.0 copy-start.3
  73.9 1.6 %copy-done.3 = bf16[4,128,2048]{2,1,0:T(8,128)(2,1)S(1)} copy-done((bf16[4,128,2048]{2,1,0:T(8,128)(2,1)S(1)}, bf16[4,128,2048]{2,1,0:T(8,128)(2,1)}, u32[]{:S(2)}) %copy-start.3) | copy-done | bytes 2097176
  75.5 1.4 %shard_map.71 = (f32[256,128]{1,0:T(8,128)S(1)}, f32[256,128]{1,0:T(8,128)S(1)}, f32[256,128]{1,0:T(8,128)S(1)}, f32[256,128]{1,0:T(8,128)S(1)}) custom-call(s32[2]{0:T(128)S(1)} %pad_add_fusion.yc, bf16[4,128,2048]{2,1,0:T(8,128)(2,1)S(1)} %copy-done.3, bf16[64,144,128]{2,1,0:T(8,128)(2,1)S(1)} %all-to-all-done.recv_ref, f32[128,512]{1,0:T(8,128)S(1)} %shard_map.69.before.after), custom_call_target="tpu_custom_call" | custom-call | flops 268435456 | bytes 5242880 | tf_op jit(solution)/shard_map/pallas_call | solution.py:158
  76.8 0.7 collective-permute-start.10
  77.6 1.0 %collective-permute-start.8 = (f32[256,128]{1,0:T(8,128)S(1)}, f32[256,128]{1,0:T(8,128)S(1)}, u32[]{:S(2)}, u32[]{:S(2)}) collective-permute-start(f32[256,128]{1,0:T(8,128)S(1)} %get-tuple-element.40), channel_id=1, source_target_pairs={{0,2},{2,4},{4,6},{6,0},{1,3},{3,5},{5,7},{7,1},{8,10},{10,12},{12... | collective-permute-start | bytes 393224 | tf_op jit(solution)/shard_map/ppermute | solution.py:39
  78.6 1.4 %collective-permute-start.9 = (f32[256,128]{1,0:T(8,128)S(1)}, f32[256,128]{1,0:T(8,128)S(1)}, u32[]{:S(2)}, u32[]{:S(2)}) collective-permute-start(f32[256,128]{1,0:T(8,128)S(1)} %get-tuple-element.41), channel_id=1, source_target_pairs={{0,4},{2,6},{4,0},{6,2},{1,5},{3,7},{5,1},{7,3},{8,12},{10,14},{12... | collective-permute-start | bytes 393224 | tf_op jit(solution)/shard_map/ppermute | solution.py:39
  80.0 0.5 shard_map.72.up
  80.5 0.0 collective-permute-done.4.x
  80.5 2.7 %shard_map.70.far = f32[128,512]{1,0:T(8,128)S(1)} custom-call(s32[2]{0:T(128)S(1)} %pad_add_fusion.yc, bf16[128,2048]{1,0:T(8,128)(2,1)} %collective-permute-done.4.x, bf16[32,4,64,256]{3,2,1,0:T(8,128)(2,1)} %bitcast.10, bf16[32,4,64,256]{3,2,1,0:T(8,128)(2,1)} %bitcast.15, f32[128,512]{1,0:T(8,128)S(1)} %shard_map.69.before.after), custom_call_target="tpu_custom_call" | custom-call | flops 268435456 | bytes 3145728 | tf_op jit(solution)/shard_map/pallas_call | solution.py:283
  83.2 0.0 collective-permute-done.10.p3
  83.2 0.8 collective-permute-done.8.p1
  84.0 0.0 collective-permute-done.9.p2
  84.0 1.5 %shard_map.73 = (bf16[4,2,128,256]{3,2,1,0:T(8,128)(2,1)}, bf16[4,128,256]{2,1,0:T(8,128)(2,1)S(1)}) custom-call(s32[2]{0:T(128)S(1)} %pad_add_fusion.yc, f32[256,512]{1,0:T(8,128)S(1)} %get-tuple-element.27.refs_3_.first, f32[128,512]{1,0:T(8,128)S(1)} %get-tuple-element.28.second, f32[128,512]{1,0:T(8,128)S(1)} %shard_map.70.far, ...), custom_call_target="tpu_custom_call" | custom-call | flops 67108864 | bytes 3145728 | tf_op jit(solution)/shard_map/pallas_call | solution.py:326
  85.5 4.0 %collective-permute-start.11 = (bf16[4,128,256]{2,1,0:T(8,128)(2,1)S(1)}, bf16[4,128,256]{2,1,0:T(8,128)(2,1)S(1)}, u32[]{:S(2)}, u32[]{:S(2)}) collective-permute-start(bf16[4,128,256]{2,1,0:T(8,128)(2,1)S(1)} %get-tuple-element.44), channel_id=1, source_target_pairs={{0,1},{1,0},{2,3},{3,2},{4,5},{5,4},{6,7},{7,6},{8,9},{9,8},{10,11... | collective-permute-start | bytes 786440 | tf_op jit(solution)/shard_map/ppermute | solution.py:39
  89.4 1.2 %collective-permute-done.11 = bf16[4,128,256]{2,1,0:T(8,128)(2,1)S(1)} collective-permute-done((bf16[4,128,256]{2,1,0:T(8,128)(2,1)S(1)}, bf16[4,128,256]{2,1,0:T(8,128)(2,1)S(1)}, u32[]{:S(2)}, u32[]{:S(2)}) %collective-permute-start.11) | collective-permute-done | bytes 262176 | tf_op jit(solution)/shard_map/ppermute | solution.py:39
  90.6 0.7 bitcast_dynamic-update-slice_fusion
Async XLA Ops:
  2.8 15.9 %collective-permute-start.1 = (bf16[128,8192]{1,0:T(8,128)(2,1)}, bf16[128,8192]{1,0:T(8,128)(2,1)}, u32[]{:S(2)}, u32[]{:S(2)}) collective-permute-start(bf16[128,8192]{1,0:T(8,128)(2,1)} %refs_0_), channel_id=1, source_target_pairs={{0,1},{1,0},{2,3},{3,2},{4,5},{5,4},{6,7},{7,6},{8,9},{9,8},{10,11... | collective-permute-start | bytes 6291464 | tf_op jit(solution)/shard_map/ppermute | solution.py:39
  6.1 25.5 %collective-permute-start = (bf16[128,8192]{1,0:T(8,128)(2,1)}, bf16[128,8192]{1,0:T(8,128)(2,1)}, u32[]{:S(2)}, u32[]{:S(2)}) collective-permute-start(bf16[128,8192]{1,0:T(8,128)(2,1)} %refs_0_), channel_id=1, source_target_pairs={{0,2},{1,7},{2,4},{3,1},{4,6},{5,3},{6,0},{7,5},{8,10},{9,15},{10,... | collective-permute-start | bytes 6291464 | tf_op jit(solution)/shard_map/ppermute | solution.py:48
  7.1 66.8 %all-to-all-start = ((bf16[64,144,128]{2,1,0:T(8,128)(2,1)}), bf16[64,144,128]{2,1,0:T(8,128)(2,1)S(1)}, u32[]{:S(2)}, u32[]{:S(2)}) async-start(bf16[64,144,128]{2,1,0:T(8,128)(2,1)} %shard_map.64), calls=%async_computation | async-start | bytes 4718592 | tf_op jit(solution)/shard_map/all_to_all | solution.py:355
  18.7 18.7 %collective-permute-start.2 = (bf16[8192,256]{1,0:T(8,128)(2,1)}, bf16[8192,256]{1,0:T(8,128)(2,1)S(1)}, u32[]{:S(2)}, u32[]{:S(2)}) collective-permute-start(bf16[8192,256]{1,0:T(8,128)(2,1)} %refs_1_), channel_id=1, source_target_pairs={{0,1},{1,0},{2,3},{3,2},{4,5},{5,4},{6,7},{7,6},{8,9},{9,8},{10,11... | collective-permute-start | bytes 12582920 | tf_op jit(solution)/shard_map/ppermute | solution.py:39
  19.3 36.5 %collective-permute-start.3 = (bf16[128,8192]{1,0:T(8,128)(2,1)}, bf16[128,8192]{1,0:T(8,128)(2,1)S(1)}, u32[]{:S(2)}, u32[]{:S(2)}) collective-permute-start(bf16[128,8192]{1,0:T(8,128)(2,1)} %collective-permute-done.1), channel_id=1, source_target_pairs={{0,3},{1,6},{2,5},{3,0},{4,7},{5,2},{6,1},{7,4},{8,11},{9,14},{10,... | collective-permute-start | bytes 6291464 | tf_op jit(solution)/shard_map/ppermute | solution.py:48
  31.6 7.4 %copy-start = (bf16[8192,256]{1,0:T(8,128)(2,1)S(1)}, bf16[8192,256]{1,0:T(8,128)(2,1)}, u32[]{:S(2)}) copy-start(bf16[8192,256]{1,0:T(8,128)(2,1)} %refs_1_) | copy-start | bytes 12582916
  35.4 24.2 %collective-permute-start.6 = (bf16[128,2048]{1,0:T(8,128)(2,1)S(1)}, bf16[128,2048]{1,0:T(8,128)(2,1)S(1)}, u32[]{:S(2)}, u32[]{:S(2)}) collective-permute-start(bf16[128,2048]{1,0:T(8,128)(2,1)S(1)} %get-tuple-element.31), channel_id=1, source_target_pairs={{0,2},{1,7},{2,4},{3,1},{4,6},{5,3},{6,0},{7,5},{8,10},{9,15},{10,... | collective-permute-start | bytes 1572872 | tf_op jit(solution)/shard_map/ppermute | solution.py:48
  37.4 27.8 %collective-permute-start.7 = (bf16[128,2048]{1,0:T(8,128)(2,1)S(1)}, bf16[128,2048]{1,0:T(8,128)(2,1)S(1)}, u32[]{:S(2)}, u32[]{:S(2)}) collective-permute-start(bf16[128,2048]{1,0:T(8,128)(2,1)S(1)} %get-tuple-element.32), channel_id=1, source_target_pairs={{0,2},{1,7},{2,4},{3,1},{4,6},{5,3},{6,0},{7,5},{8,10},{9,15},{10,... | collective-permute-start | bytes 1572872 | tf_op jit(solution)/shard_map/ppermute | solution.py:48
  37.4 33.4 %collective-permute-start.5 = (bf16[128,2048]{1,0:T(8,128)(2,1)S(1)}, bf16[128,2048]{1,0:T(8,128)(2,1)S(1)}, u32[]{:S(2)}, u32[]{:S(2)}) collective-permute-start(bf16[128,2048]{1,0:T(8,128)(2,1)S(1)} %get-tuple-element.30), channel_id=1, source_target_pairs={{0,2},{1,7},{2,4},{3,1},{4,6},{5,3},{6,0},{7,5},{8,10},{9,15},{10,... | collective-permute-start | bytes 1572872 | tf_op jit(solution)/shard_map/ppermute | solution.py:48
  37.4 33.4 %copy-start.1 = (bf16[8192,256]{1,0:T(8,128)(2,1)}, bf16[8192,256]{1,0:T(8,128)(2,1)S(1)}, u32[]{:S(2)}) copy-start(bf16[8192,256]{1,0:T(8,128)(2,1)S(1)} %collective-permute-done.2.refs_3_.refs_2_) | copy-start | bytes 12582916
  37.4 43.1 %collective-permute-start.4 = (bf16[128,2048]{1,0:T(8,128)(2,1)}, bf16[128,2048]{1,0:T(8,128)(2,1)}, u32[]{:S(2)}, u32[]{:S(2)}) collective-permute-start(bf16[128,2048]{1,0:T(8,128)(2,1)} %get-tuple-element.29), channel_id=1, source_target_pairs={{0,2},{1,7},{2,4},{3,1},{4,6},{5,3},{6,0},{7,5},{8,10},{9,15},{10,... | collective-permute-start | bytes 1572872 | tf_op jit(solution)/shard_map/ppermute | solution.py:48
  67.2 1.4 %copy-start.2 = (bf16[4,128,2048]{2,1,0:T(8,128)(2,1)}, bf16[4,128,2048]{2,1,0:T(8,128)(2,1)S(1)}, u32[]{:S(2)}) copy-start(bf16[4,128,2048]{2,1,0:T(8,128)(2,1)S(1)} %get-tuple-element.37.x_ref) | copy-start | bytes 6291460
  73.9 1.6 %copy-start.3 = (bf16[4,128,2048]{2,1,0:T(8,128)(2,1)S(1)}, bf16[4,128,2048]{2,1,0:T(8,128)(2,1)}, u32[]{:S(2)}) copy-start(bf16[4,128,2048]{2,1,0:T(8,128)(2,1)} %copy-done.2) | copy-start | bytes 6291460
  76.8 6.4 %collective-permute-start.10 = (f32[256,128]{1,0:T(8,128)S(1)}, f32[256,128]{1,0:T(8,128)S(1)}, u32[]{:S(2)}, u32[]{:S(2)}) collective-permute-start(f32[256,128]{1,0:T(8,128)S(1)} %get-tuple-element.42), channel_id=1, source_target_pairs={{0,6},{2,0},{4,2},{6,4},{1,7},{3,1},{5,3},{7,5},{8,14},{10,8},{12,... | collective-permute-start | bytes 393224 | tf_op jit(solution)/shard_map/ppermute | solution.py:39
  77.6 6.4 %collective-permute-start.8 = (f32[256,128]{1,0:T(8,128)S(1)}, f32[256,128]{1,0:T(8,128)S(1)}, u32[]{:S(2)}, u32[]{:S(2)}) collective-permute-start(f32[256,128]{1,0:T(8,128)S(1)} %get-tuple-element.40), channel_id=1, source_target_pairs={{0,2},{2,4},{4,6},{6,0},{1,3},{3,5},{5,7},{7,1},{8,10},{10,12},{12... | collective-permute-start | bytes 393224 | tf_op jit(solution)/shard_map/ppermute | solution.py:39
  78.6 5.4 %collective-permute-start.9 = (f32[256,128]{1,0:T(8,128)S(1)}, f32[256,128]{1,0:T(8,128)S(1)}, u32[]{:S(2)}, u32[]{:S(2)}) collective-permute-start(f32[256,128]{1,0:T(8,128)S(1)} %get-tuple-element.41), channel_id=1, source_target_pairs={{0,4},{2,6},{4,0},{6,2},{1,5},{3,7},{5,1},{7,3},{8,12},{10,14},{12... | collective-permute-start | bytes 393224 | tf_op jit(solution)/shard_map/ppermute | solution.py:39
  85.5 5.1 %collective-permute-start.11 = (bf16[4,128,256]{2,1,0:T(8,128)(2,1)S(1)}, bf16[4,128,256]{2,1,0:T(8,128)(2,1)S(1)}, u32[]{:S(2)}, u32[]{:S(2)}) collective-permute-start(bf16[4,128,256]{2,1,0:T(8,128)(2,1)S(1)} %get-tuple-element.44), channel_id=1, source_target_pairs={{0,1},{1,0},{2,3},{3,2},{4,5},{5,4},{6,7},{7,6},{8,9},{9,8},{10,11... | collective-permute-start | bytes 786440 | tf_op jit(solution)/shard_map/ppermute | solution.py:39

commit v6 on v5

--- a/solution.py
+++ b/solution.py
@@ -340,6 +340,25 @@
     )(yc, first, second, far, *parts, up)
 
 
+def place_kernel(yc, theirs, _, out, sem):
+    copy = pltpu.make_async_copy(theirs, out.at[:, 1 - yc[1]], sem)
+    copy.start()
+    copy.wait()
+
+
+def place(yc, theirs, out):
+    return pl.pallas_call(
+        place_kernel,
+        in_specs=[SMEM, VMEM, ANY],
+        out_specs=ANY,
+        out_shape=jax.ShapeDtypeStruct(out.shape, out.dtype),
+        scratch_shapes=[pltpu.SemaphoreType.DMA(())],
+        input_output_aliases={2: 0},
+        compiler_params=params(),
+        cost_estimate=cost(0, 1 << 19),
+    )(yc, theirs, out)
+
+
 def on_device(tokens, weight, down, up, apr, rps):
     y, c = lax.axis_index("y"), lax.axis_index("c")
     yc = jnp.stack([y, c]).astype(jnp.int32)
@@ -369,10 +388,7 @@
     up_sorted = up_rows(recv)
     out, out_partner = sum_up(yc, first, second, far, parts, up_sorted)
     theirs = shift(out_partner, "c", 1)
-    zero = jnp.zeros((), jnp.int32)
-    out = lax.dynamic_update_slice(
-        out, theirs[:, None], (zero, (1 - c).astype(jnp.int32), zero, zero)
-    )
+    out = place(yc, theirs, out)
     return out.reshape(NY * NC * SEG, COLS)
 
 

time: 91.7 us -> 92.4 us (level)
  Pallas kernels: 23.5 us -> 24.7 us
    pallas_call x0 -> x1, Pallas kernels: none -> 1.25 us  [place(): pl.pallas_call(place_kernel, in_specs=[SMEM, VMEM, ANY], out_specs=ANY, o...]
where the time goes in v6:
time: 92.4 us; the launch traced here: 92 us
  waiting for transfers between devices  36.3 us (39%)
  starting transfers between devices  27.6 us (30%)
  Pallas kernels  24.7 us (27%)
  local copies, waits for them, and re-layouts  3 us (3%)
    ppermute x6, waiting for transfers between devices, around(): return lax.ppermute(x, ('y', 'c'), pairs)  32.3 us
    all_to_all x1, starting transfers between devices, on_device(): recv = lax.all_to_all(send, ('z', 'x', 'c'), 0, 0)  11.6 us
    ppermute x6, starting transfers between devices, shift(): return lax.ppermute(x, axis, [(i, (i + by) % n) for i in range(n)])  11 us
    pallas_call x2, Pallas kernels, near_base(): pl.pallas_call(functools.partial(near_kernel, n), grid_spec=pltpu.Prefetc...  7.93 us
    ppermute x6, starting transfers between devices, around(): return lax.ppermute(x, ('y', 'c'), pairs)  4.99 us
    pallas_call x1, Pallas kernels, split_quarters(): pl.pallas_call(split_kernel, grid_spec=pltpu.PrefetchScalarGridSpec(num_s...  3.8 us
    pallas_call x2, Pallas kernels, more_base(): pl.pallas_call(more_kernel, grid_spec=pltpu.PrefetchScalarGridSpec(num_sc...  3.69 us
    unnamed x8, local copies, waits for them, and re-layouts  3 us
  transfers between devices with their start and end apart: 13, of which 8 were waited for; matrix products, arithmetic and copies ran while one was open for 0% of the time, Pallas kernels for 21%

profile of v6, /device:TPU:1, one launch (start us, length us, event | category | flops | bytes accessed | tf_op | source)
XLA Modules:
  0.0 92.0 jit_solution(10575575458336476586)
XLA Ops:
  0.0 2.8 %shard_map.64 = bf16[64,144,128]{2,1,0:T(8,128)(2,1)} custom-call(s32[128]{0:T(128)} %apr.1, s32[256]{0:T(256)} %rps.1, bf16[64,32,128]{2,1,0:T(8,128)(2,1)} %down_ref.1, bf16[64,2,256]{2,1,0:T(2,128)(2,1)} %up_ref.1), custom_call_target="tpu_custom_call" | custom-call | bytes 3145728 | tf_op jit(solution)/shard_map/pallas_call | solution.py:84
  2.8 3.3 %collective-permute-start.1 = (bf16[128,8192]{1,0:T(8,128)(2,1)}, bf16[128,8192]{1,0:T(8,128)(2,1)}, u32[]{:S(2)}, u32[]{:S(2)}) collective-permute-start(bf16[128,8192]{1,0:T(8,128)(2,1)} %refs_0_), channel_id=1, source_target_pairs={{0,1},{1,0},{2,3},{3,2},{4,5},{5,4},{6,7},{7,6},{8,9},{9,8},{10,11... | collective-permute-start | bytes 6291464 | tf_op jit(solution)/shard_map/ppermute | solution.py:39
  6.1 1.0 %collective-permute-start = (bf16[128,8192]{1,0:T(8,128)(2,1)}, bf16[128,8192]{1,0:T(8,128)(2,1)}, u32[]{:S(2)}, u32[]{:S(2)}) collective-permute-start(bf16[128,8192]{1,0:T(8,128)(2,1)} %refs_0_), channel_id=1, source_target_pairs={{0,2},{1,7},{2,4},{3,1},{4,6},{5,3},{6,0},{7,5},{8,10},{9,15},{10,... | collective-permute-start | bytes 6291464 | tf_op jit(solution)/shard_map/ppermute | solution.py:48
  7.1 11.6 %all-to-all-start = ((bf16[64,144,128]{2,1,0:T(8,128)(2,1)}), bf16[64,144,128]{2,1,0:T(8,128)(2,1)S(1)}, u32[]{:S(2)}, u32[]{:S(2)}) async-start(bf16[64,144,128]{2,1,0:T(8,128)(2,1)} %shard_map.64), calls=%async_computation | async-start | bytes 4718592 | tf_op jit(solution)/shard_map/all_to_all | solution.py:374
  18.7 0.0 collective-permute-done.1
  18.7 0.5 collective-permute-start.2
  19.3 0.5 collective-permute-start.3
  19.7 11.9 %collective-permute-done.refs_1_.x_ref = bf16[128,8192]{1,0:T(8,128)(2,1)} collective-permute-done((bf16[128,8192]{1,0:T(8,128)(2,1)}, bf16[128,8192]{1,0:T(8,128)(2,1)}, u32[]{:S(2)}, u32[]{:S(2)}) %collective-permute-start) | collective-permute-done | bytes 2097184 | tf_op jit(solution)/shard_map/ppermute | solution.py:48
  31.6 0.0 copy-start
  31.6 3.8 %shard_map.67 = (bf16[128,2048]{1,0:T(8,128)(2,1)S(1)}, bf16[128,2048]{1,0:T(8,128)(2,1)S(1)}, bf16[128,2048]{1,0:T(8,128)(2,1)S(1)}, bf16[128,2048]{1,0:T(8,128)(2,1)}) custom-call(s32[1]{0:T(128)} %bitcast.2.first, bf16[128,8192]{1,0:T(8,128)(2,1)} %collective-permute-done.refs_1_.x_ref), custom_call_target="tpu_custom_call" | custom-call | flops 99999997952 | bytes 4194304 | tf_op jit(solution)/shard_map/pallas_call | solution.py:121
  35.4 2.0 %collective-permute-start.6 = (bf16[128,2048]{1,0:T(8,128)(2,1)S(1)}, bf16[128,2048]{1,0:T(8,128)(2,1)S(1)}, u32[]{:S(2)}, u32[]{:S(2)}) collective-permute-start(bf16[128,2048]{1,0:T(8,128)(2,1)S(1)} %get-tuple-element.31), channel_id=1, source_target_pairs={{0,2},{1,7},{2,4},{3,1},{4,6},{5,3},{6,0},{7,5},{8,10},{9,15},{10,... | collective-permute-start | bytes 1572872 | tf_op jit(solution)/shard_map/ppermute | solution.py:48
  37.4 0.0 collective-permute-start.7
  37.4 0.0 collective-permute-start.5
  37.4 0.0 collective-permute-done.2.refs_3_.refs_2_
  37.4 0.0 copy-start.1
  37.4 1.5 %collective-permute-start.4 = (bf16[128,2048]{1,0:T(8,128)(2,1)}, bf16[128,2048]{1,0:T(8,128)(2,1)}, u32[]{:S(2)}, u32[]{:S(2)}) collective-permute-start(bf16[128,2048]{1,0:T(8,128)(2,1)} %get-tuple-element.29), channel_id=1, source_target_pairs={{0,2},{1,7},{2,4},{3,1},{4,6},{5,3},{6,0},{7,5},{8,10},{9,15},{10,... | collective-permute-start | bytes 1572872 | tf_op jit(solution)/shard_map/ppermute | solution.py:48
  38.9 0.1 pad_add_fusion.yc
  39.0 0.0 copy-done
  39.0 5.3 %shard_map.65 = (f32[256,512]{1,0:T(8,128)S(1)}, bf16[128,2048]{1,0:T(8,128)(2,1)S(1)}, bf16[128,2048]{1,0:T(8,128)(2,1)S(1)}) custom-call(s32[2]{0:T(128)S(1)} %pad_add_fusion.yc, bf16[128,8192]{1,0:T(8,128)(2,1)} %refs_0_, bf16[128,8192]{1,0:T(8,128)(2,1)} %collective-permute-done.refs_1_.x_ref, bf16[8192,256]{1,0:T(8,128)(2,1)S(1)} %copy-done, ...), custom_call_target="tpu_custom_call" | custom-call | flops 2147483648 | bytes 12582912 | tf_op jit(solution)/shard_map/pallas_call | solution.py:215
  44.3 11.4 %collective-permute-done.3.refs_0_ = bf16[128,8192]{1,0:T(8,128)(2,1)S(1)} collective-permute-done((bf16[128,8192]{1,0:T(8,128)(2,1)}, bf16[128,8192]{1,0:T(8,128)(2,1)S(1)}, u32[]{:S(2)}, u32[]{:S(2)}) %collective-permute-start.3) | collective-permute-done | bytes 2097184 | tf_op jit(solution)/shard_map/ppermute | solution.py:48
  55.7 2.6 %shard_map.66 = (f32[128,512]{1,0:T(8,128)S(1)}, bf16[128,2048]{1,0:T(8,128)(2,1)S(1)}) custom-call(s32[2]{0:T(128)S(1)} %pad_add_fusion.yc, bf16[128,8192]{1,0:T(8,128)(2,1)S(1)} %collective-permute-done.3.refs_0_, bf16[8192,256]{1,0:T(8,128)(2,1)S(1)} %copy-done, bf16[8192,256]{1,0:T(8,128)(2,1)S(1)} %collective-permute-done.2.refs_3_.refs_2_, ...), custom_call_target="tpu_custom_call" | custom-call | flops 1073741824 | bytes 12582912 | tf_op jit(solution)/shard_map/pallas_call | solution.py:215
  58.3 1.2 %collective-permute-done.6.q0 = bf16[128,2048]{1,0:T(8,128)(2,1)S(1)} collective-permute-done((bf16[128,2048]{1,0:T(8,128)(2,1)S(1)}, bf16[128,2048]{1,0:T(8,128)(2,1)S(1)}, u32[]{:S(2)}, u32[]{:S(2)}) %collective-permute-start.6) | collective-permute-done | bytes 524320 | tf_op jit(solution)/shard_map/ppermute | solution.py:48
  59.6 5.6 %collective-permute-done.7.q1 = bf16[128,2048]{1,0:T(8,128)(2,1)S(1)} collective-permute-done((bf16[128,2048]{1,0:T(8,128)(2,1)S(1)}, bf16[128,2048]{1,0:T(8,128)(2,1)S(1)}, u32[]{:S(2)}, u32[]{:S(2)}) %collective-permute-start.7) | collective-permute-done | bytes 524320 | tf_op jit(solution)/shard_map/ppermute | solution.py:48
  65.2 2.0 %shard_map.68 = (f32[128,512]{1,0:T(8,128)S(1)}, bf16[4,128,2048]{2,1,0:T(8,128)(2,1)S(1)}) custom-call(s32[2]{0:T(128)S(1)} %pad_add_fusion.yc, bf16[128,2048]{1,0:T(8,128)(2,1)S(1)} %collective-permute-done.6.q0, bf16[128,2048]{1,0:T(8,128)(2,1)S(1)} %collective-permute-done.7.q1, bf16[32,4,64,256]{3,2,1,0:T(8,128)(2,1)S(1)} %bitcast.7, ...), custom_call_target="tpu_custom_call" | custom-call | flops 536870912 | bytes 10485760 | tf_op jit(solution)/shard_map/pallas_call | solution.py:254
  67.2 0.0 copy-start.2
  67.2 1.4 %copy-done.2 = bf16[4,128,2048]{2,1,0:T(8,128)(2,1)} copy-done((bf16[4,128,2048]{2,1,0:T(8,128)(2,1)}, bf16[4,128,2048]{2,1,0:T(8,128)(2,1)S(1)}, u32[]{:S(2)}) %copy-start.2) | copy-done | bytes 2097176
  68.6 2.2 %collective-permute-done.5.x = bf16[128,2048]{1,0:T(8,128)(2,1)S(1)} collective-permute-done((bf16[128,2048]{1,0:T(8,128)(2,1)S(1)}, bf16[128,2048]{1,0:T(8,128)(2,1)S(1)}, u32[]{:S(2)}, u32[]{:S(2)}) %collective-permute-start.5) | collective-permute-done | bytes 524320 | tf_op jit(solution)/shard_map/ppermute | solution.py:48
  70.8 0.0 copy-done.1
  70.8 1.0 %shard_map.69.before.after = f32[128,512]{1,0:T(8,128)S(1)} custom-call(s32[2]{0:T(128)S(1)} %pad_add_fusion.yc, bf16[128,2048]{1,0:T(8,128)(2,1)S(1)} %collective-permute-done.5.x, bf16[32,4,64,256]{3,2,1,0:T(8,128)(2,1)S(1)} %bitcast.8, bf16[32,4,64,256]{3,2,1,0:T(8,128)(2,1)S(1)} %bitcast.10, f32[128,512]{1,0:T(8,128)S(1)} %get-tuple-element.36.before), custom_call_target="tpu_custom_call" | custom-call | flops 268435456 | bytes 3145728 | tf_op jit(solution)/shard_map/pallas_call | solution.py:283
  71.8 2.1 %all-to-all-done.recv_ref = bf16[64,144,128]{2,1,0:T(8,128)(2,1)S(1)} async-done(((bf16[64,144,128]{2,1,0:T(8,128)(2,1)}), bf16[64,144,128]{2,1,0:T(8,128)(2,1)S(1)}, u32[]{:S(2)}, u32[]{:S(2)}) %all-to-all-start) | async-done | bytes 2359328 | tf_op jit(solution)/shard_map/all_to_all | solution.py:374
  73.9 0.0 copy-start.3
  73.9 1.6 %copy-done.3 = bf16[4,128,2048]{2,1,0:T(8,128)(2,1)S(1)} copy-done((bf16[4,128,2048]{2,1,0:T(8,128)(2,1)S(1)}, bf16[4,128,2048]{2,1,0:T(8,128)(2,1)}, u32[]{:S(2)}) %copy-start.3) | copy-done | bytes 2097176
  75.5 1.4 %shard_map.71 = (f32[256,128]{1,0:T(8,128)S(1)}, f32[256,128]{1,0:T(8,128)S(1)}, f32[256,128]{1,0:T(8,128)S(1)}, f32[256,128]{1,0:T(8,128)S(1)}) custom-call(s32[2]{0:T(128)S(1)} %pad_add_fusion.yc, bf16[4,128,2048]{2,1,0:T(8,128)(2,1)S(1)} %copy-done.3, bf16[64,144,128]{2,1,0:T(8,128)(2,1)S(1)} %all-to-all-done.recv_ref, f32[128,512]{1,0:T(8,128)S(1)} %shard_map.69.before.after), custom_call_target="tpu_custom_call" | custom-call | flops 268435456 | bytes 5242880 | tf_op jit(solution)/shard_map/pallas_call | solution.py:158
  76.8 0.7 collective-permute-start.10
  77.6 1.0 %collective-permute-start.8 = (f32[256,128]{1,0:T(8,128)S(1)}, f32[256,128]{1,0:T(8,128)S(1)}, u32[]{:S(2)}, u32[]{:S(2)}) collective-permute-start(f32[256,128]{1,0:T(8,128)S(1)} %get-tuple-element.40), channel_id=1, source_target_pairs={{0,2},{2,4},{4,6},{6,0},{1,3},{3,5},{5,7},{7,1},{8,10},{10,12},{12... | collective-permute-start | bytes 393224 | tf_op jit(solution)/shard_map/ppermute | solution.py:39
  78.6 1.4 %collective-permute-start.9 = (f32[256,128]{1,0:T(8,128)S(1)}, f32[256,128]{1,0:T(8,128)S(1)}, u32[]{:S(2)}, u32[]{:S(2)}) collective-permute-start(f32[256,128]{1,0:T(8,128)S(1)} %get-tuple-element.41), channel_id=1, source_target_pairs={{0,4},{2,6},{4,0},{6,2},{1,5},{3,7},{5,1},{7,3},{8,12},{10,14},{12... | collective-permute-start | bytes 393224 | tf_op jit(solution)/shard_map/ppermute | solution.py:39
  80.0 0.5 shard_map.72.up
  80.5 0.0 collective-permute-done.4.x
  80.5 2.7 %shard_map.70.far = f32[128,512]{1,0:T(8,128)S(1)} custom-call(s32[2]{0:T(128)S(1)} %pad_add_fusion.yc, bf16[128,2048]{1,0:T(8,128)(2,1)} %collective-permute-done.4.x, bf16[32,4,64,256]{3,2,1,0:T(8,128)(2,1)} %bitcast.6, bf16[32,4,64,256]{3,2,1,0:T(8,128)(2,1)} %bitcast.11, f32[128,512]{1,0:T(8,128)S(1)} %shard_map.69.before.after), custom_call_target="tpu_custom_call" | custom-call | flops 268435456 | bytes 3145728 | tf_op jit(solution)/shard_map/pallas_call | solution.py:283
  83.2 0.0 collective-permute-done.10.p3
  83.2 0.8 collective-permute-done.8.p1
  84.0 0.0 collective-permute-done.9.p2
  84.0 1.5 %shard_map.73 = (bf16[4,2,128,256]{3,2,1,0:T(8,128)(2,1)}, bf16[4,128,256]{2,1,0:T(8,128)(2,1)S(1)}) custom-call(s32[2]{0:T(128)S(1)} %pad_add_fusion.yc, f32[256,512]{1,0:T(8,128)S(1)} %get-tuple-element.27.refs_3_.first, f32[128,512]{1,0:T(8,128)S(1)} %get-tuple-element.28.second, f32[128,512]{1,0:T(8,128)S(1)} %shard_map.70.far, ...), custom_call_target="tpu_custom_call" | custom-call | flops 67108864 | bytes 3145728 | tf_op jit(solution)/shard_map/pallas_call | solution.py:326
  85.5 4.0 %collective-permute-start.11 = (bf16[4,128,256]{2,1,0:T(8,128)(2,1)S(1)}, bf16[4,128,256]{2,1,0:T(8,128)(2,1)S(1)}, u32[]{:S(2)}, u32[]{:S(2)}) collective-permute-start(bf16[4,128,256]{2,1,0:T(8,128)(2,1)S(1)} %get-tuple-element.43), channel_id=1, source_target_pairs={{0,1},{1,0},{2,3},{3,2},{4,5},{5,4},{6,7},{7,6},{8,9},{9,8},{10,11... | collective-permute-start | bytes 786440 | tf_op jit(solution)/shard_map/ppermute | solution.py:39
  89.4 1.2 %collective-permute-done.11.theirs = bf16[4,128,256]{2,1,0:T(8,128)(2,1)S(1)} collective-permute-done((bf16[4,128,256]{2,1,0:T(8,128)(2,1)S(1)}, bf16[4,128,256]{2,1,0:T(8,128)(2,1)S(1)}, u32[]{:S(2)}, u32[]{:S(2)}) %collective-permute-start.11) | collective-permute-done | bytes 262176 | tf_op jit(solution)/shard_map/ppermute | solution.py:39
  90.6 1.3 %shard_map.74 = bf16[4,2,128,256]{3,2,1,0:T(8,128)(2,1)} custom-call(s32[2]{0:T(128)S(1)} %pad_add_fusion.yc, bf16[4,128,256]{2,1,0:T(8,128)(2,1)S(1)} %collective-permute-done.11.theirs, bf16[4,2,128,256]{3,2,1,0:T(8,128)(2,1)} %get-tuple-element.44._), custom_call_target="tpu_custom_call", output_to_operand_aliasing={{}: (2, {})} | custom-call | bytes 524288 | tf_op jit(solution)/shard_map/pallas_call | solution.py:350
Async XLA Ops:
  2.8 15.9 %collective-permute-start.1 = (bf16[128,8192]{1,0:T(8,128)(2,1)}, bf16[128,8192]{1,0:T(8,128)(2,1)}, u32[]{:S(2)}, u32[]{:S(2)}) collective-permute-start(bf16[128,8192]{1,0:T(8,128)(2,1)} %refs_0_), channel_id=1, source_target_pairs={{0,1},{1,0},{2,3},{3,2},{4,5},{5,4},{6,7},{7,6},{8,9},{9,8},{10,11... | collective-permute-start | bytes 6291464 | tf_op jit(solution)/shard_map/ppermute | solution.py:39
  6.1 25.5 %collective-permute-start = (bf16[128,8192]{1,0:T(8,128)(2,1)}, bf16[128,8192]{1,0:T(8,128)(2,1)}, u32[]{:S(2)}, u32[]{:S(2)}) collective-permute-start(bf16[128,8192]{1,0:T(8,128)(2,1)} %refs_0_), channel_id=1, source_target_pairs={{0,2},{1,7},{2,4},{3,1},{4,6},{5,3},{6,0},{7,5},{8,10},{9,15},{10,... | collective-permute-start | bytes 6291464 | tf_op jit(solution)/shard_map/ppermute | solution.py:48
  7.1 66.8 %all-to-all-start = ((bf16[64,144,128]{2,1,0:T(8,128)(2,1)}), bf16[64,144,128]{2,1,0:T(8,128)(2,1)S(1)}, u32[]{:S(2)}, u32[]{:S(2)}) async-start(bf16[64,144,128]{2,1,0:T(8,128)(2,1)} %shard_map.64), calls=%async_computation | async-start | bytes 4718592 | tf_op jit(solution)/shard_map/all_to_all | solution.py:374
  18.7 18.7 %collective-permute-start.2 = (bf16[8192,256]{1,0:T(8,128)(2,1)}, bf16[8192,256]{1,0:T(8,128)(2,1)S(1)}, u32[]{:S(2)}, u32[]{:S(2)}) collective-permute-start(bf16[8192,256]{1,0:T(8,128)(2,1)} %refs_1_), channel_id=1, source_target_pairs={{0,1},{1,0},{2,3},{3,2},{4,5},{5,4},{6,7},{7,6},{8,9},{9,8},{10,11... | collective-permute-start | bytes 12582920 | tf_op jit(solution)/shard_map/ppermute | solution.py:39
  19.3 36.5 %collective-permute-start.3 = (bf16[128,8192]{1,0:T(8,128)(2,1)}, bf16[128,8192]{1,0:T(8,128)(2,1)S(1)}, u32[]{:S(2)}, u32[]{:S(2)}) collective-permute-start(bf16[128,8192]{1,0:T(8,128)(2,1)} %collective-permute-done.1), channel_id=1, source_target_pairs={{0,3},{1,6},{2,5},{3,0},{4,7},{5,2},{6,1},{7,4},{8,11},{9,14},{10,... | collective-permute-start | bytes 6291464 | tf_op jit(solution)/shard_map/ppermute | solution.py:48
  31.6 7.4 %copy-start = (bf16[8192,256]{1,0:T(8,128)(2,1)S(1)}, bf16[8192,256]{1,0:T(8,128)(2,1)}, u32[]{:S(2)}) copy-start(bf16[8192,256]{1,0:T(8,128)(2,1)} %refs_1_) | copy-start | bytes 12582916
  35.4 24.2 %collective-permute-start.6 = (bf16[128,2048]{1,0:T(8,128)(2,1)S(1)}, bf16[128,2048]{1,0:T(8,128)(2,1)S(1)}, u32[]{:S(2)}, u32[]{:S(2)}) collective-permute-start(bf16[128,2048]{1,0:T(8,128)(2,1)S(1)} %get-tuple-element.31), channel_id=1, source_target_pairs={{0,2},{1,7},{2,4},{3,1},{4,6},{5,3},{6,0},{7,5},{8,10},{9,15},{10,... | collective-permute-start | bytes 1572872 | tf_op jit(solution)/shard_map/ppermute | solution.py:48
  37.4 27.8 %collective-permute-start.7 = (bf16[128,2048]{1,0:T(8,128)(2,1)S(1)}, bf16[128,2048]{1,0:T(8,128)(2,1)S(1)}, u32[]{:S(2)}, u32[]{:S(2)}) collective-permute-start(bf16[128,2048]{1,0:T(8,128)(2,1)S(1)} %get-tuple-element.32), channel_id=1, source_target_pairs={{0,2},{1,7},{2,4},{3,1},{4,6},{5,3},{6,0},{7,5},{8,10},{9,15},{10,... | collective-permute-start | bytes 1572872 | tf_op jit(solution)/shard_map/ppermute | solution.py:48
  37.4 33.4 %collective-permute-start.5 = (bf16[128,2048]{1,0:T(8,128)(2,1)S(1)}, bf16[128,2048]{1,0:T(8,128)(2,1)S(1)}, u32[]{:S(2)}, u32[]{:S(2)}) collective-permute-start(bf16[128,2048]{1,0:T(8,128)(2,1)S(1)} %get-tuple-element.30), channel_id=1, source_target_pairs={{0,2},{1,7},{2,4},{3,1},{4,6},{5,3},{6,0},{7,5},{8,10},{9,15},{10,... | collective-permute-start | bytes 1572872 | tf_op jit(solution)/shard_map/ppermute | solution.py:48
  37.4 33.4 %copy-start.1 = (bf16[8192,256]{1,0:T(8,128)(2,1)}, bf16[8192,256]{1,0:T(8,128)(2,1)S(1)}, u32[]{:S(2)}) copy-start(bf16[8192,256]{1,0:T(8,128)(2,1)S(1)} %collective-permute-done.2.refs_3_.refs_2_) | copy-start | bytes 12582916
  37.4 43.1 %collective-permute-start.4 = (bf16[128,2048]{1,0:T(8,128)(2,1)}, bf16[128,2048]{1,0:T(8,128)(2,1)}, u32[]{:S(2)}, u32[]{:S(2)}) collective-permute-start(bf16[128,2048]{1,0:T(8,128)(2,1)} %get-tuple-element.29), channel_id=1, source_target_pairs={{0,2},{1,7},{2,4},{3,1},{4,6},{5,3},{6,0},{7,5},{8,10},{9,15},{10,... | collective-permute-start | bytes 1572872 | tf_op jit(solution)/shard_map/ppermute | solution.py:48
  67.2 1.4 %copy-start.2 = (bf16[4,128,2048]{2,1,0:T(8,128)(2,1)}, bf16[4,128,2048]{2,1,0:T(8,128)(2,1)S(1)}, u32[]{:S(2)}) copy-start(bf16[4,128,2048]{2,1,0:T(8,128)(2,1)S(1)} %get-tuple-element.37.x_ref) | copy-start | bytes 6291460
  73.9 1.6 %copy-start.3 = (bf16[4,128,2048]{2,1,0:T(8,128)(2,1)S(1)}, bf16[4,128,2048]{2,1,0:T(8,128)(2,1)}, u32[]{:S(2)}) copy-start(bf16[4,128,2048]{2,1,0:T(8,128)(2,1)} %copy-done.2) | copy-start | bytes 6291460
  76.8 6.4 %collective-permute-start.10 = (f32[256,128]{1,0:T(8,128)S(1)}, f32[256,128]{1,0:T(8,128)S(1)}, u32[]{:S(2)}, u32[]{:S(2)}) collective-permute-start(f32[256,128]{1,0:T(8,128)S(1)} %get-tuple-element.42), channel_id=1, source_target_pairs={{0,6},{2,0},{4,2},{6,4},{1,7},{3,1},{5,3},{7,5},{8,14},{10,8},{12,... | collective-permute-start | bytes 393224 | tf_op jit(solution)/shard_map/ppermute | solution.py:39
  77.6 6.4 %collective-permute-start.8 = (f32[256,128]{1,0:T(8,128)S(1)}, f32[256,128]{1,0:T(8,128)S(1)}, u32[]{:S(2)}, u32[]{:S(2)}) collective-permute-start(f32[256,128]{1,0:T(8,128)S(1)} %get-tuple-element.40), channel_id=1, source_target_pairs={{0,2},{2,4},{4,6},{6,0},{1,3},{3,5},{5,7},{7,1},{8,10},{10,12},{12... | collective-permute-start | bytes 393224 | tf_op jit(solution)/shard_map/ppermute | solution.py:39
  78.6 5.4 %collective-permute-start.9 = (f32[256,128]{1,0:T(8,128)S(1)}, f32[256,128]{1,0:T(8,128)S(1)}, u32[]{:S(2)}, u32[]{:S(2)}) collective-permute-start(f32[256,128]{1,0:T(8,128)S(1)} %get-tuple-element.41), channel_id=1, source_target_pairs={{0,4},{2,6},{4,0},{6,2},{1,5},{3,7},{5,1},{7,3},{8,12},{10,14},{12... | collective-permute-start | bytes 393224 | tf_op jit(solution)/shard_map/ppermute | solution.py:39
  85.5 5.1 %collective-permute-start.11 = (bf16[4,128,256]{2,1,0:T(8,128)(2,1)S(1)}, bf16[4,128,256]{2,1,0:T(8,128)(2,1)S(1)}, u32[]{:S(2)}, u32[]{:S(2)}) collective-permute-start(bf16[4,128,256]{2,1,0:T(8,128)(2,1)S(1)} %get-tuple-element.43), channel_id=1, source_target_pairs={{0,1},{1,0},{2,3},{3,2},{4,5},{5,4},{6,7},{7,6},{8,9},{9,8},{10,11... | collective-permute-start | bytes 786440 | tf_op jit(solution)/shard_map/ppermute | solution.py:39
